TPU v7x, 128 devices: a whole 4x4x4 slice. The times are simulated.
128 devices in a mesh: tp: 4 (over z_lo, core), seq: 32 (over x, z_hi, y).
Axes of the slice: x: 4, y: 4, z: 4 (z_hi: 2, z_lo: 2; z = z_hi * 2 + z_lo), core: 2. Of those that a mesh axis runs over, the one named last changes fastest.
Arguments:
- tokens: bfloat16 [8192, 2048], P('seq'), may hold values from -6 to 6
- norm1_gain: bfloat16 [2048], P('seq'), may hold values from 0.25 to 1.75
- norm1_bias: bfloat16 [2048], P('seq'), may hold values from -3 to 3
- w_query: bfloat16 [2048, 2048], P('seq', 'tp'), may hold values from -0.125 to 0.125
- w_key: bfloat16 [2048, 2048], P('seq', 'tp'), may hold values from -0.125 to 0.125
- w_value: bfloat16 [2048, 4096], P('seq', 'tp'), may hold values from -0.125 to 0.125
- w_gate: bfloat16 [2048, 4096], P('seq', 'tp'), may hold values from -0.125 to 0.125
- w_out: bfloat16 [4096, 2048], P('tp', 'seq'), may hold values from -0.1875 to 0.1875
- norm2_gain: bfloat16 [2048], P('seq'), may hold values from 0.25 to 1.75
- norm2_bias: bfloat16 [2048], P('seq'), may hold values from -3 to 3
- w_up: bfloat16 [2048, 4096], P('seq', 'tp'), may hold values from -0.125 to 0.125
- w_down: bfloat16 [4096, 2048], P('tp', 'seq'), may hold values from -0.09375 to 0.09375
- decay_rate: float32 [8], P('tp'), may hold values from 1.2207031e-05 to 0.03
- out_grad: bfloat16 [8192, 2048], P('seq'), may hold values from -6 to 6
Outputs:
- block_out: bfloat16 [8192, 2048], P('seq')
- tokens_grad: float32 [8192, 2048], P('seq')
- norm1_gain_grad: float32 [2048], P('seq')
- norm1_bias_grad: float32 [2048], P('seq')
- w_query_grad: float32 [2048, 2048], P('seq', 'tp')
- w_key_grad: float32 [2048, 2048], P('seq', 'tp')
- w_value_grad: float32 [2048, 4096], P('seq', 'tp')
- w_gate_grad: float32 [2048, 4096], P('seq', 'tp')
- w_out_grad: float32 [4096, 2048], P('tp', 'seq')
- norm2_gain_grad: float32 [2048], P('seq')
- norm2_bias_grad: float32 [2048], P('seq')
- w_up_grad: float32 [2048, 4096], P('seq', 'tp')
- w_down_grad: float32 [4096, 2048], P('tp', 'seq')
All inputs are finite; a program needn't handle non-finite values.
Results may differ from a plain program's by a relative error of at most 0.025.
Values may be sent and summed in bfloat16 or wider, within the bound.
No kernel may reach another device: no remote copies, remote signals or barrier semaphores. Data moves between devices by JAX's collectives and lax.ppermute only.
A program may use at most 192 MiB of HBM per device.

v0:
```python
import jax
import jax.numpy as jnp
from jax import lax
from jax.sharding import PartitionSpec as P

DK = 256
DV = 512


def prefix(part, axis, combine, identity, reverse):
    count = lax.axis_size(axis)
    place = lax.axis_index(axis)
    ahead = count - 1 - place if reverse else place
    gathered = jax.tree.map(lambda a: lax.all_gather(a, axis), part)
    state = jax.tree.map(lambda a, e: jnp.zeros_like(a) + jnp.asarray(e, a.dtype), part, identity)

    def one(step, state):
        source = count - 1 - step if reverse else step
        return combine(
            state, jax.tree.map(lambda a: lax.dynamic_index_in_dim(a, source, 0, False), gathered)
        )

    return lax.fori_loop(0, ahead, one, state)


def layer_norm(values, gain, bias):
    center = values - jnp.mean(values, axis=-1, keepdims=True)
    spread = jnp.mean(center * center, axis=-1, keepdims=True)
    return center * lax.rsqrt(spread + 1e-05) * gain + bias


def group_norm(values):
    center = values - jnp.mean(values, axis=-1, keepdims=True)
    spread = jnp.mean(center * center, axis=-1, keepdims=True)
    return center * lax.rsqrt(spread + 1e-05)


def rotate(values, cosine, sine):
    half = values.shape[-1] // 2
    first = values[..., :half]
    second = values[..., half:]
    return jnp.concatenate(
        [first * cosine - second * sine, second * cosine + first * sine], axis=-1
    )


def low_dot(left, right):
    return jnp.dot(left, right, preferred_element_type=jnp.float32)


def low_form(form, left, right):
    return jnp.einsum(form, left, right, preferred_element_type=jnp.float32)


def exact_form(form, left, right):
    return jnp.einsum(form, left, right, precision=lax.Precision.HIGHEST)


def decay_chain(earlier, later):
    return (later[1][:, None, None] * earlier[0] + later[0], earlier[1] * later[1])


def body(
    tokens,
    norm1_gain,
    norm1_bias,
    w_query,
    w_key,
    w_value,
    w_gate,
    w_out,
    norm2_gain,
    norm2_bias,
    w_up,
    w_down,
    decay_rate,
    out_grad,
):
    tok_rows = tokens.shape[0]
    local_heads = decay_rate.shape[0]
    (
        gain1,
        bias1,
        gain2,
        bias2,
        full_query,
        full_key,
        full_value,
        full_gate,
        full_out,
        full_up,
        full_down,
    ) = (
        lax.all_gather(norm1_gain, "seq", axis=0, tiled=True),
        lax.all_gather(norm1_bias, "seq", axis=0, tiled=True),
        lax.all_gather(norm2_gain, "seq", axis=0, tiled=True),
        lax.all_gather(norm2_bias, "seq", axis=0, tiled=True),
        lax.all_gather(w_query, "seq", axis=0, tiled=True),
        lax.all_gather(w_key, "seq", axis=0, tiled=True),
        lax.all_gather(w_value, "seq", axis=0, tiled=True),
        lax.all_gather(w_gate, "seq", axis=0, tiled=True),
        lax.all_gather(w_out, "seq", axis=1, tiled=True),
        lax.all_gather(w_up, "seq", axis=0, tiled=True),
        lax.all_gather(w_down, "seq", axis=1, tiled=True),
    )
    gain1 = gain1.astype(jnp.float32)
    bias1 = bias1.astype(jnp.float32)
    gain2 = gain2.astype(jnp.float32)
    bias2 = bias2.astype(jnp.float32)
    stream = tokens.astype(jnp.float32)
    normed1 = layer_norm(stream, gain1, bias1).astype(jnp.bfloat16)
    query_raw = low_dot(normed1, full_query).reshape(tok_rows, local_heads, DK)
    key_raw = low_dot(normed1, full_key).reshape(tok_rows, local_heads, DK)
    value = low_dot(normed1, full_value).astype(jnp.bfloat16).reshape(tok_rows, local_heads, DV)
    gate_raw = low_dot(normed1, full_gate)
    half = DK // 2
    position = (lax.axis_index("seq") * tok_rows + jnp.arange(tok_rows)).astype(jnp.float32)
    freq = 10000.0 ** (-jnp.arange(half).astype(jnp.float32) / half)
    angle = position[:, None] * freq[None, :]
    cosine = jnp.cos(angle)[:, None, :]
    sine = jnp.sin(angle)[:, None, :]

    def turn(values):
        return rotate(values, cosine, sine)

    query = turn(query_raw).astype(jnp.bfloat16)
    key = turn(key_raw).astype(jnp.bfloat16)
    index = jnp.arange(tok_rows).astype(jnp.float32)
    offset = index[:, None] - index[None, :]
    dmask = jnp.where(
        offset[None] >= 0.0,
        jnp.exp(-decay_rate[:, None, None] * jnp.maximum(offset, 0.0)[None]),
        0.0,
    )
    qdec = jnp.exp(-decay_rate[None, :] * (index[:, None] + 1.0))[:, :, None]
    kdec = jnp.exp(-decay_rate[None, :] * (tok_rows - 1.0 - index[:, None]))[:, :, None]
    carry_decay = jnp.exp(-decay_rate * tok_rows)
    query_wide = query.astype(jnp.float32)
    key_wide = key.astype(jnp.float32)
    value_wide = value.astype(jnp.float32)
    scores = low_form("ihd,jhd->hij", query, key)
    probs = (scores * dmask).astype(jnp.bfloat16)
    fresh = exact_form("jhd,jhv->hdv", kdec * key_wide, value_wide)
    empty_state = jnp.zeros((local_heads, DK, DV), jnp.float32)
    unit_decay = jnp.ones((local_heads,), jnp.float32)
    prior_state, unused = prefix(
        (fresh, carry_decay), "seq", decay_chain, (empty_state, unit_decay), False
    )
    retained = low_form("hij,jhv->ihv", probs, value) + qdec * exact_form(
        "ihd,hdv->ihv", query_wide, prior_state
    )
    grouped, group_back = jax.vjp(group_norm, retained)
    grouped_flat = grouped.reshape(tok_rows, local_heads * DV)

    def gated(gate_in, norm_in):
        return jax.nn.silu(gate_in) * norm_in

    mixed_wide, gate_back = jax.vjp(gated, gate_raw, grouped_flat)
    mixed = mixed_wide.astype(jnp.bfloat16)
    attn = lax.psum(low_dot(mixed, full_out), "tp")
    resid = stream + attn
    normed2_wide, norm2_back = jax.vjp(layer_norm, resid, gain2, bias2)
    normed2 = normed2_wide.astype(jnp.bfloat16)
    up_raw = low_dot(normed2, full_up)

    def smooth(values):
        return jax.nn.gelu(values, approximate=True)

    hidden_wide, smooth_back = jax.vjp(smooth, up_raw)
    hidden = hidden_wide.astype(jnp.bfloat16)
    ffn = lax.psum(low_dot(hidden, full_down).astype(jnp.bfloat16), "tp").astype(jnp.float32)
    block_out = (resid + ffn).astype(jnp.bfloat16)
    back_query, back_key, back_value, back_gate, back_out, back_up, back_down = (
        lax.all_gather(w_query, "seq", axis=0, tiled=True),
        lax.all_gather(w_key, "seq", axis=0, tiled=True),
        lax.all_gather(w_value, "seq", axis=0, tiled=True),
        lax.all_gather(w_gate, "seq", axis=0, tiled=True),
        lax.all_gather(w_out, "seq", axis=1, tiled=True),
        lax.all_gather(w_up, "seq", axis=0, tiled=True),
        lax.all_gather(w_down, "seq", axis=1, tiled=True),
    )
    d_hidden = low_dot(out_grad, back_down.T)
    d_up = smooth_back(d_hidden)[0].astype(jnp.bfloat16)
    grad_down = low_dot(hidden.T, out_grad)
    grad_up = low_dot(normed2.T, d_up)
    d_normed2 = lax.psum(low_dot(d_up, back_up.T), "tp")
    d_resid_part, grad_gain2, grad_bias2 = norm2_back(d_normed2)
    d_resid = out_grad.astype(jnp.float32) + d_resid_part
    d_attn = d_resid.astype(jnp.bfloat16)
    grad_out = low_dot(mixed.T, d_attn)
    d_mixed = low_dot(d_attn, back_out.T)
    d_gate_wide, d_grouped = gate_back(d_mixed)
    d_gate = d_gate_wide.astype(jnp.bfloat16)
    d_ret = group_back(d_grouped.reshape(tok_rows, local_heads, DV))[0].astype(jnp.bfloat16)
    d_ret_wide = d_ret.astype(jnp.float32)
    outgoing = exact_form("ihd,ihv->hdv", qdec * query_wide, d_ret_wide)
    later_grad, unused_back = prefix(
        (outgoing, carry_decay), "seq", decay_chain, (empty_state, unit_decay), True
    )
    d_probs = low_form("ihv,jhv->hij", d_ret, value)
    d_scores = (d_probs * dmask).astype(jnp.bfloat16)
    d_query = low_form("hij,jhd->ihd", d_scores, key) + qdec * exact_form(
        "ihv,hdv->ihd", d_ret_wide, prior_state
    )
    d_key = low_form("hij,ihd->jhd", d_scores, query) + kdec * exact_form(
        "jhv,hdv->jhd", value_wide, later_grad
    )
    d_value = low_form("hij,ihv->jhv", probs, d_ret) + kdec * exact_form(
        "jhd,hdv->jhv", key_wide, later_grad
    )
    unused_turn, turn_back = jax.vjp(turn, query_raw)
    d_query_raw = turn_back(d_query)[0].reshape(tok_rows, local_heads * DK).astype(jnp.bfloat16)
    d_key_raw = turn_back(d_key)[0].reshape(tok_rows, local_heads * DK).astype(jnp.bfloat16)
    d_value_flat = d_value.reshape(tok_rows, local_heads * DV).astype(jnp.bfloat16)
    grad_query = low_dot(normed1.T, d_query_raw)
    grad_key = low_dot(normed1.T, d_key_raw)
    grad_value = low_dot(normed1.T, d_value_flat)
    grad_gate = low_dot(normed1.T, d_gate)
    d_normed1_part = (
        low_dot(d_query_raw, back_query.T)
        + low_dot(d_key_raw, back_key.T)
        + low_dot(d_value_flat, back_value.T)
        + low_dot(d_gate, back_gate.T)
    )
    d_normed1 = lax.psum(d_normed1_part.astype(jnp.bfloat16), "tp").astype(jnp.float32)
    unused_norm, norm1_back = jax.vjp(layer_norm, stream, gain1, bias1)
    d_stream_part, grad_gain1, grad_bias1 = norm1_back(d_normed1)
    tokens_grad = d_resid + d_stream_part
    (
        gain1_grad,
        bias1_grad,
        gain2_grad,
        bias2_grad,
        query_grad,
        key_grad,
        value_grad,
        gate_grad,
        out_weight_grad,
        up_grad,
        down_grad,
    ) = (
        lax.psum_scatter(
            grad_gain1.astype(jnp.bfloat16), "seq", scatter_dimension=0, tiled=True
        ).astype(jnp.float32),
        lax.psum_scatter(
            grad_bias1.astype(jnp.bfloat16), "seq", scatter_dimension=0, tiled=True
        ).astype(jnp.float32),
        lax.psum_scatter(
            grad_gain2.astype(jnp.bfloat16), "seq", scatter_dimension=0, tiled=True
        ).astype(jnp.float32),
        lax.psum_scatter(
            grad_bias2.astype(jnp.bfloat16), "seq", scatter_dimension=0, tiled=True
        ).astype(jnp.float32),
        lax.psum_scatter(
            grad_query.astype(jnp.bfloat16), "seq", scatter_dimension=0, tiled=True
        ).astype(jnp.float32),
        lax.psum_scatter(
            grad_key.astype(jnp.bfloat16), "seq", scatter_dimension=0, tiled=True
        ).astype(jnp.float32),
        lax.psum_scatter(
            grad_value.astype(jnp.bfloat16), "seq", scatter_dimension=0, tiled=True
        ).astype(jnp.float32),
        lax.psum_scatter(
            grad_gate.astype(jnp.bfloat16), "seq", scatter_dimension=0, tiled=True
        ).astype(jnp.float32),
        lax.psum_scatter(
            grad_out.astype(jnp.bfloat16), "seq", scatter_dimension=1, tiled=True
        ).astype(jnp.float32),
        lax.psum_scatter(
            grad_up.astype(jnp.bfloat16), "seq", scatter_dimension=0, tiled=True
        ).astype(jnp.float32),
        lax.psum_scatter(
            grad_down.astype(jnp.bfloat16), "seq", scatter_dimension=1, tiled=True
        ).astype(jnp.float32),
    )
    return (
        block_out,
        tokens_grad,
        gain1_grad,
        bias1_grad,
        query_grad,
        key_grad,
        value_grad,
        gate_grad,
        out_weight_grad,
        gain2_grad,
        bias2_grad,
        up_grad,
        down_grad,
    )


def solution(mesh):
    in_specs = (
        P("seq", None),
        P("seq"),
        P("seq"),
        P("seq", "tp"),
        P("seq", "tp"),
        P("seq", "tp"),
        P("seq", "tp"),
        P("tp", "seq"),
        P("seq"),
        P("seq"),
        P("seq", "tp"),
        P("tp", "seq"),
        P("tp"),
        P("seq", None),
    )
    out_specs = (
        P("seq", None),
        P("seq", None),
        P("seq"),
        P("seq"),
        P("seq", "tp"),
        P("seq", "tp"),
        P("seq", "tp"),
        P("seq", "tp"),
        P("tp", "seq"),
        P("seq"),
        P("seq"),
        P("seq", "tp"),
        P("tp", "seq"),
    )
    return jax.shard_map(body, mesh=mesh, in_specs=in_specs, out_specs=out_specs, check_vma=False)
```

profile of v0, /device:TPU:1, one launch (start us, length us, event | category | flops | bytes accessed | tf_op | source)
XLA Modules:
  0.0 2610.0 jit_solution(10040538969281708651)
XLA Ops:
  15.5 158.1 %all-reduce.14 = (bf16[2048]{0:T(1024)(128)(2,1)S(1)}, bf16[2048]{0:T(1024)(128)(2,1)S(1)}, bf16[2048]{0:T(1024)(128)(2,1)}, bf16[2048]{0:T(1024)(128)(2,1)}) all-reduce(bf16[2048]{0:T(1024)(128)(2,1)S(1)} %dynamic-update-slice.1, bf16[2048]{0:T(1024)(128)(2,1)S(1)} %dynamic-update-slice, ...), channel_id=1, replica_groups=mesh['tp'=4,'seq'=32] {'seq'}, use_global_device_ids=true, to_apply=%add.5 | all-reduce | flops 8192 | bytes 32768
  184.1 56.0 %all-gather.15.cloned.1.call-done = bf16[2048,1024]{1,0:T(8,128)(2,1)} async-done(((bf16[64,1024]{1,0:T(8,128)(2,1)}), bf16[2048,1024]{1,0:T(8,128)(2,1)}) %all-gather.15.cloned.1.call-update) | async-done | bytes 4194320 | tf_op jit(solution)/shard_map/all_gather | solution.py:100
  248.1 78.4 %all-reduce.6 = f32[64]{0:T(128)S(1)} all-reduce(f32[64]{0:T(128)} %get-tuple-element.207), channel_id=2, replica_groups=mesh['tp'=4,'seq'=32] {'seq'}, use_global_device_ids=true, to_apply=%add.6 | all-reduce | flops 64 | bytes 512
  327.9 178.8 %all-gather.27.cloned.1.call-done = f32[64,256,512]{2,1,0:T(8,128)} async-done(((f32[2,256,512]{2,1,0:T(8,128)}), f32[64,256,512]{2,1,0:T(8,128)}) %all-gather.27.cloned.1.call-update) | async-done | bytes 33554448 | tf_op jit(solution)/shard_map/all_gather | solution.py:14
  512.7 75.9 %all-gather.13.cloned.1.call-done = bf16[2048,1024]{1,0:T(8,128)(2,1)} async-done(((bf16[64,1024]{1,0:T(8,128)(2,1)}), bf16[2048,1024]{1,0:T(8,128)(2,1)}) %all-gather.13.cloned.1.call-update) | async-done | bytes 4194320 | tf_op jit(solution)/shard_map/all_gather | solution.py:101
  593.3 77.5 %all-gather.21.cloned.1.call-done = bf16[1024,2048]{0,1:T(8,128)(2,1)} async-done(((bf16[1024,64]{0,1:T(8,128)(2,1)}), bf16[1024,2048]{0,1:T(8,128)(2,1)}) %all-gather.21.cloned.1.call-update) | async-done | bytes 4194320 | tf_op jit(solution)/shard_map/all_gather | solution.py:102
  677.2 76.0 %all-gather.25.cloned.1.call-done = bf16[1024,2048]{0,1:T(8,128)(2,1)} async-done(((bf16[1024,64]{0,1:T(8,128)(2,1)}), bf16[1024,2048]{0,1:T(8,128)(2,1)}) %all-gather.25.cloned.1.call-update) | async-done | bytes 4194320 | tf_op jit(solution)/shard_map/all_gather | solution.py:104
  757.7 54.9 %all-reduce.20.cloned.1.call-done = f32[256,2048]{1,0:T(8,128)} async-done(((f32[256,2048]{1,0:T(8,128)}), f32[256,2048]{1,0:T(8,128)}) %all-reduce.20.cloned.1.call-update) | async-done | bytes 2097168 | tf_op jit(solution)/shard_map/psum | solution.py:160
  816.9 80.9 %all-gather.23.cloned.1.call-done = bf16[2048,1024]{1,0:T(8,128)(2,1)} async-done(((bf16[64,1024]{1,0:T(8,128)(2,1)}), bf16[2048,1024]{1,0:T(8,128)(2,1)}) %all-gather.23.cloned.1.call-update) | async-done | bytes 4194320 | tf_op jit(solution)/shard_map/all_gather | solution.py:103
  897.8 5.5 fusion.33
  907.0 56.2 %all-reduce.22.cloned.1.call-done = f32[256,2048]{1,0:T(8,128)} async-done(((f32[256,2048]{1,0:T(8,128)}), f32[256,2048]{1,0:T(8,128)}) %all-reduce.22.cloned.1.call-update) | async-done | bytes 2097168 | tf_op jit(solution)/shard_map/psum | solution.py:186
  986.6 5.0 convolution_convert_fusion
  992.3 5.0 convolution_convert_fusion.3
  1002.6 5.0 convolution_convert_fusion.7
  1014.1 229.7 %all-gather.29.cloned.1.call-done = f32[64,256,512]{2,1,0:T(8,128)} async-done(((f32[2,256,512]{2,1,0:T(8,128)}), f32[64,256,512]{2,1,0:T(8,128)}) %all-gather.29.cloned.1.call-update) | async-done | bytes 33554448 | tf_op jit(solution)/shard_map/all_gather | solution.py:14
  1244.0 70.6 %while.27 = (s32[]{:T(128)}, f32[2,256,512]{2,1,0:T(8,128)S(1)}, s32[]{:T(128)}, f32[32,2]{1,0:T(8,128)}, f32[32,2,256,512]{3,2,1,0:T(8,128)}, /*index=5*/s32[]{:T(128)}, s32[]{:T(128)}, s32[]{:T(128)}, s32[]{:T(128)}) while((s32[]{:T(128)}, f32[2,256,512]{2,1,0:T(8,128)S(1)}, s32[]{:T(128)}, f32[32,2]{1,0:T(8,128)}, ...), condition=%wide.region_16.17_spmd, body=%wide.region_15.16_spmd.sunk | while | flops 524294 | bytes 3145907 | solution.py:23
  1344.3 69.2 %reduce-scatter.18.cloned.1.call-done = bf16[64,1024]{1,0:T(8,128)(2,1)} async-done(((bf16[2048,1024]{1,0:T(8,128)(2,1)}), bf16[64,1024]{1,0:T(8,128)(2,1)}) %reduce-scatter.18.cloned.1.call-update) | async-done | bytes 131088 | tf_op jit(solution)/shard_map/reduce_scatter | solution.py:269
  1415.2 188.3 %reduce-scatter.20.cloned.1.call-done = bf16[1024,64]{0,1:T(8,128)(2,1)} async-done(((bf16[1024,2048]{0,1:T(8,128)(2,1)}), bf16[1024,64]{0,1:T(8,128)(2,1)}) %reduce-scatter.20.cloned.1.call-update) | async-done | bytes 131088 | tf_op jit(solution)/shard_map/reduce_scatter | solution.py:272
  1605.1 187.3 %reduce-scatter.14.cloned.1.call-done = bf16[64,1024]{1,0:T(8,128)(2,1)} async-done(((bf16[2048,1024]{1,0:T(8,128)(2,1)}), bf16[64,1024]{1,0:T(8,128)(2,1)}) %reduce-scatter.14.cloned.1.call-update) | async-done | bytes 131088 | tf_op jit(solution)/shard_map/reduce_scatter | solution.py:263
  1794.0 187.6 %reduce-scatter.16.cloned.1.call-done = bf16[1024,64]{0,1:T(8,128)(2,1)} async-done(((bf16[1024,2048]{0,1:T(8,128)(2,1)}), bf16[1024,64]{0,1:T(8,128)(2,1)}) %reduce-scatter.16.cloned.1.call-update) | async-done | bytes 131088 | tf_op jit(solution)/shard_map/reduce_scatter | solution.py:266
  1983.3 77.6 %all-reduce.24.cloned.1.call-done = (bf16[256,2048]{1,0:T(8,128)(2,1)}, bf16[256,2048]{1,0:T(8,128)(2,1)}) async-done(((bf16[256,2048]{1,0:T(8,128)(2,1)}, bf16[256,2048]{1,0:T(8,128)(2,1)}), (bf16[256,2048]{1,0:T(8,128)(2,1)}, bf16[256,2048]{1,0:T(8,128)(2,1)})) %all-reduce.24.cloned.1.call-update) | async-done | bytes 2097168 | tf_op jit(solution)/shard_map/psum | solution.py:171
  2065.2 158.7 %all-reduce.13 = (bf16[2048]{0:T(1024)(128)(2,1)S(1)}, bf16[2048]{0:T(1024)(128)(2,1)S(1)}, bf16[2048]{0:T(1024)(128)(2,1)S(1)}, bf16[2048]{0:T(1024)(128)(2,1)S(1)}) all-reduce(bf16[2048]{0:T(1024)(128)(2,1)S(1)} %get-tuple-element.145, bf16[2048]{0:T(1024)(128)(2,1)S(1)} %reduce_sum.168, ...), channel_id=5, replica_groups=mesh['tp'=4,'seq'=32] {'seq'}, use_global_device_ids=true, to_apply=%region_21.22.clone | all-reduce | flops 8192 | bytes 32768
  2232.7 178.2 %reduce-scatter.10.cloned.1.call-done = bf16[64,512]{1,0:T(8,128)(2,1)} async-done(((bf16[2048,512]{1,0:T(8,128)(2,1)}), bf16[64,512]{1,0:T(8,128)(2,1)}) %reduce-scatter.10.cloned.1.call-update) | async-done | bytes 65552 | tf_op jit(solution)/shard_map/reduce_scatter | solution.py:257
  2412.4 189.3 %reduce-scatter.12.cloned.1.call-done = bf16[64,1024]{1,0:T(8,128)(2,1)} async-done(((bf16[2048,1024]{1,0:T(8,128)(2,1)}), bf16[64,1024]{1,0:T(8,128)(2,1)}) %reduce-scatter.12.cloned.1.call-update) | async-done | bytes 131088 | tf_op jit(solution)/shard_map/reduce_scatter | solution.py:260
  (376 shorter events, 212.9 us)
Async XLA Ops:
  7.2 170.8 %all-gather.17.cloned.1.call-start = ((), (), s32[]{:S(2)}) async-start(), calls=%async_computation.9 | async-start | bytes 2162688 | tf_op jit(solution)/shard_map/all_gather | solution.py:98
  7.9 172.9 %all-gather.19.cloned.1.call-start = ((), (), s32[]{:S(2)}) async-start(), calls=%async_computation.10 | async-start | bytes 2162688 | tf_op jit(solution)/shard_map/all_gather | solution.py:99
  8.7 231.4 %all-gather.15.cloned.1.call-start = ((), (), s32[]{:S(2)}) async-start(), calls=%async_computation.8 | async-start | bytes 4325376 | tf_op jit(solution)/shard_map/all_gather | solution.py:100
  9.4 497.2 %all-gather.27.cloned.1.call-start = ((), (), s32[]{:S(2)}) async-start(), calls=%async_computation.23 | async-start | bytes 34603008 | tf_op jit(solution)/shard_map/all_gather | solution.py:14
  177.4 329.6 %copy-start.50 = (f32[256,2]{0,1:T(2,128)}, f32[256,2]{0,1:T(2,128)S(1)}, u32[]{:S(2)}) copy-start(f32[256,2]{0,1:T(2,128)S(1)} %get-tuple-element.204) | copy-start | bytes 6148
  184.1 322.9 %copy-start.24 = (bf16[256,2,128]{2,0,1:T(8,128)(2,1)}, bf16[256,2,128]{2,0,1:T(8,128)(2,1)S(1)}, u32[]{:S(2)}) copy-start(bf16[256,2,128]{2,0,1:T(8,128)(2,1)S(1)} %get-tuple-element.189) | copy-start | bytes 393220
  246.1 342.5 %all-gather.13.cloned.1.call-start = ((), (), s32[]{:S(2)}) async-start(), calls=%async_computation.7 | async-start | bytes 4325376 | tf_op jit(solution)/shard_map/all_gather | solution.py:101
  246.7 424.2 %all-gather.21.cloned.1.call-start = ((), (), s32[]{:S(2)}) async-start(), calls=%async_computation.11 | async-start | bytes 4325376 | tf_op jit(solution)/shard_map/all_gather | solution.py:102
  247.3 506.0 %all-gather.25.cloned.1.call-start = ((), (), s32[]{:S(2)}) async-start(), calls=%async_computation.14 | async-start | bytes 4325376 | tf_op jit(solution)/shard_map/all_gather | solution.py:104
  248.0 564.6 %all-reduce.20.cloned.1.call-start = ((), (), s32[]{:S(2)}) async-start(), calls=%async_computation.12 | async-start | bytes 4194304 | tf_op jit(solution)/shard_map/psum | solution.py:160
  326.7 180.0 %copy-start.42 = (pred[256,256]{1,0:T(8,128)(4,1)}, pred[256,256]{1,0:T(8,128)(4,1)S(1)}, u32[]{:S(2)}) copy-start(pred[256,256]{1,0:T(8,128)(4,1)S(1)} %subtract_compare_fusion) | copy-start | bytes 196612
  326.9 179.9 %copy-start.38 = (f32[256,256]{1,0:T(8,128)}, f32[256,256]{1,0:T(8,128)S(1)}, u32[]{:S(2)}) copy-start(f32[256,256]{1,0:T(8,128)S(1)} %subtract_maximum_fusion) | copy-start | bytes 786436
  675.8 221.9 %all-gather.23.cloned.1.call-start = ((), (), s32[]{:S(2)}) async-start(), calls=%async_computation.13 | async-start | bytes 4325376 | tf_op jit(solution)/shard_map/all_gather | solution.py:103
  676.6 286.6 %all-reduce.22.cloned.1.call-start = ((), (), s32[]{:S(2)}) async-start(), calls=%async_computation.15 | async-start | bytes 4194304 | tf_op jit(solution)/shard_map/psum | solution.py:186
  906.7 337.1 %all-gather.29.cloned.1.call-start = ((), (), s32[]{:S(2)}) async-start(), calls=%async_computation.24 | async-start | bytes 34603008 | tf_op jit(solution)/shard_map/all_gather | solution.py:14
  981.9 431.6 %reduce-scatter.18.cloned.1.call-start = ((), (), s32[]{:S(2)}) async-start(), calls=%async_computation.21 | async-start | bytes 4325376 | tf_op jit(solution)/shard_map/reduce_scatter | solution.py:269
  986.5 617.0 %reduce-scatter.20.cloned.1.call-start = ((), (), s32[]{:S(2)}) async-start(), calls=%async_computation.22 | async-start | bytes 4325376 | tf_op jit(solution)/shard_map/reduce_scatter | solution.py:272
  991.6 800.7 %reduce-scatter.14.cloned.1.call-start = ((), (), s32[]{:S(2)}) async-start(), calls=%async_computation.19 | async-start | bytes 4325376 | tf_op jit(solution)/shard_map/reduce_scatter | solution.py:263
  997.3 984.3 %reduce-scatter.16.cloned.1.call-start = ((), (), s32[]{:S(2)}) async-start(), calls=%async_computation.20 | async-start | bytes 4325376 | tf_op jit(solution)/shard_map/reduce_scatter | solution.py:266
  1002.1 1058.7 %all-reduce.24.cloned.1.call-start = ((), (), s32[]{:S(2)}) async-start(), calls=%async_computation.25 | async-start | bytes 4194304 | tf_op jit(solution)/shard_map/psum | solution.py:171
  1332.3 898.9 %reduce-scatter.8.cloned.1.call-start = ((), (), s32[]{:S(2)}) async-start(), calls=%async_computation.16 | async-start | bytes 2162688 | tf_op jit(solution)/shard_map/reduce_scatter | solution.py:254
  1336.7 1074.2 %reduce-scatter.10.cloned.1.call-start = ((), (), s32[]{:S(2)}) async-start(), calls=%async_computation.17 | async-start | bytes 2162688 | tf_op jit(solution)/shard_map/reduce_scatter | solution.py:257
  1339.0 1262.7 %reduce-scatter.12.cloned.1.call-start = ((), (), s32[]{:S(2)}) async-start(), calls=%async_computation.18 | async-start | bytes 4325376 | tf_op jit(solution)/shard_map/reduce_scatter | solution.py:260
  1415.2 648.9 %copy-start.68 = (f32[256]{0:T(256)S(1)}, f32[256]{0:T(256)}, u32[]{:S(2)}) copy-start(f32[256]{0:T(256)} %copy-done.67) | copy-start | bytes 3076
  (78 other events, 1059.6 us)
Sparse Core Ops, SparseCore 0:
  11.1 74.2 all-gather.16
  88.6 69.3 all-gather.18
  161.0 79.0 all-gather.14
  246.2 260.3 all-gather.26
  509.6 78.9 all-gather.12
  591.5 79.2 all-gather.20
  673.9 79.2 all-gather.24
  756.4 56.2 all-reduce.19
  816.2 81.5 all-gather.22
  906.8 56.2 all-reduce.21
  982.1 261.7 all-gather.28
  1246.1 167.4 reduce-scatter.17
  1415.9 187.4 reduce-scatter.19
  1605.7 186.5 reduce-scatter.13
  1794.6 186.9 reduce-scatter.15
  1984.6 76.1 all-reduce.23
  2063.1 164.7 reduce-scatter.7
  2230.1 180.7 reduce-scatter.9
  2413.4 188.2 reduce-scatter.11
where the time goes:
time: 2640 us; the launch traced here: 2610 us
  waiting for transfers between devices  1970 us (75%)
  blocking collectives  395 us (15%)
  other arithmetic  90.4 us (3%)
  matrix products  87.6 us (3%)
  local copies, waits for them, and re-layouts  49 us (2%)
    all_gather x2, waiting for transfers between devices, prefix(): gathered = jax.tree.map(lambda a: lax.all_gather(a, axis), part)  408 us
    unnamed x3, blocking collectives  395 us
    reduce_scatter x1, waiting for transfers between devices, body(): lax.psum_scatter(grad_value.astype(jnp.bfloat16), 'seq', scatter_dimensio...  189 us
    reduce_scatter x1, waiting for transfers between devices, body(): lax.psum_scatter(grad_down.astype(jnp.bfloat16), 'seq', scatter_dimension...  188 us
    reduce_scatter x1, waiting for transfers between devices, body(): lax.psum_scatter(grad_out.astype(jnp.bfloat16), 'seq', scatter_dimension=...  188 us
    reduce_scatter x1, waiting for transfers between devices, body(): lax.psum_scatter(grad_gate.astype(jnp.bfloat16), 'seq', scatter_dimension...  187 us
    reduce_scatter x1, waiting for transfers between devices, body(): lax.psum_scatter(grad_key.astype(jnp.bfloat16), 'seq', scatter_dimension=...  178 us
    all_gather x1, waiting for transfers between devices, body(): lax.all_gather(w_up, 'seq', axis=0, tiled=True)  80.9 us
  transfers between devices with their start and end apart: 19, of which 16 were waited for; matrix products, arithmetic and copies ran while one was open for 7% of the time, Pallas kernels for 0%

commit v1 on v0

v1 whole, which is shorter than its diff:
```python
import itertools

import jax
import jax.numpy as jnp
from jax import lax
from jax.sharding import Mesh, PartitionSpec as P

DK = 256
DV = 512
AXES = ("zl", "c", "x", "zh", "y")
SIZES = {"zl": 2, "c": 2, "x": 4, "zh": 2, "y": 4}
SPANS = ("x", "c", "y")
BF = jnp.bfloat16
F32 = jnp.float32


def pairs(axes, move):
    def flat(place):
        at = 0
        for axis in axes:
            at = at * SIZES[axis] + place[axis]
        return at

    found = []
    for values in itertools.product(*[range(SIZES[axis]) for axis in axes]):
        place = dict(zip(axes, values))
        target = move(dict(place))
        if target is not None:
            found.append((flat(place), flat(target)))
    return found


def swap_roles(values):
    return lax.ppermute(
        values, ("c", "zh"), pairs(("c", "zh"), lambda p: {"c": p["zh"], "zh": p["c"]})
    )


def z_shift(values, shift):
    def move(place):
        z = (place["zh"] * 2 + place["zl"] + shift) % 4
        return {"zl": z % 2, "zh": z // 2}

    return lax.ppermute(values, ("zl", "zh"), pairs(("zl", "zh"), move))


def z_shift_home(values, shift):
    def move(place):
        z = (place["zh"] * 2 + place["zl"] + shift) % 4
        if z // 2 != place["c"]:
            return None
        return {"zl": z % 2, "zh": z // 2, "c": place["c"]}

    return lax.ppermute(values, ("zl", "c", "zh"), pairs(("zl", "c", "zh"), move))


def core_from_home(values):
    def move(place):
        if place["zh"] != place["c"]:
            return None
        return {"c": 1 - place["c"], "zh": place["zh"]}

    return lax.ppermute(values, ("c", "zh"), pairs(("c", "zh"), move))


def core_swap(values):
    return lax.ppermute(values, "c", [(0, 1), (1, 0)])


def z_reduce(values):
    part = values.astype(BF)
    rows = part.shape[0] // 4
    total = values[:rows]
    for shift in (1, 3, 2):
        total = total + z_shift(part[shift * rows : (shift + 1) * rows], shift).astype(F32)
    return total


def z_gather(values):
    near, far, across = z_shift(values, 3), z_shift(values, 1), z_shift(values, 2)
    return jnp.concatenate([values, near, across, far], axis=0)


def z_gather_home(values, place, home):
    rows = values.shape[0]
    near, far, across = z_shift_home(values, 3), z_shift_home(values, 1), z_shift_home(values, 2)
    full = jnp.concatenate([values, near, across, far] * 2, axis=0)
    full = lax.dynamic_slice_in_dim(full, (4 - place) % 4 * rows, 4 * rows, 0)
    return jnp.where(home, full, core_from_home(full))


def nn(left, right):
    return jnp.dot(left, right, preferred_element_type=F32)


def nt(left, right):
    return lax.dot_general(left, right, (((1,), (1,)), ((), ())), preferred_element_type=F32)


def tn(left, right):
    return lax.dot_general(left, right, (((0,), (0,)), ((), ())), preferred_element_type=F32)


def norm_parts(values):
    center = values - jnp.mean(values, axis=-1, keepdims=True)
    spread = jnp.mean(center * center, axis=-1, keepdims=True)
    scale = lax.rsqrt(spread + 1e-05)
    return center * scale, scale


def norm_back(grad, hat, scale):
    mean_grad = jnp.mean(grad, axis=-1, keepdims=True)
    mean_both = jnp.mean(grad * hat, axis=-1, keepdims=True)
    return (grad - mean_grad - hat * mean_both) * scale


def span_scan(fresh, rate, reverse):
    parts = fresh.astype(BF).reshape(32, 16, DV)
    parts = lax.all_to_all(parts, SPANS, 0, 0, tiled=True)
    at = jnp.arange(32).astype(F32)
    steps = at[:, None] - 1.0 - at[None, :]
    decay = jnp.where(steps >= 0.0, jnp.exp(-256.0 * rate * jnp.maximum(steps, 0.0)), 0.0)
    if reverse:
        decay = decay.T
    carried = lax.dot_general(
        decay,
        parts.astype(F32),
        (((1,), (0,)), ((), ())),
        precision=lax.Precision.HIGHEST,
    ).astype(BF)
    return lax.all_to_all(carried, SPANS, 0, 0, tiled=True).reshape(2, DK, DV)


def scatter_direct(grad, core):
    cols = grad.shape[1]
    grad = grad.astype(BF).reshape(4, 2, 256, cols)
    mine = lax.dynamic_index_in_dim(grad, core, 1, False)
    other = lax.dynamic_index_in_dim(grad, 1 - core, 1, False)
    total = (mine.astype(F32) + core_swap(other).astype(F32)).astype(BF)
    total = lax.all_to_all(total.reshape(16, 64, cols), ("x", "y"), 0, 0, tiled=True)
    return jnp.sum(total.astype(F32), axis=0)


def scatter_wide(grad):
    return lax.psum_scatter(grad.astype(BF), SPANS, scatter_dimension=0, tiled=True)


def body(
    tokens,
    norm1_gain,
    norm1_bias,
    w_query,
    w_key,
    w_value,
    w_gate,
    w_out,
    norm2_gain,
    norm2_bias,
    w_up,
    w_down,
    decay_rate,
    out_grad,
):
    x, y, c = lax.axis_index("x"), lax.axis_index("y"), lax.axis_index("c")
    zl, zh = lax.axis_index("zl"), lax.axis_index("zh")
    z = zh * 2 + zl
    home = zh == c
    span = x * 8 + c * 4 + y

    gains = jnp.stack([norm1_gain, norm1_bias, norm2_gain, norm2_bias], axis=1)
    gains = jnp.pad(gains, ((0, 0), (0, 124)))
    first = swap_roles(jnp.concatenate([w_key, w_value, gains], axis=1))
    second = swap_roles(jnp.concatenate([w_query, w_gate, w_out.T, w_up, w_down.T], axis=1))
    rate = swap_roles(decay_rate)
    tokens = swap_roles(tokens)
    out_grad = swap_roles(out_grad)

    cols = first.shape[1]
    early = lax.all_to_all(
        jnp.broadcast_to(first[None], (16, 64, cols)), ("x", "y"), 0, 0, tiled=True
    )
    early_other = core_swap(early)
    low = jnp.where(c == 0, early, early_other).reshape(4, 1, 256, cols)
    high = jnp.where(c == 0, early_other, early).reshape(4, 1, 256, cols)
    early = jnp.concatenate([low, high], axis=1).reshape(2048, cols)
    late = lax.all_gather(second, SPANS, axis=0, tiled=True)
    full_key, full_value, gains = early[:, :512], early[:, 512:1536], early[:, 1536:].T.astype(F32)
    gain1, bias1, gain2, bias2 = gains[0], gains[1], gains[2], gains[3]
    full_query, full_gate = late[:, :512], late[:, 512:1536]
    full_out, full_up, full_down = late[:, 1536:2560], late[:, 2560:3584], late[:, 3584:]

    tokens = lax.dynamic_slice_in_dim(jnp.concatenate([tokens, tokens]), z * 64, 256, 0)
    out_grad = lax.dynamic_slice_in_dim(jnp.concatenate([out_grad, out_grad]), z * 64, 256, 0)
    index = ((jnp.arange(256) + z * 64) % 256).astype(F32)
    half = DK // 2
    position = (span * 256).astype(F32) + index
    freq = 10000.0 ** (-jnp.arange(half).astype(F32) / half)
    angle = position[:, None] * freq[None, :]
    cosine, sine = jnp.cos(angle), jnp.sin(angle)

    def turn(values):
        a, b = values[:, :half], values[:, half:]
        return jnp.concatenate([a * cosine - b * sine, b * cosine + a * sine], axis=1)

    def turn_back(values):
        a, b = values[:, :half], values[:, half:]
        return jnp.concatenate([a * cosine + b * sine, b * cosine - a * sine], axis=1)

    stream = tokens.astype(F32)
    hat1, scale1 = norm_parts(stream)
    normed1 = (hat1 * gain1 + bias1).astype(BF)

    offset = index[:, None] - index[None, :]
    masks, qdecs, kdecs = [], [], []
    for h in range(2):
        masks.append(
            jnp.where(offset >= 0.0, jnp.exp(-rate[h] * jnp.maximum(offset, 0.0)), 0.0)
        )
        qdecs.append(jnp.exp(-rate[h] * (index + 1.0))[:, None])
        kdecs.append(jnp.exp(-rate[h] * (255.0 - index))[:, None])

    key_raw = nn(normed1, full_key)
    value = nn(normed1, full_value).astype(BF)
    keys, values, fresh = [], [], []
    for h in range(2):
        keys.append(turn(key_raw[:, h * DK : (h + 1) * DK]).astype(BF))
        values.append(value[:, h * DV : (h + 1) * DV])
        fresh.append(tn((kdecs[h] * keys[h].astype(F32)).astype(BF), values[h]))
    scan_rate = jnp.where(x < 2, rate[0], rate[1])
    state = span_scan(jnp.stack(fresh), scan_rate, False)

    query_raw = nn(normed1, full_query)
    gate_raw = nn(normed1, full_gate)
    queries, probs, hats, scales = [], [], [], []
    for h in range(2):
        queries.append(turn(query_raw[:, h * DK : (h + 1) * DK]).astype(BF))
        probs.append((nt(queries[h], keys[h]) * masks[h]).astype(BF))
        retained = nn(probs[h], values[h]) + qdecs[h] * nn(queries[h], state[h])
        hat, scale = norm_parts(retained)
        hats.append(hat)
        scales.append(scale)
    grouped = jnp.concatenate(hats, axis=1)
    gate_sig = jax.nn.sigmoid(gate_raw)
    gate_act = gate_raw * gate_sig
    mixed = (gate_act * grouped).astype(BF)

    resid = stream[:64] + z_reduce(nt(mixed, full_out))
    hat2, scale2 = norm_parts(resid)
    normed2 = z_gather((hat2 * gain2 + bias2).astype(BF))
    up_raw = nn(normed2, full_up)

    def smooth(values):
        return jax.nn.gelu(values, approximate=True)

    hidden_wide, smooth_back = jax.vjp(smooth, up_raw)
    hidden = hidden_wide.astype(BF)
    d_hidden = nn(out_grad, full_down)
    d_up = smooth_back(d_hidden)[0].astype(BF)
    d_normed2 = z_reduce(nt(d_up, full_up))

    ffn = z_reduce(nt(hidden, full_down))
    block_out = z_gather_home((resid + ffn).astype(BF), z, home)

    own_grad = out_grad[:64].astype(F32)
    d_resid = own_grad + norm_back(d_normed2 * gain2, hat2, scale2)
    grad_gain2 = jnp.sum(d_normed2 * hat2, axis=0)
    grad_bias2 = jnp.sum(d_normed2, axis=0)
    d_attn = z_gather(d_resid.astype(BF))

    grad_ffn = scatter_wide(jnp.concatenate([tn(normed2, d_up), tn(out_grad, hidden)], axis=1))

    d_mixed = nn(d_attn, full_out)
    d_gate = (d_mixed * grouped * gate_sig * (1.0 + gate_raw * (1.0 - gate_sig))).astype(BF)
    d_grouped = d_mixed * gate_act
    d_rets, outgoing = [], []
    for h in range(2):
        d_ret = norm_back(d_grouped[:, h * DV : (h + 1) * DV], hats[h], scales[h]).astype(BF)
        d_rets.append(d_ret)
        outgoing.append(tn((qdecs[h] * queries[h].astype(F32)).astype(BF), d_ret))
    later = span_scan(jnp.stack(outgoing), scan_rate, True)

    grad_gate = scatter_wide(jnp.concatenate([tn(normed1, d_gate), tn(d_attn, mixed)], axis=1))

    d_query_raw, d_key_raw, d_value = [], [], []
    for h in range(2):
        d_scores = (nt(d_rets[h], values[h]) * masks[h]).astype(BF)
        d_query = nn(d_scores, keys[h]) + qdecs[h] * nt(d_rets[h], state[h])
        d_key = tn(d_scores, queries[h]) + kdecs[h] * nt(values[h], later[h])
        d_value.append((tn(probs[h], d_rets[h]) + kdecs[h] * nn(keys[h], later[h])).astype(BF))
        d_query_raw.append(turn_back(d_query).astype(BF))
        d_key_raw.append(turn_back(d_key).astype(BF))
    d_query_raw = jnp.concatenate(d_query_raw, axis=1)
    d_key_raw = jnp.concatenate(d_key_raw, axis=1)
    d_value = jnp.concatenate(d_value, axis=1)

    d_normed1 = z_reduce(
        nt(d_query_raw, full_query)
        + nt(d_key_raw, full_key)
        + nt(d_value, full_value)
        + nt(d_gate, full_gate)
    )
    grad_qkv = scatter_direct(
        tn(normed1, jnp.concatenate([d_query_raw, d_key_raw, d_value], axis=1)), c
    )
    tokens_grad = d_resid + norm_back(d_normed1 * gain1, hat1[:64], scale1[:64])
    tokens_grad = z_gather_home(tokens_grad.astype(BF), z, home).astype(F32)
    grad_gain1 = jnp.sum(d_normed1 * hat1[:64], axis=0)
    grad_bias1 = jnp.sum(d_normed1, axis=0)

    vectors = jnp.stack([grad_gain1, grad_bias1, grad_gain2, grad_bias2])
    vectors = vectors.reshape(4, 32, 64).transpose(1, 0, 2).reshape(1, 32, 256)
    vectors = jnp.broadcast_to(vectors, (4, 32, 256)).reshape(128, 256)
    vectors = lax.all_to_all(vectors, AXES, 0, 0, tiled=True)
    vectors = jnp.sum(vectors, axis=0)

    grad_qkv = swap_roles(grad_qkv.astype(BF)).astype(F32)
    grad_gate = swap_roles(grad_gate).astype(F32)
    grad_ffn = swap_roles(grad_ffn).astype(F32)
    return (
        block_out,
        tokens_grad,
        vectors[:64],
        vectors[64:128],
        grad_qkv[:, :512],
        grad_qkv[:, 512:1024],
        grad_qkv[:, 1024:],
        grad_gate[:, :1024],
        grad_gate[:, 1024:].T,
        vectors[128:192],
        vectors[192:],
        grad_ffn[:, :1024],
        grad_ffn[:, 1024:].T,
    )


def solution(mesh):
    fine = Mesh(mesh.devices.reshape(2, 2, 4, 2, 4), AXES)
    seq, tp = ("x", "zh", "y"), ("zl", "c")
    rows, wide, tall, vector = P(seq, None), P(seq, tp), P(tp, seq), P(seq)
    in_specs = (
        rows,
        vector,
        vector,
        wide,
        wide,
        wide,
        wide,
        tall,
        vector,
        vector,
        wide,
        tall,
        P(tp),
        rows,
    )
    out_specs = (
        rows,
        rows,
        vector,
        vector,
        wide,
        wide,
        wide,
        wide,
        tall,
        vector,
        vector,
        wide,
        tall,
    )
    return jax.shard_map(body, mesh=fine, in_specs=in_specs, out_specs=out_specs, check_vma=False)
```

time: 2640 us -> 555 us (0.21)
  the two profiles are of different devices: /device:TPU:1 before, /device:TPU:53 now
where the time goes in v1:
time: 555 us; the launch traced here: 544 us
  starting transfers between devices  148 us (27%)
  waiting for transfers between devices  128 us (23%)
  matrix products  73.3 us (13%)
  local copies, waits for them, and re-layouts  73 us (13%)
  other arithmetic  67 us (12%)
  blocking collectives  36.4 us (7%)
  between operations  18.8 us (3%)
    unnamed x233, local copies, waits for them, and re-layouts  54.1 us
    all_to_all x1, waiting for transfers between devices, scatter_direct(): lax.all_to_all(total.reshape(16, 64, cols), ('x', 'y'), 0, 0, tiled=True)  41.5 us
    ppermute x8, starting transfers between devices, swap_roles(): lax.ppermute(values, ('c', 'zh'), pairs(('c', 'zh'), lambda p: {'c': p['z...  40 us
    all_to_all x1, blocking collectives, body(): lax.all_to_all(jnp.broadcast_to(first[None], (16, 64, cols)), ('x', 'y'),...  36.4 us
    ppermute x18, starting transfers between devices, z_shift(): return lax.ppermute(values, ('zl', 'zh'), pairs(('zl', 'zh'), move))  33.7 us
    ppermute x8, waiting for transfers between devices, swap_roles(): lax.ppermute(values, ('c', 'zh'), pairs(('c', 'zh'), lambda p: {'c': p['z...  31.5 us
    dot_general x15, matrix products, nt(): lax.dot_general(left, right, (((1,), (1,)), ((), ())), preferred_element_...  25.6 us
    ppermute x18, waiting for transfers between devices, z_shift(): return lax.ppermute(values, ('zl', 'zh'), pairs(('zl', 'zh'), move))  25.6 us
  transfers between devices with their start and end apart: 45, of which 18 were waited for; matrix products, arithmetic and copies ran while one was open for 28% of the time, Pallas kernels for 0%

profile of v1, /device:TPU:53, one launch (start us, length us, event | category | flops | bytes accessed | tf_op | source)
XLA Modules:
  0.0 544.3 jit_solution(11925740209257179921)
XLA Ops:
  16.9 7.6 %collective-permute-done.3 = bf16[64,4608]{1,0:T(8,128)(2,1)S(1)} collective-permute-done((bf16[64,4608]{1,0:T(8,128)(2,1)S(1)}, bf16[64,4608]{1,0:T(8,128)(2,1)S(1)}, u32[]{:S(2)}, u32[]{:S(2)}) %collective-permute-start.3) | collective-permute-done | bytes 589856 | tf_op jit(solution)/shard_map/ppermute | solution.py:34
  36.5 36.4 %all_to_all.39 = bf16[16,64,1664]{2,1,0:T(8,128)(2,1)} all-to-all(bf16[16,64,1664]{2,1,0:T(8,128)(2,1)S(1)} %broadcast_in_dim.10), channel_id=1, replica_groups=mesh['zl'=2,'c'=2,'x'=4,'zh'=2,'y'=4] {'x','y'}, dimensions={0} | all-to-all | bytes 6815744 | tf_op jit(solution)/shard_map/all_to_all | solution.py:179
  80.1 10.5 %collective-permute-done.4 = f32[2]{0:T(128)S(1)} collective-permute-done((f32[2]{0:T(128)S(1)}, f32[2]{0:T(128)S(1)}, u32[]{:S(2)}, u32[]{:S(2)}) %collective-permute-start.4) | collective-permute-done | bytes 40 | tf_op jit(solution)/shard_map/ppermute | solution.py:34
  106.1 14.6 %all-gather.2.cloned.1.call-done = bf16[2048,4608]{1,0:T(8,128)(2,1)} async-done(((bf16[64,4608]{1,0:T(8,128)(2,1)}), bf16[2048,4608]{1,0:T(8,128)(2,1)}) %all-gather.2.cloned.1.call-update) | async-done | bytes 18874384 | tf_op jit(solution)/shard_map/all_gather | solution.py:186
  125.3 7.3 %all-to-all-start.1 = ((bf16[32,16,512]{2,1,0:T(8,128)(2,1)}), bf16[32,16,512]{2,1,0:T(8,128)(2,1)S(1)}, u32[]{:S(2)}, u32[]{:S(2)}) async-start(bf16[32,16,512]{2,1,0:T(8,128)(2,1)} %bitcast.15), calls=%async_computation.1 | async-start | bytes 1048576 | tf_op jit(solution)/shard_map/all_to_all | solution.py:119
  134.2 5.9 %all-to-all-done.1 = bf16[32,16,512]{2,1,0:T(8,128)(2,1)S(1)} async-done(((bf16[32,16,512]{2,1,0:T(8,128)(2,1)}), bf16[32,16,512]{2,1,0:T(8,128)(2,1)S(1)}, u32[]{:S(2)}, u32[]{:S(2)}) %all-to-all-start.1) | async-done | bytes 524320 | tf_op jit(solution)/shard_map/all_to_all | solution.py:119
  142.1 9.2 %all-to-all-start.2 = ((bf16[32,16,512]{2,1,0:T(8,128)(2,1)}), bf16[32,16,512]{2,1,0:T(8,128)(2,1)}, u32[]{:S(2)}, u32[]{:S(2)}) async-start(bf16[32,16,512]{2,1,0:T(8,128)(2,1)} %copy.66), calls=%async_computation.2 | async-start | bytes 1048576 | tf_op jit(solution)/shard_map/all_to_all | solution.py:131
  152.9 5.8 %all-to-all-done.2 = bf16[32,16,512]{2,1,0:T(8,128)(2,1)} async-done(((bf16[32,16,512]{2,1,0:T(8,128)(2,1)}), bf16[32,16,512]{2,1,0:T(8,128)(2,1)}, u32[]{:S(2)}, u32[]{:S(2)}) %all-to-all-start.2) | async-done | bytes 524320 | tf_op jit(solution)/shard_map/all_to_all | solution.py:131
  180.9 6.3 %collective-permute-done.6 = bf16[64,2048]{1,0:T(8,128)(2,1)S(1)} collective-permute-done((bf16[64,2048]{1,0:T(8,128)(2,1)S(1)}, bf16[64,2048]{1,0:T(8,128)(2,1)S(1)}, u32[]{:S(2)}, u32[]{:S(2)}) %collective-permute-start.6) | collective-permute-done | bytes 262176 | tf_op jit(solution)/shard_map/ppermute | solution.py:44
  193.8 7.9 %collective-permute-done.18 = bf16[256,2048]{1,0:T(8,128)(2,1)S(1)} collective-permute-done((bf16[256,2048]{1,0:T(8,128)(2,1)S(1)}, bf16[256,2048]{1,0:T(8,128)(2,1)S(1)}, u32[]{:S(2)}, u32[]{:S(2)}) %collective-permute-start.18) | collective-permute-done | bytes 1048608 | tf_op jit(solution)/shard_map/ppermute | solution.py:34
  220.1 8.4 %pad_maximum_fusion.1 = bf16[2048,2048]{0,1:T(8,128)(2,1)} fusion(bf16[2048,1024]{0,1:T(8,128)(2,1)} %convolution_convert_fusion.1, bf16[2048,1024]{0,1:T(8,128)(2,1)} %convolution_convert_fusion.2), kind=kLoop, calls=%fused_computation.1 | loop fusion | flops 16777216 | bytes 16777216 | tf_op jit(solution)/shard_map/concatenate | solution.py:270
  228.6 12.3 %copy.93 = bf16[2048,2048]{1,0:T(8,128)(2,1)} copy(bf16[2048,2048]{0,1:T(8,128)(2,1)} %pad_maximum_fusion.1) | data formatting | bytes 16777216
  254.2 10.4 %collective-permute-start.11 = (bf16[64,2048]{1,0:T(8,128)(2,1)S(1)}, bf16[64,2048]{1,0:T(8,128)(2,1)S(1)}, u32[]{:S(2)}, u32[]{:S(2)}) collective-permute-start(bf16[64,2048]{1,0:T(8,128)(2,1)S(1)} %get-tuple-element.108), channel_id=1, source_target_pairs={{0,64},{4,68},{64,4},{68,0},{1,65},{5,69},{65,5},{69,1},{2,66},{6,... | collective-permute-start | bytes 786440 | tf_op jit(solution)/shard_map/ppermute | solution.py:44
  290.1 9.7 %all-to-all-start.3 = ((bf16[32,16,512]{2,1,0:T(8,128)(2,1)}), bf16[32,16,512]{2,1,0:T(8,128)(2,1)}, u32[]{:S(2)}, u32[]{:S(2)}) async-start(bf16[32,16,512]{2,1,0:T(8,128)(2,1)} %bitcast.100), calls=%async_computation.3 | async-start | bytes 1048576 | tf_op jit(solution)/shard_map/all_to_all | solution.py:119
  316.0 8.5 %pad_maximum_fusion = bf16[2048,2048]{0,1:T(8,128)(2,1)} fusion(bf16[2048,1024]{0,1:T(8,128)(2,1)} %convolution_convert_fusion.3, bf16[2048,1024]{0,1:T(8,128)(2,1)} %convolution_convert_fusion.4), kind=kLoop, calls=%fused_computation | loop fusion | flops 16777216 | bytes 16777216 | tf_op jit(solution)/shard_map/concatenate | solution.py:282
  327.4 7.4 %all-to-all-start.4 = ((bf16[32,16,512]{2,1,0:T(8,128)(2,1)}), bf16[32,16,512]{2,1,0:T(8,128)(2,1)S(1)}, u32[]{:S(2)}, u32[]{:S(2)}) async-start(bf16[32,16,512]{2,1,0:T(8,128)(2,1)} %copy.72), calls=%async_computation.4 | async-start | bytes 1048576 | tf_op jit(solution)/shard_map/all_to_all | solution.py:131
  336.3 12.3 %copy.91 = bf16[2048,2048]{1,0:T(8,128)(2,1)} copy(bf16[2048,2048]{0,1:T(8,128)(2,1)} %pad_maximum_fusion) | data formatting | bytes 16777216
  403.0 6.0 %collective-permute-done.26 = bf16[64,2048]{1,0:T(8,128)(2,1)S(1)} collective-permute-done((bf16[64,2048]{1,0:T(8,128)(2,1)S(1)}, bf16[64,2048]{1,0:T(8,128)(2,1)S(1)}, u32[]{:S(2)}, u32[]{:S(2)}) %collective-permute-start.26) | collective-permute-done | bytes 262176 | tf_op jit(solution)/shard_map/ppermute | solution.py:44
  410.6 9.7 %all-to-all-start.5 = ((f32[128,1,256]{2,1,0:T(1,128)}), f32[128,1,256]{2,1,0:T(1,128)S(1)}, u32[]{:S(2)}, u32[]{:S(2)}) async-start(f32[128,1,256]{2,1,0:T(1,128)} %all_to_all.29), calls=%async_computation.5 | async-start | bytes 262144 | tf_op jit(solution)/shard_map/all_to_all | solution.py:313
  420.8 7.8 %fusion = bf16[4,256,2048]{2,1,0:T(8,128)(2,1)} fusion(bf16[4,256,2048]{2,1,0:T(8,128)(2,1)} %collective-permute-done.32, bf16[4,2,256,2048]{3,2,1,0:T(8,128)(2,1)} %bitcast.83, s32[]{:T(128)S(6)} %select_n.107), kind=kLoop, calls=%fused_computation.3 | loop fusion | flops 8388608 | bytes 12582916 | tf_op jit(solution)/shard_map/convert_element_type | solution.py:139
  428.6 6.8 %all-to-all-start.6 = ((bf16[16,64,2048]{2,1,0:T(8,128)(2,1)}), bf16[16,64,2048]{2,1,0:T(8,128)(2,1)}, u32[]{:S(2)}, u32[]{:S(2)}) async-start(bf16[16,64,2048]{2,1,0:T(8,128)(2,1)} %bitcast.84), calls=%async_computation.6 | async-start | bytes 8388608 | tf_op jit(solution)/shard_map/all_to_all | solution.py:140
  437.7 5.8 %collective-permute-start.29 = (bf16[64,2048]{1,0:T(8,128)(2,1)S(1)}, bf16[64,2048]{1,0:T(8,128)(2,1)S(1)}, u32[]{:S(2)}, u32[]{:S(2)}) collective-permute-start(bf16[64,2048]{1,0:T(8,128)(2,1)S(1)} %get-tuple-element.85), channel_id=1, source_target_pairs={{4,0},{32,36},{68,64},{96,100},{5,1},{33,37},{69,65},{97,101},{6,2... | collective-permute-start | bytes 786440 | tf_op jit(solution)/shard_map/ppermute | solution.py:54
  460.5 41.5 %all-to-all-done.6 = bf16[16,64,2048]{2,1,0:T(8,128)(2,1)} async-done(((bf16[16,64,2048]{2,1,0:T(8,128)(2,1)}), bf16[16,64,2048]{2,1,0:T(8,128)(2,1)}, u32[]{:S(2)}, u32[]{:S(2)}) %all-to-all-start.6) | async-done | bytes 4194336 | tf_op jit(solution)/shard_map/all_to_all | solution.py:140
  505.0 10.4 %collective-permute-start.33 = (bf16[64,2048]{1,0:T(8,128)(2,1)S(1)}, bf16[64,2048]{1,0:T(8,128)(2,1)S(1)}, u32[]{:S(2)}, u32[]{:S(2)}) collective-permute-start(bf16[64,2048]{1,0:T(8,128)(2,1)S(1)} %reduce_sum.222), channel_id=1, source_target_pairs={{0,0},{4,32},{32,4},{36,36},{1,1},{5,33},{33,5},{37,37},{2,2},{6,3... | collective-permute-start | bytes 786440 | tf_op jit(solution)/shard_map/ppermute | solution.py:34
  (449 shorter events, 257.0 us)
Async XLA Ops:
  7.2 113.5 %all-gather.2.cloned.1.call-start = ((), (), s32[]{:S(2)}) async-start(), calls=%async_computation.9 | async-start | bytes 19464192 | tf_op jit(solution)/shard_map/all_gather | solution.py:186
  72.9 23.6 %collective-permute-start.2 = (bf16[16,64,1664]{2,1,0:T(8,128)(2,1)}, bf16[16,64,1664]{2,1,0:T(8,128)(2,1)}, u32[]{:S(2)}, u32[]{:S(2)}) collective-permute-start(bf16[16,64,1664]{2,1,0:T(8,128)(2,1)} %all_to_all.39), channel_id=1, source_target_pairs={{0,32},{32,0},{1,33},{33,1},{2,34},{34,2},{3,35},{35,3},{4,36},{36... | collective-permute-start | bytes 10223624 | tf_op jit(solution)/shard_map/ppermute | solution.py:67
  72.9 20.7 %collective-permute-start = (bf16[256,2048]{1,0:T(8,128)(2,1)S(1)}, bf16[256,2048]{1,0:T(8,128)(2,1)S(1)}, u32[]{:S(2)}, u32[]{:S(2)}) collective-permute-start(bf16[256,2048]{1,0:T(8,128)(2,1)S(1)} %copy-done.88), channel_id=1, source_target_pairs={{0,0},{4,32},{32,4},{36,36},{1,1},{5,33},{33,5},{37,37},{2,2},{6,3... | collective-permute-start | bytes 3145736 | tf_op jit(solution)/shard_map/ppermute | solution.py:34
  142.1 16.6 %all-to-all-start.2 = ((bf16[32,16,512]{2,1,0:T(8,128)(2,1)}), bf16[32,16,512]{2,1,0:T(8,128)(2,1)}, u32[]{:S(2)}, u32[]{:S(2)}) async-start(bf16[32,16,512]{2,1,0:T(8,128)(2,1)} %copy.66), calls=%async_computation.2 | async-start | bytes 1048576 | tf_op jit(solution)/shard_map/all_to_all | solution.py:131
  151.3 364.0 %reduce-scatter.9.cloned.1.call-start = ((), (), s32[]{:S(2)}) async-start(), calls=%async_computation.11 | async-start | bytes 8650752
  175.3 26.3 %collective-permute-start.18 = (bf16[256,2048]{1,0:T(8,128)(2,1)S(1)}, bf16[256,2048]{1,0:T(8,128)(2,1)S(1)}, u32[]{:S(2)}, u32[]{:S(2)}) collective-permute-start(bf16[256,2048]{1,0:T(8,128)(2,1)S(1)} %copy-done.89), channel_id=1, source_target_pairs={{0,0},{4,32},{32,4},{36,36},{1,1},{5,33},{33,5},{37,37},{2,2},{6,3... | collective-permute-start | bytes 3145736 | tf_op jit(solution)/shard_map/ppermute | solution.py:34
  189.0 18.2 %collective-permute-start.10 = (bf16[64,2048]{1,0:T(8,128)(2,1)S(1)}, bf16[64,2048]{1,0:T(8,128)(2,1)S(1)}, u32[]{:S(2)}, u32[]{:S(2)}) collective-permute-start(bf16[64,2048]{1,0:T(8,128)(2,1)S(1)} %add_convert_fusion.2), channel_id=1, source_target_pairs={{0,64},{4,68},{64,4},{68,0},{1,65},{5,69},{65,5},{69,1},{2,66},{6,... | collective-permute-start | bytes 786440 | tf_op jit(solution)/shard_map/ppermute | solution.py:44
  191.0 16.1 %collective-permute-start.9 = (bf16[64,2048]{1,0:T(8,128)(2,1)S(1)}, bf16[64,2048]{1,0:T(8,128)(2,1)S(1)}, u32[]{:S(2)}, u32[]{:S(2)}) collective-permute-start(bf16[64,2048]{1,0:T(8,128)(2,1)S(1)} %add_convert_fusion.2), channel_id=1, source_target_pairs={{0,4},{4,0},{64,68},{68,64},{1,5},{5,1},{65,69},{69,65},{2,6},{6,2... | collective-permute-start | bytes 786440 | tf_op jit(solution)/shard_map/ppermute | solution.py:44
  191.8 17.9 %collective-permute-start.8 = (bf16[64,2048]{1,0:T(8,128)(2,1)S(1)}, bf16[64,2048]{1,0:T(8,128)(2,1)S(1)}, u32[]{:S(2)}, u32[]{:S(2)}) collective-permute-start(bf16[64,2048]{1,0:T(8,128)(2,1)S(1)} %add_convert_fusion.2), channel_id=1, source_target_pairs={{0,68},{4,64},{64,0},{68,4},{1,69},{5,65},{65,1},{69,5},{2,70},{6,... | collective-permute-start | bytes 786440 | tf_op jit(solution)/shard_map/ppermute | solution.py:44
  246.8 17.9 %collective-permute-start.20 = (bf16[64,2048]{1,0:T(8,128)(2,1)S(1)}, bf16[64,2048]{1,0:T(8,128)(2,1)S(1)}, u32[]{:S(2)}, u32[]{:S(2)}) collective-permute-start(bf16[64,2048]{1,0:T(8,128)(2,1)S(1)} %get-tuple-element.107), channel_id=1, source_target_pairs={{0,68},{4,64},{64,0},{68,4},{1,69},{5,65},{65,1},{69,5},{2,70},{6,... | collective-permute-start | bytes 786440 | tf_op jit(solution)/shard_map/ppermute | solution.py:44
  247.7 16.9 %collective-permute-start.19 = (bf16[64,2048]{1,0:T(8,128)(2,1)S(1)}, bf16[64,2048]{1,0:T(8,128)(2,1)S(1)}, u32[]{:S(2)}, u32[]{:S(2)}) collective-permute-start(bf16[64,2048]{1,0:T(8,128)(2,1)S(1)} %get-tuple-element.105), channel_id=1, source_target_pairs={{0,64},{4,68},{64,4},{68,0},{1,65},{5,69},{65,5},{69,1},{2,66},{6,... | collective-permute-start | bytes 786440 | tf_op jit(solution)/shard_map/ppermute | solution.py:44
  251.9 17.9 %collective-permute-start.13 = (bf16[64,2048]{1,0:T(8,128)(2,1)S(1)}, bf16[64,2048]{1,0:T(8,128)(2,1)S(1)}, u32[]{:S(2)}, u32[]{:S(2)}) collective-permute-start(bf16[64,2048]{1,0:T(8,128)(2,1)S(1)} %get-tuple-element.109), channel_id=1, source_target_pairs={{0,4},{4,0},{64,68},{68,64},{1,5},{5,1},{65,69},{69,65},{2,6},{6,2... | collective-permute-start | bytes 786440 | tf_op jit(solution)/shard_map/ppermute | solution.py:44
  254.2 17.6 %collective-permute-start.12 = (bf16[64,2048]{1,0:T(8,128)(2,1)S(1)}, bf16[64,2048]{1,0:T(8,128)(2,1)S(1)}, u32[]{:S(2)}, u32[]{:S(2)}) collective-permute-start(bf16[64,2048]{1,0:T(8,128)(2,1)S(1)} %get-tuple-element.110), channel_id=1, source_target_pairs={{0,68},{4,64},{64,0},{68,4},{1,69},{5,65},{65,1},{69,5},{2,70},{6,... | collective-permute-start | bytes 786440 | tf_op jit(solution)/shard_map/ppermute | solution.py:44
  254.2 17.6 %collective-permute-start.11 = (bf16[64,2048]{1,0:T(8,128)(2,1)S(1)}, bf16[64,2048]{1,0:T(8,128)(2,1)S(1)}, u32[]{:S(2)}, u32[]{:S(2)}) collective-permute-start(bf16[64,2048]{1,0:T(8,128)(2,1)S(1)} %get-tuple-element.108), channel_id=1, source_target_pairs={{0,64},{4,68},{64,4},{68,0},{1,65},{5,69},{65,5},{69,1},{2,66},{6,... | collective-permute-start | bytes 786440 | tf_op jit(solution)/shard_map/ppermute | solution.py:44
  272.8 101.6 %collective-permute-start.14 = (bf16[64,2048]{1,0:T(8,128)(2,1)}, bf16[64,2048]{1,0:T(8,128)(2,1)}, u32[]{:S(2)}, u32[]{:S(2)}) collective-permute-start(bf16[64,2048]{1,0:T(8,128)(2,1)} %get-tuple-element.91), channel_id=1, source_target_pairs={{4,64},{32,100},{64,0},{100,36},{5,65},{33,101},{65,1},{101,37},{6... | collective-permute-start | bytes 786440 | tf_op jit(solution)/shard_map/ppermute | solution.py:54
  274.1 101.9 %collective-permute-start.15 = (bf16[64,2048]{1,0:T(8,128)(2,1)}, bf16[64,2048]{1,0:T(8,128)(2,1)}, u32[]{:S(2)}, u32[]{:S(2)}) collective-permute-start(bf16[64,2048]{1,0:T(8,128)(2,1)} %get-tuple-element.91), channel_id=1, source_target_pairs={{4,0},{32,36},{68,64},{96,100},{5,1},{33,37},{69,65},{97,101},{6,2... | collective-permute-start | bytes 786440 | tf_op jit(solution)/shard_map/ppermute | solution.py:54
  290.1 34.3 %all-to-all-start.3 = ((bf16[32,16,512]{2,1,0:T(8,128)(2,1)}), bf16[32,16,512]{2,1,0:T(8,128)(2,1)}, u32[]{:S(2)}, u32[]{:S(2)}) async-start(bf16[32,16,512]{2,1,0:T(8,128)(2,1)} %bitcast.100), calls=%async_computation.3 | async-start | bytes 1048576 | tf_op jit(solution)/shard_map/all_to_all | solution.py:119
  327.4 23.6 %all-to-all-start.4 = ((bf16[32,16,512]{2,1,0:T(8,128)(2,1)}), bf16[32,16,512]{2,1,0:T(8,128)(2,1)S(1)}, u32[]{:S(2)}, u32[]{:S(2)}) async-start(bf16[32,16,512]{2,1,0:T(8,128)(2,1)} %copy.72), calls=%async_computation.4 | async-start | bytes 1048576 | tf_op jit(solution)/shard_map/all_to_all | solution.py:131
  334.8 187.4 %reduce-scatter.7.cloned.1.call-start = ((), (), s32[]{:S(2)}) async-start(), calls=%async_computation.10 | async-start | bytes 8650752
  368.2 52.6 %collective-permute-start.32 = (bf16[4,256,2048]{2,1,0:T(8,128)(2,1)}, bf16[4,256,2048]{2,1,0:T(8,128)(2,1)}, u32[]{:S(2)}, u32[]{:S(2)}) collective-permute-start(bf16[4,256,2048]{2,1,0:T(8,128)(2,1)} %dynamic-slice_bitcast_fusion), channel_id=1, source_target_pairs={{0,32},{32,0},{1,33},{33,1},{2,34},{34,2},{3,35},{35,3},{4,36},{36... | collective-permute-start | bytes 12582920 | tf_op jit(solution)/shard_map/ppermute | solution.py:67
  410.6 18.0 %all-to-all-start.5 = ((f32[128,1,256]{2,1,0:T(1,128)}), f32[128,1,256]{2,1,0:T(1,128)S(1)}, u32[]{:S(2)}, u32[]{:S(2)}) async-start(f32[128,1,256]{2,1,0:T(1,128)} %all_to_all.29), calls=%async_computation.5 | async-start | bytes 262144 | tf_op jit(solution)/shard_map/all_to_all | solution.py:313
  428.6 73.4 %all-to-all-start.6 = ((bf16[16,64,2048]{2,1,0:T(8,128)(2,1)}), bf16[16,64,2048]{2,1,0:T(8,128)(2,1)}, u32[]{:S(2)}, u32[]{:S(2)}) async-start(bf16[16,64,2048]{2,1,0:T(8,128)(2,1)} %bitcast.84), calls=%async_computation.6 | async-start | bytes 8388608 | tf_op jit(solution)/shard_map/all_to_all | solution.py:140
  455.8 63.5 %collective-permute-start.31 = (bf16[256,2048]{1,0:T(8,128)(2,1)}, bf16[256,2048]{1,0:T(8,128)(2,1)}, u32[]{:S(2)}, u32[]{:S(2)}) collective-permute-start(bf16[256,2048]{1,0:T(8,128)(2,1)} %constant_dynamic-slice_fusion), channel_id=1, source_target_pairs={{0,32},{36,4},{1,33},{37,5},{2,34},{38,6},{3,35},{39,7},{8,40},{44... | collective-permute-start | bytes 3145736 | tf_op jit(solution)/shard_map/ppermute | solution.py:63
  505.0 23.6 %collective-permute-start.33 = (bf16[64,2048]{1,0:T(8,128)(2,1)S(1)}, bf16[64,2048]{1,0:T(8,128)(2,1)S(1)}, u32[]{:S(2)}, u32[]{:S(2)}) collective-permute-start(bf16[64,2048]{1,0:T(8,128)(2,1)S(1)} %reduce_sum.222), channel_id=1, source_target_pairs={{0,0},{4,32},{32,4},{36,36},{1,1},{5,33},{33,5},{37,37},{2,2},{6,3... | collective-permute-start | bytes 786440 | tf_op jit(solution)/shard_map/ppermute | solution.py:34
  (126 other events, 1354.7 us)
Sparse Core Ops, SparseCore 0:
  25.4 95.2 all-gather.1
  241.0 95.7 reduce-scatter.8
  348.8 135.5 reduce-scatter.6

commit v2 on v1

v2 whole, which is shorter than its diff:
```python
import functools
import itertools

import jax
import jax.numpy as jnp
from jax import lax
from jax.experimental import pallas as pl
from jax.experimental.pallas import tpu as pltpu
from jax.sharding import Mesh, PartitionSpec as P

DK = 256
DV = 512
AXES = ("zl", "c", "x", "zh", "y")
SIZES = {"zl": 2, "c": 2, "x": 4, "zh": 2, "y": 4}
SPANS = ("x", "c", "y")
BF = jnp.bfloat16
F32 = jnp.float32


def pairs(axes, move):
    def flat(place):
        at = 0
        for axis in axes:
            at = at * SIZES[axis] + place[axis]
        return at

    found = []
    for values in itertools.product(*[range(SIZES[axis]) for axis in axes]):
        place = dict(zip(axes, values))
        target = move(dict(place))
        if target is not None:
            found.append((flat(place), flat(target)))
    return found


def swap_roles(values):
    return lax.ppermute(
        values, ("c", "zh"), pairs(("c", "zh"), lambda p: {"c": p["zh"], "zh": p["c"]})
    )


def z_shift(values, shift):
    def move(place):
        z = (place["zh"] * 2 + place["zl"] + shift) % 4
        return {"zl": z % 2, "zh": z // 2}

    return lax.ppermute(values, ("zl", "zh"), pairs(("zl", "zh"), move))


def z_shift_home(values, shift):
    def move(place):
        z = (place["zh"] * 2 + place["zl"] + shift) % 4
        if z // 2 != place["c"]:
            return None
        return {"zl": z % 2, "zh": z // 2, "c": place["c"]}

    return lax.ppermute(values, ("zl", "c", "zh"), pairs(("zl", "c", "zh"), move))


def core_from_home(values):
    def move(place):
        if place["zh"] != place["c"]:
            return None
        return {"c": 1 - place["c"], "zh": place["zh"]}

    return lax.ppermute(values, ("c", "zh"), pairs(("c", "zh"), move))


def core_swap(values):
    return lax.ppermute(values, "c", [(0, 1), (1, 0)])


def z_reduce(part, mine):
    rows = part.shape[0] // 4
    total = mine
    for shift in (1, 3, 2):
        total = total + z_shift(part[shift * rows : (shift + 1) * rows], shift).astype(F32)
    return total


def z_gather(values):
    near, far, across = z_shift(values, 3), z_shift(values, 1), z_shift(values, 2)
    return jnp.concatenate([values, near, across, far], axis=0)


def z_gather_home(values, place, home, dtype):
    near, far, across = z_shift_home(values, 3), z_shift_home(values, 1), z_shift_home(values, 2)
    full = in_place(place, values, near, across, far)
    return chosen(home, full, core_from_home(full), dtype)


def nn(left, right):
    return jnp.dot(left, right, preferred_element_type=F32)


def nt(left, right):
    return lax.dot_general(left, right, (((1,), (1,)), ((), ())), preferred_element_type=F32)


def tn(left, right):
    return lax.dot_general(left, right, (((0,), (0,)), ((), ())), preferred_element_type=F32)


def norm_parts(values):
    center = values - jnp.mean(values, axis=-1, keepdims=True)
    spread = jnp.mean(center * center, axis=-1, keepdims=True)
    scale = lax.rsqrt(spread + 1e-05)
    return center * scale, scale


def norm_back(grad, hat, scale):
    mean_grad = jnp.mean(grad, axis=-1, keepdims=True)
    mean_both = jnp.mean(grad * hat, axis=-1, keepdims=True)
    return (grad - mean_grad - hat * mean_both) * scale


def scan_parts(fresh):
    return lax.all_to_all(fresh.reshape(32, 16, DV), SPANS, 0, 0, tiled=True)


def scan_back(carried):
    return lax.all_to_all(carried, SPANS, 0, 0, tiled=True).reshape(2 * DK, DV)


def halves_sum(own, other):
    total = (own.astype(F32) + core_swap(other).astype(F32)).astype(BF)
    return total.reshape(16, 64, own.shape[1])


def scatter_sum(total):
    total = lax.all_to_all(total, ("x", "y"), 0, 0, tiled=True)
    return jnp.sum(total.astype(F32), axis=0).astype(BF)


def run(kernel, grid, ins, outs, operands, flops, scratch=()):
    moved = sum(a.size * a.dtype.itemsize for a in operands)
    moved += sum(o[0].size * o[0].dtype.itemsize for o in outs)
    return pl.pallas_call(
        kernel,
        grid=grid,
        in_specs=ins,
        out_specs=[o[1] for o in outs],
        out_shape=[o[0] for o in outs],
        scratch_shapes=list(scratch),
        compiler_params=pltpu.CompilerParams(vmem_limit_bytes=48 * 1024 * 1024),
        cost_estimate=pl.CostEstimate(flops=int(flops), bytes_accessed=int(moved), transcendentals=0),
    )(*operands)


def shape(dims, dtype):
    return jax.ShapeDtypeStruct(dims, dtype)


def columns(rows, cols, first=0):
    return pl.BlockSpec((rows, cols), lambda h: (0, first + h))


def whole(dims):
    return pl.BlockSpec(dims, lambda h: (0,) * len(dims))


SCALARS = pl.BlockSpec(memory_space=pltpu.SMEM)


def places(dims, axis, z):
    at = lax.broadcasted_iota(jnp.int32, dims, axis) + z * 64
    return jnp.where(at >= 256, at - 256, at).astype(F32)


def decays(rate, z):
    at = places((256, 1), 0, z)
    return jnp.exp(-rate * (at + 1.0)), jnp.exp(-rate * (255.0 - at))


def span_mask(rate, z):
    offset = places((256, 256), 0, z) - places((256, 256), 1, z)
    return jnp.where(offset >= 0.0, jnp.exp(-rate * jnp.maximum(offset, 0.0)), 0.0)


def turn_into(ref, values, cosine, sine, start=0):
    half = DK // 2
    a, b = values[:, :half], values[:, half:]
    ref[:, start : start + half] = (a * cosine - b * sine).astype(ref.dtype)
    ref[:, start + half : start + DK] = (b * cosine + a * sine).astype(ref.dtype)


def in_place_kernel(place, *refs):
    out = refs[-1]
    for k in range(4):
        at = place[0] + k
        at = pl.multiple_of(jnp.where(at >= 4, at - 4, at) * 64, 64)
        out[pl.ds(at, 64), :] = refs[k][...]


def in_place(place, *pieces):
    return run(
        in_place_kernel,
        (1,),
        [SCALARS] + [whole((64, 2048))] * 4,
        [(shape((256, 2048), BF), whole((256, 2048)))],
        [place, *pieces],
        1,
    )[0]


def chosen_kernel(home, mine, other, out):
    @pl.when(home[0] == 1)
    def here():
        out[...] = mine[...].astype(out.dtype)

    @pl.when(home[0] == 0)
    def there():
        out[...] = other[...].astype(out.dtype)


def chosen(home, mine, other, dtype):
    block = pl.BlockSpec((128, 2048), lambda i: (i, 0))
    return run(
        chosen_kernel,
        (2,),
        [SCALARS, block, block],
        [(shape((256, 2048), dtype), block)],
        [home, mine, other],
        1,
    )[0]


def scan_kernel(reverse, rate, parts, out):
    decay = jnp.exp(jnp.full((16, DV), -256.0 * rate[0], F32))
    state = jnp.zeros((16, DV), F32)
    for k in range(31, -1, -1) if reverse else range(32):
        out[k] = state.astype(BF)
        state = decay * state + parts[k].astype(F32)


def scan_spans(rate, parts, reverse):
    dims = (32, 16, DV)
    return run(
        functools.partial(scan_kernel, reverse),
        (1,),
        [SCALARS, whole(dims)],
        [(shape(dims, BF), whole(dims))],
        [rate, parts],
        2 * 32 * 16 * DV,
    )[0]


def pack_kernel(*refs):
    out, start = refs[-1], 0
    for ref in refs[:-1]:
        out[:, start : start + ref.shape[1]] = ref[...]
        start += ref.shape[1]


def pack(*parts):
    cols = sum(p.shape[1] for p in parts)
    return run(
        pack_kernel,
        (1,),
        [whole(p.shape) for p in parts],
        [(shape((64, cols), BF), whole((64, cols)))],
        list(parts),
        1,
    )[0]


def pack_first_kernel(w_key, w_value, gains, out):
    out[:, :512] = w_key[...]
    out[:, 512:1536] = w_value[...]
    wide = gains[...].astype(F32)
    same = lax.broadcasted_iota(jnp.int32, (64, 64), 0) == lax.broadcasted_iota(
        jnp.int32, (64, 64), 1
    )
    lane = lax.broadcasted_iota(jnp.int32, (64, 128), 1)
    total = jnp.zeros((64, 128), F32)
    for k in range(4):
        column = jnp.sum(jnp.where(same, wide[k : k + 1, :], 0.0), axis=1, keepdims=True)
        total = jnp.where(lane == k, column, total)
    out[:, 1536:] = total.astype(BF)


def pack_first(w_key, w_value, gains):
    return run(
        pack_first_kernel,
        (1,),
        [whole((64, 512)), whole((64, 1024)), whole((4, 64))],
        [(shape((64, 1664), BF), whole((64, 1664)))],
        [w_key, w_value, gains],
        1,
    )[0]


def norm_kernel(place, tokens, gains_own, gains_other, normed, own, other, hat, scale, gains):
    values = tokens[...].astype(F32)
    made, spread = norm_parts(values)
    scale[...] = spread
    hat[...] = made
    mine = gains_own[...].astype(F32).T
    yours = gains_other[...].astype(F32).T
    for i in range(4):
        for ref, rows, side in ((own, mine, place[1]), (other, yours, 1 - place[1])):
            at = pl.multiple_of((2 * i + side) * 256, 256)
            rows = rows[:8, i * 256 : i * 256 + 256]
            gains[:, pl.ds(at, 256)] = rows
            out = (hat[:, pl.ds(at, 256)] * rows[0:1] + rows[1:2]).astype(BF)
            normed[:, pl.ds(at, 256)] = out
            ref[:, i * 256 : i * 256 + 256] = out


def norm_first(place, tokens, early, early_other):
    gains = pl.BlockSpec((1024, 128), lambda h: (0, 12))
    return run(
        norm_kernel,
        (1,),
        [SCALARS, whole((256, 2048)), gains, gains],
        [
            (shape((256, 2048), BF), whole((256, 2048))),
            (shape((256, 1024), BF), whole((256, 1024))),
            (shape((256, 1024), BF), whole((256, 1024))),
            (shape((256, 2048), F32), whole((256, 2048))),
            (shape((256, 1), F32), whole((256, 1))),
            (shape((8, 2048), F32), whole((8, 2048))),
        ],
        [place, tokens, early, early_other],
        10 * 256 * 2048,
    )


def kv_kernel(
    rate, place, own, other, key_own, key_other, value_own, value_other, cosine, sine, key, value, fresh
):
    qdec, kdec = decays(rate[pl.program_id(0)], place[0])
    raw = nn(own[...], key_own[...]) + nn(other[...], key_other[...])
    turn_into(key, raw, cosine[...], sine[...])
    made = (nn(own[...], value_own[...]) + nn(other[...], value_other[...])).astype(BF)
    value[...] = made
    fresh[...] = tn((kdec * key[...].astype(F32)).astype(BF), made).astype(BF)


def key_value(rate, place, own, other, early, early_other, cosine, sine):
    return run(
        kv_kernel,
        (2,),
        [
            SCALARS,
            SCALARS,
            whole((256, 1024)),
            whole((256, 1024)),
            columns(1024, 256),
            columns(1024, 256),
            columns(1024, 512, 1),
            columns(1024, 512, 1),
            whole((256, 128)),
            whole((256, 128)),
        ],
        [
            (shape((256, 512), BF), columns(256, 256)),
            (shape((256, 1024), BF), columns(256, 512)),
            (shape((512, 512), BF), pl.BlockSpec((256, 512), lambda h: (h, 0))),
        ],
        [rate, place, own, other, early, early_other, early, early_other, cosine, sine],
        2 * 256 * 2048 * 1536,
    )


def query_kernel(
    rate, place, normed, w_query, w_gate, key, value, cosine, sine, query, gate, probs, inner
):
    raw = nn(normed[...], w_query[...])
    turn_into(query, raw, cosine[...], sine[...])
    gate[...] = nn(normed[...], w_gate[...])
    mask = span_mask(rate[pl.program_id(0)], place[0])
    made = (nt(query[...], key[...]) * mask).astype(BF)
    probs[0] = made
    inner[...] = nn(made, value[...])


def query_gate(rate, place, normed1, late, key, value, cosine, sine):
    return run(
        query_kernel,
        (2,),
        [
            SCALARS,
            SCALARS,
            whole((256, 2048)),
            columns(2048, 256, 16),
            columns(2048, 512),
            columns(256, 256),
            columns(256, 512),
            whole((256, 128)),
            whole((256, 128)),
        ],
        [
            (shape((256, 512), BF), columns(256, 256)),
            (shape((256, 1024), F32), columns(256, 512)),
            (shape((2, 256, 256), BF), pl.BlockSpec((1, 256, 256), lambda h: (h, 0, 0))),
            (shape((256, 1024), F32), columns(256, 512)),
        ],
        [rate, place, normed1, late, late, key, value, cosine, sine],
        2 * 256 * 2048 * 1536,
    )


def retain_kernel(
    rate, place, query, state, inner, gate, w_out, hat, scale, mixed, part, own, total
):
    h = pl.program_id(0)
    qdec, kdec = decays(rate[h], place[0])
    retained = inner[...] + qdec * nn(query[...], state[...])
    made, spread = norm_parts(retained)
    hat[...] = made
    scale[0] = spread
    wide = gate[...]
    made = (wide * jax.nn.sigmoid(wide) * made).astype(BF)
    mixed[...] = made
    partial = nt(made, w_out[...])

    @pl.when(h == 0)
    def first():
        total[...] = partial

    @pl.when(h == 1)
    def last():
        full = total[...] + partial
        part[...] = full.astype(BF)
        own[...] = full[:64]


def retain(rate, place, query, state, inner, gate, late):
    return run(
        retain_kernel,
        (2,),
        [
            SCALARS,
            SCALARS,
            columns(256, 256),
            pl.BlockSpec((256, 512), lambda h: (h, 0)),
            columns(256, 512),
            columns(256, 512),
            columns(2048, 512, 2),
        ],
        [
            (shape((256, 1024), F32), columns(256, 512)),
            (shape((2, 256, 1), F32), pl.BlockSpec((1, 256, 1), lambda h: (h, 0, 0))),
            (shape((256, 1024), BF), columns(256, 512)),
            (shape((256, 2048), BF), whole((256, 2048))),
            (shape((64, 2048), F32), whole((64, 2048))),
        ],
        [rate, place, query, state, inner, gate, late],
        2 * 256 * 2048 * 1024,
        [pltpu.VMEM((256, 2048), F32)],
    )


def up_kernel(normed, w_up, d_hidden, hidden, d_up, part, own, total):
    j = pl.program_id(0)
    raw = nn(normed[...], w_up[...])
    root = 0.7978845608028654
    square = raw * raw
    tanh = jnp.tanh(root * raw * (1.0 + 0.044715 * square))
    half = 0.5 * (1.0 + tanh)
    hidden[...] = (raw * half).astype(BF)
    slope = half + 0.5 * raw * (1.0 - tanh * tanh) * root * (1.0 + 0.134145 * square)
    made = (slope * d_hidden[...]).astype(BF)
    d_up[...] = made
    partial = nt(made, w_up[...])

    @pl.when(j == 0)
    def first():
        total[...] = partial

    @pl.when(j == 1)
    def last():
        full = total[...] + partial
        part[...] = full.astype(BF)
        own[...] = full[:64]


def up_back(normed2, late, d_hidden):
    return run(
        up_kernel,
        (2,),
        [whole((256, 2048)), columns(2048, 512, 4), columns(256, 512)],
        [
            (shape((256, 1024), BF), columns(256, 512)),
            (shape((256, 1024), BF), columns(256, 512)),
            (shape((256, 2048), BF), whole((256, 2048))),
            (shape((64, 2048), F32), whole((64, 2048))),
        ],
        [normed2, late, d_hidden],
        4 * 256 * 2048 * 1024,
        [pltpu.VMEM((256, 2048), F32)],
    )


def mixed_kernel(rate, place, d_attn, w_out, gate, hat, scale, query, d_gate, d_ret, outgoing):
    qdec, kdec = decays(rate[pl.program_id(0)], place[0])
    d_mixed = nn(d_attn[...], w_out[...])
    wide, normed = gate[...], hat[...]
    sig = jax.nn.sigmoid(wide)
    d_gate[...] = (d_mixed * normed * sig * (1.0 + wide * (1.0 - sig))).astype(BF)
    made = norm_back(d_mixed * wide * sig, normed, scale[0]).astype(BF)
    d_ret[...] = made
    outgoing[...] = tn((qdec * query[...].astype(F32)).astype(BF), made).astype(BF)


def mixed_back(rate, place, d_attn, late, gate, hat, scale, query):
    return run(
        mixed_kernel,
        (2,),
        [
            SCALARS,
            SCALARS,
            whole((256, 2048)),
            columns(2048, 512, 2),
            columns(256, 512),
            columns(256, 512),
            pl.BlockSpec((1, 256, 1), lambda h: (h, 0, 0)),
            columns(256, 256),
        ],
        [
            (shape((256, 1024), BF), columns(256, 512)),
            (shape((256, 1024), BF), columns(256, 512)),
            (shape((512, 512), BF), pl.BlockSpec((256, 512), lambda h: (h, 0))),
        ],
        [rate, place, d_attn, late, gate, hat, scale, query],
        2 * 256 * 2048 * 1024,
    )


def query_back_kernel(
    rate, place, d_ret, value, key, query, probs, state, cosine, sine, d_query, key_part, value_part
):
    h = pl.program_id(0)
    qdec, kdec = decays(rate[h], place[0])
    mask = span_mask(rate[h], place[0])
    d_scores = (nt(d_ret[...], value[...]) * mask).astype(BF)
    turned = nn(d_scores, key[...]) + qdec * nt(d_ret[...], state[...])
    turn_into(d_query, turned, cosine[...], -sine[...])
    key_part[...] = tn(d_scores, query[...])
    value_part[...] = tn(probs[0], d_ret[...])


def query_back(rate, place, d_ret, value, key, query, probs, state, cosine, sine):
    return run(
        query_back_kernel,
        (2,),
        [
            SCALARS,
            SCALARS,
            columns(256, 512),
            columns(256, 512),
            columns(256, 256),
            columns(256, 256),
            pl.BlockSpec((1, 256, 256), lambda h: (h, 0, 0)),
            pl.BlockSpec((256, 512), lambda h: (h, 0)),
            whole((256, 128)),
            whole((256, 128)),
        ],
        [
            (shape((256, 512), BF), columns(256, 256)),
            (shape((256, 512), F32), columns(256, 256)),
            (shape((256, 1024), F32), columns(256, 512)),
        ],
        [rate, place, d_ret, value, key, query, probs, state, cosine, sine],
        2 * 256 * 256 * 2 * 2000,
    )


def key_value_back_kernel(
    rate, place, key_part, value_part, key, value, later, cosine, sine, d_both
):
    for h in range(2):
        qdec, kdec = decays(rate[h], place[0])
        keys, values = slice(h * DK, h * DK + DK), slice(h * DV, h * DV + DV)
        carried = later[keys, :]
        d_key = key_part[:, keys] + kdec * nt(value[:, values], carried)
        turn_into(d_both, d_key, cosine[...], -sine[...], h * DK)
        d_value = value_part[:, values] + kdec * nn(key[:, keys], carried)
        d_both[:, 512 + h * DV : 512 + h * DV + DV] = d_value.astype(BF)


def key_value_back(rate, place, key_part, value_part, key, value, later, cosine, sine):
    return run(
        key_value_back_kernel,
        (1,),
        [
            SCALARS,
            SCALARS,
            whole((256, 512)),
            whole((256, 1024)),
            whole((256, 512)),
            whole((256, 1024)),
            whole((512, 512)),
            whole((256, 128)),
            whole((256, 128)),
        ],
        [(shape((256, 1536), BF), whole((256, 1536)))],
        [rate, place, key_part, value_part, key, value, later, cosine, sine],
        2 * 256 * 256 * 512 * 4,
    )[0]


def normed_first_kernel(d_query, d_gate, w_query, w_gate, part):
    part[...] = nt(d_query[...], w_query[...]) + nt(d_gate[...], w_gate[...])


def normed_back_first(d_query, d_gate, late):
    return run(
        normed_first_kernel,
        (4,),
        [
            whole((256, 512)),
            whole((256, 1024)),
            pl.BlockSpec((512, 512), lambda i: (i, 8)),
            pl.BlockSpec((512, 1024), lambda i: (i, 0)),
        ],
        [(shape((256, 2048), F32), columns(256, 512))],
        [d_query, d_gate, late, late],
        2 * 256 * 2048 * 1536,
    )[0]


def normed_back_kernel(place, first, d_both, w_own, w_other, hat, part, own, vectors):
    left = nt(d_both[...], w_own[:, :1536])
    right = nt(d_both[...], w_other[:, :1536])
    low = place[1] == 0
    total = first[...] + jnp.concatenate(
        [jnp.where(low, left, right), jnp.where(low, right, left)], axis=1
    )
    part[...] = total.astype(BF)
    own[...] = total[:64]
    vectors[0:1] = jnp.sum(total * hat[...], axis=0, keepdims=True)
    vectors[1:2] = jnp.sum(total, axis=0, keepdims=True)


def normed_back(place, first, d_both, early, early_other, hat):
    weights = pl.BlockSpec((256, 1664), lambda i: (i, 0))
    return run(
        normed_back_kernel,
        (4,),
        [
            SCALARS,
            columns(256, 512),
            whole((256, 1536)),
            weights,
            weights,
            columns(256, 512),
        ],
        [
            (shape((256, 2048), BF), columns(256, 512)),
            (shape((64, 2048), F32), columns(64, 512)),
            (shape((2, 2048), F32), columns(2, 512)),
        ],
        [place, first, d_both, early, early_other, hat],
        2 * 256 * 2048 * 1536,
    )


def triple_kernel(*refs):
    w, out = pl.program_id(0), refs[-1]
    for k in range(3):

        @pl.when(w == k)
        def one(k=k):
            out[...] = tn(refs[2 * k][...], refs[2 * k + 1][...]).astype(BF)


def grad_triple(*operands):
    def left(w):
        return pl.BlockSpec(
            (256, 512), lambda v, i: (0, jnp.where(v == w, i, jnp.where(v > w, 3, 0)))
        )

    right = pl.BlockSpec((256, 1024), lambda v, i: (0, 0))
    return run(
        triple_kernel,
        (3, 4),
        [left(0), right, left(1), right, left(2), right],
        [(shape((2048, 3072), BF), pl.BlockSpec((512, 1024), lambda v, i: (i, v)))],
        list(operands),
        2 * 256 * 2048 * 3072,
    )[0]


def split_kernel(place, left, *refs):
    rights, own, other = refs[:-2], refs[-2], refs[-1]
    for ref, side in ((own, place[1]), (other, 1 - place[1])):
        at = pl.multiple_of(side * 256, 256)
        rows = left[:, pl.ds(at, 256)]
        start = 0
        for right in rights:
            ref[:, start : start + right.shape[1]] = tn(rows, right[...]).astype(BF)
            start += right.shape[1]


def grad_split(place, left, rights):
    cols = sum(r.shape[1] for r in rights)
    half = (shape((1024, cols), BF), pl.BlockSpec((256, cols), lambda i: (i, 0)))
    return run(
        split_kernel,
        (4,),
        [SCALARS, columns(256, 512)] + [whole(r.shape) for r in rights],
        [half, half],
        [place, left, *rights],
        2 * 256 * 2048 * cols,
    )


def widen_kernel(values, *outs):
    start = 0
    for out in outs:
        out[...] = values[:, start : start + out.shape[1]].astype(F32)
        start += out.shape[1]


def widen(values, widths):
    return run(
        widen_kernel,
        (1,),
        [whole(values.shape)],
        [(shape((64, n), F32), whole((64, n))) for n in widths],
        [values],
        1,
    )


def body(
    tokens,
    norm1_gain,
    norm1_bias,
    w_query,
    w_key,
    w_value,
    w_gate,
    w_out,
    norm2_gain,
    norm2_bias,
    w_up,
    w_down,
    decay_rate,
    out_grad,
):
    x, y, c = lax.axis_index("x"), lax.axis_index("y"), lax.axis_index("c")
    zl, zh = lax.axis_index("zl"), lax.axis_index("zh")
    z = zh * 2 + zl
    home = (zh == c).astype(jnp.int32).reshape(1)
    span = x * 8 + c * 4 + y
    place = jnp.stack([z, c]).astype(jnp.int32)

    first = pack_first(
        w_key, w_value, jnp.stack([norm1_gain, norm1_bias, norm2_gain, norm2_bias])
    )
    first, w_gate = lax.optimization_barrier((first, w_gate))
    first = swap_roles(first)
    second = swap_roles(pack(w_gate, w_out.T, w_up, w_down.T, w_query))
    rate = swap_roles(decay_rate)
    tokens = swap_roles(tokens)
    out_grad = swap_roles(out_grad)

    cols = first.shape[1]
    early = lax.all_to_all(
        jnp.broadcast_to(first[None], (16, 64, cols)), ("x", "y"), 0, 0, tiled=True
    ).reshape(1024, cols)
    late = lax.all_gather(second, SPANS, axis=0, tiled=True)

    tokens = lax.dynamic_slice_in_dim(jnp.concatenate([tokens, tokens]), z * 64, 256, 0)
    out_grad = lax.dynamic_slice_in_dim(jnp.concatenate([out_grad, out_grad]), z * 64, 256, 0)
    index = ((jnp.arange(256) + z * 64) % 256).astype(F32)
    half = DK // 2
    position = (span * 256).astype(F32) + index
    freq = 10000.0 ** (-jnp.arange(half).astype(F32) / half)
    angle = position[:, None] * freq[None, :]
    cosine, sine = jnp.cos(angle), jnp.sin(angle)
    early, tokens, out_grad, cosine, sine, rate = lax.optimization_barrier(
        (early, tokens, out_grad, cosine, sine, rate)
    )

    early_other = core_swap(early)
    normed1, own, other, hat1, scale1, gains = norm_first(place, tokens, early, early_other)
    gain1, gain2, bias2 = gains[0], gains[2], gains[3]
    key, value, fresh = key_value(rate, place, own, other, early, early_other, cosine, sine)
    scan_rate = jnp.where(x < 2, rate[0], rate[1]).reshape(1)
    carried = scan_spans(scan_rate, scan_parts(fresh), False)
    late, carried = lax.optimization_barrier((late, carried))
    state = scan_back(carried)
    query, gate, probs, inner = query_gate(
        rate, place, normed1, late, key, value, cosine, sine
    )
    hat, scale, mixed, part, mine = retain(rate, place, query, state, inner, gate, late)

    full_down = late[:, 3072:4096]
    d_hidden = nn(out_grad, full_down)
    resid = tokens[:64].astype(F32) + z_reduce(part, mine)
    hat2, scale2 = norm_parts(resid)
    normed2 = z_gather((hat2 * gain2 + bias2).astype(BF))
    hidden, d_up, part, mine = up_back(normed2, late, d_hidden)
    d_normed2 = z_reduce(part, mine)

    ffn = nt(hidden, full_down)
    ffn = z_reduce(ffn.astype(BF), ffn[:64])
    block_out = z_gather_home((resid + ffn).astype(BF), place, home, BF)

    own_grad = out_grad[:64].astype(F32)
    d_resid = own_grad + norm_back(d_normed2 * gain2, hat2, scale2)
    grad_gain2 = jnp.sum(d_normed2 * hat2, axis=0)
    grad_bias2 = jnp.sum(d_normed2, axis=0)
    d_attn = z_gather(d_resid.astype(BF))

    d_gate, d_ret, outgoing = mixed_back(rate, place, d_attn, late, gate, hat, scale, query)
    carried = scan_spans(scan_rate, scan_parts(outgoing), True)
    grad_wide = swap_roles(
        lax.psum_scatter(
            grad_triple(normed2, d_up, out_grad, hidden, d_attn, mixed),
            SPANS,
            scatter_dimension=0,
            tiled=True,
        )
    )
    later = scan_back(carried)

    d_query, key_part, value_part = query_back(
        rate, place, d_ret, value, key, query, probs, state, cosine, sine
    )
    d_first = normed_back_first(d_query, d_gate, late)
    grad_gate = halves_sum(*grad_split(place, normed1, [d_gate, d_query]))
    grad_gate, later = lax.optimization_barrier((grad_gate, later))
    grad_gate = scatter_sum(grad_gate)
    d_both = key_value_back(
        rate, place, key_part, value_part, key, value, later, cosine, sine
    )
    grad_both = halves_sum(*grad_split(place, normed1, [d_both]))
    grad_both, grad_gate = lax.optimization_barrier((grad_both, grad_gate))
    grad_both = scatter_sum(grad_both)

    part, mine, vectors1 = normed_back(place, d_first, d_both, early, early_other, hat1)
    d_normed1 = z_reduce(part, mine)
    tokens_grad = d_resid + norm_back(d_normed1 * gain1, hat1[:64], scale1[:64])
    tokens_grad = z_gather_home(tokens_grad.astype(BF), place, home, F32)

    vectors = jnp.concatenate([vectors1, jnp.stack([grad_gain2, grad_bias2])])
    vectors = vectors.reshape(4, 32, 64).transpose(1, 0, 2).reshape(1, 32, 256)
    vectors = jnp.broadcast_to(vectors, (4, 32, 256)).reshape(128, 256)
    vectors, grad_both = lax.optimization_barrier((vectors, grad_both))
    vectors = lax.all_to_all(vectors, AXES, 0, 0, tiled=True)
    vectors = jnp.sum(vectors, axis=0)

    grad_key, grad_value = widen(swap_roles(grad_both), [512, 1024])
    grad_gate, grad_query = widen(swap_roles(grad_gate), [1024, 512])
    grad_up, grad_down, grad_out = widen(grad_wide, [1024, 1024, 1024])
    return (
        block_out,
        tokens_grad,
        vectors[:64],
        vectors[64:128],
        grad_query,
        grad_key,
        grad_value,
        grad_gate,
        grad_out.T,
        vectors[128:192],
        vectors[192:],
        grad_up,
        grad_down.T,
    )


def solution(mesh):
    fine = Mesh(mesh.devices.reshape(2, 2, 4, 2, 4), AXES)
    seq, tp = ("x", "zh", "y"), ("zl", "c")
    rows, wide, tall, vector = P(seq, None), P(seq, tp), P(tp, seq), P(seq)
    in_specs = (
        rows,
        vector,
        vector,
        wide,
        wide,
        wide,
        wide,
        tall,
        vector,
        vector,
        wide,
        tall,
        P(tp),
        rows,
    )
    out_specs = (
        rows,
        rows,
        vector,
        vector,
        wide,
        wide,
        wide,
        wide,
        tall,
        vector,
        vector,
        wide,
        tall,
    )
    return jax.shard_map(body, mesh=fine, in_specs=in_specs, out_specs=out_specs, check_vma=False)
```

time: 555 us -> 478 us (0.86)
  the two profiles are of different devices: /device:TPU:53 before, /device:TPU:1 now
where the time goes in v2:
time: 478 us; the launch traced here: 474 us
  waiting for transfers between devices  165 us (35%)
  starting transfers between devices  134 us (28%)
  Pallas kernels  68 us (14%)
  local copies, waits for them, and re-layouts  39.1 us (8%)
  other arithmetic  30.5 us (6%)
  between operations  16.2 us (3%)
  blocking collectives  14.4 us (3%)
  matrix products  6.9 us (1%)
    pallas_call x24, Pallas kernels, run(): pl.pallas_call(kernel, grid=grid, in_specs=ins, out_specs=[o[1] for o in...  68 us
    all_to_all x2, waiting for transfers between devices, scatter_sum(): total = lax.all_to_all(total, ('x', 'y'), 0, 0, tiled=True)  50.3 us
    ppermute x18, waiting for transfers between devices, z_shift(): return lax.ppermute(values, ('zl', 'zh'), pairs(('zl', 'zh'), move))  46.8 us
    ppermute x8, starting transfers between devices, swap_roles(): lax.ppermute(values, ('c', 'zh'), pairs(('c', 'zh'), lambda p: {'c': p['z...  39.5 us
    unnamed x112, local copies, waits for them, and re-layouts  32.5 us
    ppermute x8, waiting for transfers between devices, swap_roles(): lax.ppermute(values, ('c', 'zh'), pairs(('c', 'zh'), lambda p: {'c': p['z...  25.7 us
    ppermute x18, starting transfers between devices, z_shift(): return lax.ppermute(values, ('zl', 'zh'), pairs(('zl', 'zh'), move))  24.3 us
    ppermute x6, starting transfers between devices, z_shift_home(): lax.ppermute(values, ('zl', 'c', 'zh'), pairs(('zl', 'c', 'zh'), move))  18.1 us
  transfers between devices with their start and end apart: 46, of which 27 were waited for; matrix products, arithmetic and copies ran while one was open for 8% of the time, Pallas kernels for 10%

profile of v2, /device:TPU:1, one launch (start us, length us, event | category | flops | bytes accessed | tf_op | source)
XLA Modules:
  0.0 474.0 jit_solution(14766958955760201517)
XLA Ops:
  14.3 6.9 %collective-permute-start.5 = (bf16[64,4608]{1,0:T(8,128)(2,1)S(1)}, bf16[64,4608]{1,0:T(8,128)(2,1)S(1)}, u32[]{:S(2)}, u32[]{:S(2)}) collective-permute-start(bf16[64,4608]{1,0:T(8,128)(2,1)S(1)} %shard_map.239), channel_id=1, source_target_pairs={{0,0},{4,32},{32,4},{36,36},{1,1},{5,33},{33,5},{37,37},{2,2},{6,3... | collective-permute-start | bytes 1769480 | tf_op jit(solution)/shard_map/ppermute | solution.py:37
  21.2 7.6 %collective-permute-done.5 = bf16[64,4608]{1,0:T(8,128)(2,1)S(1)} collective-permute-done((bf16[64,4608]{1,0:T(8,128)(2,1)S(1)}, bf16[64,4608]{1,0:T(8,128)(2,1)S(1)}, u32[]{:S(2)}, u32[]{:S(2)}) %collective-permute-start.5) | collective-permute-done | bytes 589856 | tf_op jit(solution)/shard_map/ppermute | solution.py:37
  40.7 6.7 %all-to-all-start = ((bf16[16,64,1664]{2,1,0:T(8,128)(2,1)}), bf16[16,64,1664]{2,1,0:T(8,128)(2,1)S(1)}, u32[]{:S(2)}, u32[]{:S(2)}) async-start(bf16[16,64,1664]{2,1,0:T(8,128)(2,1)} %broadcast_in_dim.6), calls=%async_computation | async-start | bytes 6815744 | tf_op jit(solution)/shard_map/all_to_all | solution.py:762
  68.6 8.2 %collective-permute-done.2 = bf16[256,2048]{1,0:T(8,128)(2,1)} collective-permute-done((bf16[256,2048]{1,0:T(8,128)(2,1)}, bf16[256,2048]{1,0:T(8,128)(2,1)}, u32[]{:S(2)}, u32[]{:S(2)}) %collective-permute-start.2) | collective-permute-done | bytes 1048608 | tf_op jit(solution)/shard_map/ppermute | solution.py:37
  81.0 6.0 %collective-permute-done.4.gains_other.key_other.value_other.w_other = bf16[1024,1664]{1,0:T(8,128)(2,1)S(1)} collective-permute-done((bf16[1024,1664]{1,0:T(8,128)(2,1)S(1)}, bf16[1024,1664]{1,0:T(8,128)(2,1)S(1)}, u32[]{:S(2)}, u32[]{:S(2)}) %collective-permute-start.4) | collective-permute-done | bytes 3407904 | tf_op jit(solution)/shard_map/ppermute | solution.py:70
  102.3 7.6 %all-to-all-start.1 = ((bf16[32,16,512]{2,1,0:T(8,128)(2,1)}), bf16[32,16,512]{2,1,0:T(8,128)(2,1)S(1)}, u32[]{:S(2)}, u32[]{:S(2)}) async-start(bf16[32,16,512]{2,1,0:T(8,128)(2,1)} %bitcast.13), calls=%async_computation.1 | async-start | bytes 1048576 | tf_op jit(solution)/shard_map/all_to_all | solution.py:118
  111.8 13.4 %all-to-all-done.1.parts = bf16[32,16,512]{2,1,0:T(8,128)(2,1)S(1)} async-done(((bf16[32,16,512]{2,1,0:T(8,128)(2,1)}), bf16[32,16,512]{2,1,0:T(8,128)(2,1)S(1)}, u32[]{:S(2)}, u32[]{:S(2)}) %all-to-all-start.1) | async-done | bytes 524320 | tf_op jit(solution)/shard_map/all_to_all | solution.py:118
  126.2 10.5 %all-gather.2.cloned.1.call-done.w_query.w_gate.w_out.w_up = bf16[2048,4608]{1,0:T(8,128)(2,1)} async-done(((bf16[64,4608]{1,0:T(8,128)(2,1)}), bf16[2048,4608]{1,0:T(8,128)(2,1)}) %all-gather.2.cloned.1.call-update) | async-done | bytes 18874384 | tf_op jit(solution)/shard_map/all_gather | solution.py:765
  136.7 5.4 %all-to-all-start.2 = ((bf16[32,16,512]{2,1,0:T(8,128)(2,1)}), bf16[32,16,512]{2,1,0:T(8,128)(2,1)S(1)}, u32[]{:S(2)}, u32[]{:S(2)}) async-start(bf16[32,16,512]{2,1,0:T(8,128)(2,1)} %shard_map.241), calls=%async_computation.2 | async-start | bytes 1048576 | tf_op jit(solution)/shard_map/all_to_all | solution.py:122
  167.1 6.8 %collective-permute-done.8 = bf16[64,2048]{1,0:T(8,128)(2,1)S(1)} collective-permute-done((bf16[64,2048]{1,0:T(8,128)(2,1)S(1)}, bf16[64,2048]{1,0:T(8,128)(2,1)S(1)}, u32[]{:S(2)}, u32[]{:S(2)}) %collective-permute-start.8) | collective-permute-done | bytes 262176 | tf_op jit(solution)/shard_map/ppermute | solution.py:47
  184.1 7.7 %collective-permute-done.10 = bf16[64,2048]{1,0:T(8,128)(2,1)S(1)} collective-permute-done((bf16[64,2048]{1,0:T(8,128)(2,1)S(1)}, bf16[64,2048]{1,0:T(8,128)(2,1)S(1)}, u32[]{:S(2)}, u32[]{:S(2)}) %collective-permute-start.10) | collective-permute-done | bytes 262176 | tf_op jit(solution)/shard_map/ppermute | solution.py:47
  213.8 5.7 %collective-permute-done.12 = bf16[64,2048]{1,0:T(8,128)(2,1)S(1)} collective-permute-done((bf16[64,2048]{1,0:T(8,128)(2,1)S(1)}, bf16[64,2048]{1,0:T(8,128)(2,1)S(1)}, u32[]{:S(2)}, u32[]{:S(2)}) %collective-permute-start.12) | collective-permute-done | bytes 262176 | tf_op jit(solution)/shard_map/ppermute | solution.py:47
  233.0 7.7 %collective-permute-done.23 = bf16[64,2048]{1,0:T(8,128)(2,1)S(1)} collective-permute-done((bf16[64,2048]{1,0:T(8,128)(2,1)S(1)}, bf16[64,2048]{1,0:T(8,128)(2,1)S(1)}, u32[]{:S(2)}, u32[]{:S(2)}) %collective-permute-start.23) | collective-permute-done | bytes 262176 | tf_op jit(solution)/shard_map/ppermute | solution.py:47
  240.8 9.8 %shard_map.259 = bf16[2048,3072]{1,0:T(8,128)(2,1)} custom-call(bf16[256,2048]{1,0:T(8,128)(2,1)S(1)} %pad_maximum_fusion.normed.refs_0_, bf16[256,1024]{1,0:T(8,128)(2,1)S(1)} %get-tuple-element.124.refs_1_, bf16[256,2048]{1,0:T(8,128)(2,1)S(1)} %copy-done.2, bf16[256,1024]{1,0:T(8,128)(2,1)S(1)} %get-tuple-element.93.refs_3_, ...), custom_call_target="tpu_custom_call" | custom-call | flops 3221225472 | bytes 17301504 | tf_op jit(solution)/shard_map/pallas_call | solution.py:138
  270.7 14.4 %all_to_all.44.parts = bf16[32,16,512]{2,1,0:T(8,128)(2,1)S(1)} all-to-all(bf16[32,16,512]{2,1,0:T(8,128)(2,1)S(1)} %bitcast.37), channel_id=1, replica_groups=mesh['zl'=2,'c'=2,'x'=4,'zh'=2,'y'=4] {'x','c','y'}, dimensions={0} | all-to-all | bytes 1048576 | tf_op jit(solution)/shard_map/all_to_all | solution.py:118
  290.5 5.7 %add_convert_fusion.1 = bf16[1024,1536]{1,0:T(8,128)(2,1)} fusion(bf16[1024,1536]{1,0:T(8,128)(2,1)} %collective-permute-done.25, bf16[1024,1536]{1,0:T(8,128)(2,1)} %copy-done.12), kind=kLoop, calls=%fused_computation.1 | loop fusion | flops 6291456 | bytes 9437184 | tf_op jit(solution)/shard_map/convert_element_type | solution.py:126
  321.4 5.6 %shard_map.253 = (bf16[256,2048]{1,0:T(8,128)(2,1)S(1)}, f32[64,2048]{1,0:T(8,128)S(1)}, f32[2,2048]{1,0:T(2,128)S(1)}) custom-call(s32[2]{0:T(128)S(1)} %pad_add_fusion.place, f32[256,2048]{1,0:T(8,128)S(1)} %shard_map.249.first, bf16[256,1536]{1,0:T(8,128)(2,1)S(1)} %shard_map.252.d_both.refs_0_, bf16[1024,1664]{1,0:T(8,128)(2,1)} %bitcast.31, ...), custom_call_target="tpu_custom_call" | custom-call | flops 1610612736 | bytes 13385736 | tf_op jit(solution)/shard_map/pallas_call | solution.py:138
  328.8 50.3 %all-to-all-done.5 = bf16[16,64,1536]{2,1,0:T(8,128)(2,1)} async-done(((bf16[16,64,1536]{2,1,0:T(8,128)(2,1)}), bf16[16,64,1536]{2,1,0:T(8,128)(2,1)}, u32[]{:S(2)}, u32[]{:S(2)}) %all-to-all-start.5) | async-done | bytes 3145760 | tf_op jit(solution)/shard_map/all_to_all | solution.py:131
  386.6 8.9 %all-to-all-start.6 = ((bf16[16,64,1536]{2,1,0:T(8,128)(2,1)}), bf16[16,64,1536]{2,1,0:T(8,128)(2,1)}, u32[]{:S(2)}, u32[]{:S(2)}) async-start(bf16[16,64,1536]{2,1,0:T(8,128)(2,1)} %bitcast.40), calls=%async_computation.6 | async-start | bytes 6291456 | tf_op jit(solution)/shard_map/all_to_all | solution.py:131
  400.0 5.5 %collective-permute-start.16 = (bf16[64,2048]{1,0:T(8,128)(2,1)S(1)}, bf16[64,2048]{1,0:T(8,128)(2,1)S(1)}, u32[]{:S(2)}, u32[]{:S(2)}) collective-permute-start(bf16[64,2048]{1,0:T(8,128)(2,1)S(1)} %copy-done.29), channel_id=1, source_target_pairs={{4,0},{32,36},{68,64},{96,100},{5,1},{33,37},{69,65},{97,101},{6,2... | collective-permute-start | bytes 786440 | tf_op jit(solution)/shard_map/ppermute | solution.py:57
  412.8 8.3 %collective-permute-start.30 = (bf16[64,2048]{1,0:T(8,128)(2,1)S(1)}, bf16[64,2048]{1,0:T(8,128)(2,1)S(1)}, u32[]{:S(2)}, u32[]{:S(2)}) collective-permute-start(bf16[64,2048]{1,0:T(8,128)(2,1)S(1)} %add_convert_fusion.2.refs_0_), channel_id=1, source_target_pairs={{4,0},{32,36},{68,64},{96,100},{5,1},{33,37},{69,65},{97,101},{6,2... | collective-permute-start | bytes 786440 | tf_op jit(solution)/shard_map/ppermute | solution.py:57
  427.9 7.8 %collective-permute-start.34 = (bf16[64,1536]{1,0:T(8,128)(2,1)}, bf16[64,1536]{1,0:T(8,128)(2,1)S(1)}, u32[]{:S(2)}, u32[]{:S(2)}) collective-permute-start(bf16[64,1536]{1,0:T(8,128)(2,1)} %reduce_sum.113), channel_id=1, source_target_pairs={{0,0},{4,32},{32,4},{36,36},{1,1},{5,33},{33,5},{37,37},{2,2},{6,3... | collective-permute-start | bytes 589832 | tf_op jit(solution)/shard_map/ppermute | solution.py:37
  441.7 9.6 %all-to-all-start.7 = ((f32[128,1,256]{2,1,0:T(1,128)}), f32[128,1,256]{2,1,0:T(1,128)}, u32[]{:S(2)}, u32[]{:S(2)}) async-start(f32[128,1,256]{2,1,0:T(1,128)} %all_to_all.34), calls=%async_computation.7 | async-start | bytes 262144 | tf_op jit(solution)/shard_map/all_to_all | solution.py:845
  455.5 5.4 %collective-permute-start.35 = (bf16[64,1536]{1,0:T(8,128)(2,1)}, bf16[64,1536]{1,0:T(8,128)(2,1)S(1)}, u32[]{:S(2)}, u32[]{:S(2)}) collective-permute-start(bf16[64,1536]{1,0:T(8,128)(2,1)} %reduce_sum.114), channel_id=1, source_target_pairs={{0,0},{4,32},{32,4},{36,36},{1,1},{5,33},{33,5},{37,37},{2,2},{6,3... | collective-permute-start | bytes 589832 | tf_op jit(solution)/shard_map/ppermute | solution.py:37
  (252 shorter events, 226.3 us)
Async XLA Ops:
  7.2 129.5 %all-gather.2.cloned.1.call-start = ((), (), s32[]{:S(2)}) async-start(), calls=%async_computation.9 | async-start | bytes 19464192 | tf_op jit(solution)/shard_map/all_gather | solution.py:765
  14.3 14.5 %collective-permute-start.5 = (bf16[64,4608]{1,0:T(8,128)(2,1)S(1)}, bf16[64,4608]{1,0:T(8,128)(2,1)S(1)}, u32[]{:S(2)}, u32[]{:S(2)}) collective-permute-start(bf16[64,4608]{1,0:T(8,128)(2,1)S(1)} %shard_map.239), channel_id=1, source_target_pairs={{0,0},{4,32},{32,4},{36,36},{1,1},{5,33},{33,5},{37,37},{2,2},{6,3... | collective-permute-start | bytes 1769480 | tf_op jit(solution)/shard_map/ppermute | solution.py:37
  40.7 40.2 %all-to-all-start = ((bf16[16,64,1664]{2,1,0:T(8,128)(2,1)}), bf16[16,64,1664]{2,1,0:T(8,128)(2,1)S(1)}, u32[]{:S(2)}, u32[]{:S(2)}) async-start(bf16[16,64,1664]{2,1,0:T(8,128)(2,1)} %broadcast_in_dim.6), calls=%async_computation | async-start | bytes 6815744 | tf_op jit(solution)/shard_map/all_to_all | solution.py:762
  47.5 18.1 %collective-permute-start.1 = (bf16[256,2048]{1,0:T(8,128)(2,1)}, bf16[256,2048]{1,0:T(8,128)(2,1)}, u32[]{:S(2)}, u32[]{:S(2)}) collective-permute-start(bf16[256,2048]{1,0:T(8,128)(2,1)} %param.14), channel_id=1, source_target_pairs={{0,0},{4,32},{32,4},{36,36},{1,1},{5,33},{33,5},{37,37},{2,2},{6,3... | collective-permute-start | bytes 3145736 | tf_op jit(solution)/shard_map/ppermute | solution.py:37
  52.7 24.0 %collective-permute-start.2 = (bf16[256,2048]{1,0:T(8,128)(2,1)}, bf16[256,2048]{1,0:T(8,128)(2,1)}, u32[]{:S(2)}, u32[]{:S(2)}) collective-permute-start(bf16[256,2048]{1,0:T(8,128)(2,1)} %param.27), channel_id=1, source_target_pairs={{0,0},{4,32},{32,4},{36,36},{1,1},{5,33},{33,5},{37,37},{2,2},{6,3... | collective-permute-start | bytes 3145736 | tf_op jit(solution)/shard_map/ppermute | solution.py:37
  54.7 25.1 %collective-permute-start.3 = (f32[2]{0:T(128)S(1)}, f32[2]{0:T(128)S(1)}, u32[]{:S(2)}, u32[]{:S(2)}) collective-permute-start(f32[2]{0:T(128)S(1)} %copy-done.55), channel_id=1, source_target_pairs={{0,0},{4,32},{32,4},{36,36},{1,1},{5,33},{33,5},{37,37},{2,2},{6,3... | collective-permute-start | bytes 32 | tf_op jit(solution)/shard_map/ppermute | solution.py:37
  102.3 22.9 %all-to-all-start.1 = ((bf16[32,16,512]{2,1,0:T(8,128)(2,1)}), bf16[32,16,512]{2,1,0:T(8,128)(2,1)S(1)}, u32[]{:S(2)}, u32[]{:S(2)}) async-start(bf16[32,16,512]{2,1,0:T(8,128)(2,1)} %bitcast.13), calls=%async_computation.1 | async-start | bytes 1048576 | tf_op jit(solution)/shard_map/all_to_all | solution.py:118
  136.7 16.4 %all-to-all-start.2 = ((bf16[32,16,512]{2,1,0:T(8,128)(2,1)}), bf16[32,16,512]{2,1,0:T(8,128)(2,1)S(1)}, u32[]{:S(2)}, u32[]{:S(2)}) async-start(bf16[32,16,512]{2,1,0:T(8,128)(2,1)} %shard_map.241), calls=%async_computation.2 | async-start | bytes 1048576 | tf_op jit(solution)/shard_map/all_to_all | solution.py:122
  142.1 293.6 %reduce-scatter.2.cloned.1.call-start = ((), (), s32[]{:S(2)}) async-start(), calls=%async_computation.10 | async-start | bytes 12976128 | tf_op jit(solution)/shard_map/reduce_scatter | solution.py:813
  204.8 14.7 %collective-permute-start.12 = (bf16[64,2048]{1,0:T(8,128)(2,1)S(1)}, bf16[64,2048]{1,0:T(8,128)(2,1)S(1)}, u32[]{:S(2)}, u32[]{:S(2)}) collective-permute-start(bf16[64,2048]{1,0:T(8,128)(2,1)S(1)} %get-tuple-element.147), channel_id=1, source_target_pairs={{0,64},{4,68},{64,4},{68,0},{1,65},{5,69},{65,5},{69,1},{2,66},{6,... | collective-permute-start | bytes 786440 | tf_op jit(solution)/shard_map/ppermute | solution.py:47
  206.3 17.7 %collective-permute-start.14 = (bf16[64,2048]{1,0:T(8,128)(2,1)S(1)}, bf16[64,2048]{1,0:T(8,128)(2,1)S(1)}, u32[]{:S(2)}, u32[]{:S(2)}) collective-permute-start(bf16[64,2048]{1,0:T(8,128)(2,1)S(1)} %get-tuple-element.148), channel_id=1, source_target_pairs={{0,4},{4,0},{64,68},{68,64},{1,5},{5,1},{65,69},{69,65},{2,6},{6,2... | collective-permute-start | bytes 786440 | tf_op jit(solution)/shard_map/ppermute | solution.py:47
  206.5 17.5 %collective-permute-start.13 = (bf16[64,2048]{1,0:T(8,128)(2,1)S(1)}, bf16[64,2048]{1,0:T(8,128)(2,1)S(1)}, u32[]{:S(2)}, u32[]{:S(2)}) collective-permute-start(bf16[64,2048]{1,0:T(8,128)(2,1)S(1)} %get-tuple-element.149), channel_id=1, source_target_pairs={{0,68},{4,64},{64,0},{68,4},{1,69},{5,65},{65,1},{69,5},{2,70},{6,... | collective-permute-start | bytes 786440 | tf_op jit(solution)/shard_map/ppermute | solution.py:47
  269.1 21.4 %collective-permute-start.25 = (bf16[1024,1536]{1,0:T(8,128)(2,1)}, bf16[1024,1536]{1,0:T(8,128)(2,1)}, u32[]{:S(2)}, u32[]{:S(2)}) collective-permute-start(bf16[1024,1536]{1,0:T(8,128)(2,1)} %get-tuple-element.105), channel_id=1, source_target_pairs={{0,32},{32,0},{1,33},{33,1},{2,34},{34,2},{3,35},{35,3},{4,36},{36... | collective-permute-start | bytes 9437192 | tf_op jit(solution)/shard_map/ppermute | solution.py:70
  286.0 15.7 %all-to-all-start.4 = ((bf16[32,16,512]{2,1,0:T(8,128)(2,1)}), bf16[32,16,512]{2,1,0:T(8,128)(2,1)S(1)}, u32[]{:S(2)}, u32[]{:S(2)}) async-start(bf16[32,16,512]{2,1,0:T(8,128)(2,1)} %shard_map.251), calls=%async_computation.4 | async-start | bytes 1048576 | tf_op jit(solution)/shard_map/all_to_all | solution.py:122
  310.9 71.3 %collective-permute-start.33 = (bf16[1024,1536]{1,0:T(8,128)(2,1)}, bf16[1024,1536]{1,0:T(8,128)(2,1)}, u32[]{:S(2)}, u32[]{:S(2)}) collective-permute-start(bf16[1024,1536]{1,0:T(8,128)(2,1)} %get-tuple-element.114), channel_id=1, source_target_pairs={{0,32},{32,0},{1,33},{33,1},{2,34},{34,2},{3,35},{35,3},{4,36},{36... | collective-permute-start | bytes 9437192 | tf_op jit(solution)/shard_map/ppermute | solution.py:70
  311.9 67.2 %all-to-all-start.5 = ((bf16[16,64,1536]{2,1,0:T(8,128)(2,1)}), bf16[16,64,1536]{2,1,0:T(8,128)(2,1)}, u32[]{:S(2)}, u32[]{:S(2)}) async-start(bf16[16,64,1536]{2,1,0:T(8,128)(2,1)} %bitcast.41), calls=%async_computation.5 | async-start | bytes 6291456 | tf_op jit(solution)/shard_map/all_to_all | solution.py:131
  386.6 51.2 %all-to-all-start.6 = ((bf16[16,64,1536]{2,1,0:T(8,128)(2,1)}), bf16[16,64,1536]{2,1,0:T(8,128)(2,1)}, u32[]{:S(2)}, u32[]{:S(2)}) async-start(bf16[16,64,1536]{2,1,0:T(8,128)(2,1)} %bitcast.40), calls=%async_computation.6 | async-start | bytes 6291456 | tf_op jit(solution)/shard_map/all_to_all | solution.py:131
  399.3 21.8 %collective-permute-start.17 = (bf16[64,2048]{1,0:T(8,128)(2,1)S(1)}, bf16[64,2048]{1,0:T(8,128)(2,1)S(1)}, u32[]{:S(2)}, u32[]{:S(2)}) collective-permute-start(bf16[64,2048]{1,0:T(8,128)(2,1)S(1)} %copy-done.29), channel_id=1, source_target_pairs={{0,64},{36,100},{68,0},{96,36},{1,65},{37,101},{69,1},{97,37},{2,6... | collective-permute-start | bytes 786440 | tf_op jit(solution)/shard_map/ppermute | solution.py:57
  400.0 22.5 %collective-permute-start.16 = (bf16[64,2048]{1,0:T(8,128)(2,1)S(1)}, bf16[64,2048]{1,0:T(8,128)(2,1)S(1)}, u32[]{:S(2)}, u32[]{:S(2)}) collective-permute-start(bf16[64,2048]{1,0:T(8,128)(2,1)S(1)} %copy-done.29), channel_id=1, source_target_pairs={{4,0},{32,36},{68,64},{96,100},{5,1},{33,37},{69,65},{97,101},{6,2... | collective-permute-start | bytes 786440 | tf_op jit(solution)/shard_map/ppermute | solution.py:57
  423.1 28.2 %collective-permute-start.18 = (bf16[256,2048]{1,0:T(8,128)(2,1)S(1)}, bf16[256,2048]{1,0:T(8,128)(2,1)}, u32[]{:S(2)}, u32[]{:S(2)}) collective-permute-start(bf16[256,2048]{1,0:T(8,128)(2,1)S(1)} %shard_map.245.mine), channel_id=1, source_target_pairs={{0,32},{36,4},{1,33},{37,5},{2,34},{38,6},{3,35},{39,7},{8,40},{44... | collective-permute-start | bytes 3145736 | tf_op jit(solution)/shard_map/ppermute | solution.py:66
  426.3 27.0 %collective-permute-start.32 = (bf16[256,2048]{1,0:T(8,128)(2,1)S(1)}, bf16[256,2048]{1,0:T(8,128)(2,1)S(1)}, u32[]{:S(2)}, u32[]{:S(2)}) collective-permute-start(bf16[256,2048]{1,0:T(8,128)(2,1)S(1)} %shard_map.254.mine), channel_id=1, source_target_pairs={{0,32},{36,4},{1,33},{37,5},{2,34},{38,6},{3,35},{39,7},{8,40},{44... | collective-permute-start | bytes 3145736 | tf_op jit(solution)/shard_map/ppermute | solution.py:66
  427.9 26.8 %collective-permute-start.34 = (bf16[64,1536]{1,0:T(8,128)(2,1)}, bf16[64,1536]{1,0:T(8,128)(2,1)S(1)}, u32[]{:S(2)}, u32[]{:S(2)}) collective-permute-start(bf16[64,1536]{1,0:T(8,128)(2,1)} %reduce_sum.113), channel_id=1, source_target_pairs={{0,0},{4,32},{32,4},{36,36},{1,1},{5,33},{33,5},{37,37},{2,2},{6,3... | collective-permute-start | bytes 589832 | tf_op jit(solution)/shard_map/ppermute | solution.py:37
  435.7 29.5 %collective-permute-start.36 = (bf16[64,3072]{1,0:T(8,128)(2,1)}, bf16[64,3072]{1,0:T(8,128)(2,1)}, u32[]{:S(2)}, u32[]{:S(2)}) collective-permute-start(bf16[64,3072]{1,0:T(8,128)(2,1)} %reduce-scatter.2.cloned.1.call-done), channel_id=1, source_target_pairs={{0,0},{4,32},{32,4},{36,36},{1,1},{5,33},{33,5},{37,37},{2,2},{6,3... | collective-permute-start | bytes 1179656 | tf_op jit(solution)/shard_map/ppermute | solution.py:37
  441.7 19.5 %all-to-all-start.7 = ((f32[128,1,256]{2,1,0:T(1,128)}), f32[128,1,256]{2,1,0:T(1,128)}, u32[]{:S(2)}, u32[]{:S(2)}) async-start(f32[128,1,256]{2,1,0:T(1,128)} %all_to_all.34), calls=%async_computation.7 | async-start | bytes 262144 | tf_op jit(solution)/shard_map/all_to_all | solution.py:845
  (78 other events, 718.0 us)
Sparse Core Ops, SparseCore 0:
  29.7 106.9 all-gather.1
  250.8 136.2 reduce-scatter.1

commit v3 on v2

--- a/solution.py
+++ b/solution.py
@@ -13,6 +13,17 @@
 AXES = ("zl", "c", "x", "zh", "y")
 SIZES = {"zl": 2, "c": 2, "x": 4, "zh": 2, "y": 4}
 SPANS = ("x", "c", "y")
+CHIPS = ("c", "x", "y")
+ALONG_X = [[x * 4 + y for x in range(4)] for y in range(4)]
+ALONG_Y = [[x * 4 + y for y in range(4)] for x in range(4)]
+
+
+def other_core(groups):
+    return [[16 + i for i in group] for group in groups]
+
+
+FIRST_WAY = ALONG_X + other_core(ALONG_Y)
+SECOND_WAY = ALONG_Y + other_core(ALONG_X)
 BF = jnp.bfloat16
 F32 = jnp.float32
 
@@ -70,23 +81,25 @@
     return lax.ppermute(values, "c", [(0, 1), (1, 0)])
 
 
-def z_reduce(part, mine):
-    rows = part.shape[0] // 4
-    total = mine
-    for shift in (1, 3, 2):
-        total = total + z_shift(part[shift * rows : (shift + 1) * rows], shift).astype(F32)
-    return total
+def z_collect(parts):
+    return [z_shift(parts[shift - 1], shift) for shift in (1, 3, 2)]
 
 
 def z_gather(values):
-    near, far, across = z_shift(values, 3), z_shift(values, 1), z_shift(values, 2)
-    return jnp.concatenate([values, near, across, far], axis=0)
+    return [values, z_shift(values, 3), z_shift(values, 2), z_shift(values, 1)]
 
 
 def z_gather_home(values, place, home, dtype):
     near, far, across = z_shift_home(values, 3), z_shift_home(values, 1), z_shift_home(values, 2)
     full = in_place(place, values, near, across, far)
     return chosen(home, full, core_from_home(full), dtype)
+
+
+def to_owner(values, flip_z, flip_core):
+    def move(place):
+        return {"zl": place["zl"] ^ flip_z, "zh": place["c"], "c": place["zh"] ^ flip_core}
+
+    return lax.ppermute(values, ("zl", "c", "zh"), pairs(("zl", "c", "zh"), move))
 
 
 def nn(left, right):
@@ -122,28 +135,20 @@
     return lax.all_to_all(carried, SPANS, 0, 0, tiled=True).reshape(2 * DK, DV)
 
 
-def halves_sum(own, other):
-    total = (own.astype(F32) + core_swap(other).astype(F32)).astype(BF)
-    return total.reshape(16, 64, own.shape[1])
-
-
-def scatter_sum(total):
-    total = lax.all_to_all(total, ("x", "y"), 0, 0, tiled=True)
-    return jnp.sum(total.astype(F32), axis=0).astype(BF)
-
-
-def run(kernel, grid, ins, outs, operands, flops, scratch=()):
-    moved = sum(a.size * a.dtype.itemsize for a in operands)
-    moved += sum(o[0].size * o[0].dtype.itemsize for o in outs)
+def exchange(values, groups):
+    return lax.all_to_all(values, CHIPS, 0, 0, axis_index_groups=groups, tiled=True)
+
+
+def run(kernel, grid, ins, outs, operands, scratch=(), limit=48, flops=1, moved=1):
     return pl.pallas_call(
         kernel,
         grid=grid,
         in_specs=ins,
         out_specs=[o[1] for o in outs],
-        out_shape=[o[0] for o in outs],
+        out_shape=[pltpu.HBM(o[0].shape, o[0].dtype) if len(o) > 2 else o[0] for o in outs],
         scratch_shapes=list(scratch),
-        compiler_params=pltpu.CompilerParams(vmem_limit_bytes=48 * 1024 * 1024),
-        cost_estimate=pl.CostEstimate(flops=int(flops), bytes_accessed=int(moved), transcendentals=0),
+        compiler_params=pltpu.CompilerParams(vmem_limit_bytes=limit * 1024 * 1024),
+        cost_estimate=pl.CostEstimate(flops=flops, bytes_accessed=moved, transcendentals=0),
     )(*operands)
 
 
@@ -199,7 +204,6 @@
         [SCALARS] + [whole((64, 2048))] * 4,
         [(shape((256, 2048), BF), whole((256, 2048)))],
         [place, *pieces],
-        1,
     )[0]
 
 
@@ -221,7 +225,6 @@
         [SCALARS, block, block],
         [(shape((256, 2048), dtype), block)],
         [home, mine, other],
-        1,
     )[0]
 
 
@@ -241,32 +244,16 @@
         [SCALARS, whole(dims)],
         [(shape(dims, BF), whole(dims))],
         [rate, parts],
-        2 * 32 * 16 * DV,
-    )[0]
-
-
-def pack_kernel(*refs):
+    )[0]
+
+
+def pack_kernel(gains, *refs):
     out, start = refs[-1], 0
     for ref in refs[:-1]:
         out[:, start : start + ref.shape[1]] = ref[...]
         start += ref.shape[1]
-
-
-def pack(*parts):
-    cols = sum(p.shape[1] for p in parts)
-    return run(
-        pack_kernel,
-        (1,),
-        [whole(p.shape) for p in parts],
-        [(shape((64, cols), BF), whole((64, cols)))],
-        list(parts),
-        1,
-    )[0]
-
-
-def pack_first_kernel(w_key, w_value, gains, out):
-    out[:, :512] = w_key[...]
-    out[:, 512:1536] = w_value[...]
+        if start == 1536:
+            start += 128
     wide = gains[...].astype(F32)
     same = lax.broadcasted_iota(jnp.int32, (64, 64), 0) == lax.broadcasted_iota(
         jnp.int32, (64, 64), 1
@@ -276,17 +263,18 @@
     for k in range(4):
         column = jnp.sum(jnp.where(same, wide[k : k + 1, :], 0.0), axis=1, keepdims=True)
         total = jnp.where(lane == k, column, total)
-    out[:, 1536:] = total.astype(BF)
-
-
-def pack_first(w_key, w_value, gains):
-    return run(
-        pack_first_kernel,
-        (1,),
-        [whole((64, 512)), whole((64, 1024)), whole((4, 64))],
-        [(shape((64, 1664), BF), whole((64, 1664)))],
-        [w_key, w_value, gains],
-        1,
+    out[:, 1536:1664] = total.astype(BF)
+
+
+def pack(gains, *parts):
+    cols = 128 + sum(p.shape[1] for p in parts)
+    return run(
+        pack_kernel,
+        (1,),
+        [whole((4, 64))] + [whole(p.shape) for p in parts],
+        [(shape((64, cols), BF), whole((64, cols)))],
+        [gains, *parts],
+        limit=61,
     )[0]
 
 
@@ -317,13 +305,144 @@
             (shape((256, 2048), BF), whole((256, 2048))),
             (shape((256, 1024), BF), whole((256, 1024))),
             (shape((256, 1024), BF), whole((256, 1024))),
-            (shape((256, 2048), F32), whole((256, 2048))),
+            (shape((256, 2048), F32), whole((256, 2048)), "hbm"),
             (shape((256, 1), F32), whole((256, 1))),
             (shape((8, 2048), F32), whole((8, 2048))),
         ],
         [place, tokens, early, early_other],
-        10 * 256 * 2048,
-    )
+        limit=61,
+    )
+
+
+def roll_kernel(place, values, out):
+    for k in range(4):
+        at = place[0] + k
+        at = pl.multiple_of(jnp.where(at >= 4, at - 4, at) * 64, 64)
+        out[k * 64 : k * 64 + 64, :] = values[pl.ds(at, 64), :]
+
+
+def roll_rows(place, values):
+    return run(
+        roll_kernel,
+        (1,),
+        [SCALARS, whole((256, 2048))],
+        [(shape((256, 2048), BF), whole((256, 2048)))],
+        [place, values],
+    )[0]
+
+
+def add_kernel(*refs):
+    out, start = refs[-1], 0
+    for own, other in zip(refs[:-1:2], refs[1:-1:2]):
+        cols = own.shape[1]
+        total = own[...].astype(F32) + other[...].astype(F32)
+        out[:, start : start + cols] = total.astype(BF)
+        start += cols
+
+
+def add_halves(*pairs_of):
+    operands = [a for own, other in pairs_of for a in (own, core_swap(other))]
+    cols = sum(own.shape[1] for own, other in pairs_of)
+
+    def block(n):
+        return pl.BlockSpec((256, n), lambda i: (i, 0))
+
+    return run(
+        add_kernel,
+        (4,),
+        [block(a.shape[1]) for a in operands],
+        [(shape((1024, cols), BF), block(cols))],
+        operands,
+    )[0]
+
+
+def collected(mine, others):
+    total = mine[...]
+    for other in others:
+        total = total + other[...].astype(F32)
+    return total
+
+
+ROWS = pl.BlockSpec((64, 2048), lambda h: (0, 0))
+
+
+def resid_kernel(tokens, mine, one, two, three, gains, resid, hat, scale, normed):
+    total = tokens[...].astype(F32) + collected(mine, (one, two, three))
+    resid[...] = total
+    made, spread = norm_parts(total)
+    hat[...] = made
+    scale[...] = spread
+    normed[...] = (made * gains[2:3] + gains[3:4]).astype(BF)
+
+
+def resid_norm(tokens, mine, others, gains):
+    return run(
+        resid_kernel,
+        (1,),
+        [ROWS] * 5 + [whole((8, 2048))],
+        [
+            (shape((64, 2048), F32), ROWS),
+            (shape((64, 2048), F32), ROWS),
+            (shape((64, 1), F32), whole((64, 1))),
+            (shape((64, 2048), BF), ROWS),
+        ],
+        [tokens, mine, *others, gains],
+    )
+
+
+def resid_back_kernel(
+    out_grad, mine, one, two, three, gains, hat, scale, d_resid, d_attn, vectors
+):
+    total = collected(mine, (one, two, three))
+    made = out_grad[...].astype(F32) + norm_back(total * gains[2:3], hat[...], scale[...])
+    d_resid[...] = made
+    d_attn[...] = made.astype(BF)
+    vectors[0:1] = jnp.sum(total * hat[...], axis=0, keepdims=True)
+    vectors[1:2] = jnp.sum(total, axis=0, keepdims=True)
+
+
+def resid_back(out_grad, mine, others, gains, hat, scale):
+    return run(
+        resid_back_kernel,
+        (1,),
+        [ROWS] * 5 + [whole((8, 2048)), ROWS, whole((64, 1))],
+        [
+            (shape((64, 2048), F32), ROWS),
+            (shape((64, 2048), BF), ROWS),
+            (shape((2, 2048), F32), whole((2, 2048))),
+        ],
+        [out_grad, mine, *others, gains, hat, scale],
+    )
+
+
+def out_kernel(resid, mine, one, two, three, out):
+    out[...] = (resid[...] + collected(mine, (one, two, three))).astype(BF)
+
+
+def block_rows(resid, mine, others):
+    return run(
+        out_kernel,
+        (1,),
+        [ROWS] * 5,
+        [(shape((64, 2048), BF), ROWS)],
+        [resid, mine, *others],
+    )[0]
+
+
+def tokens_kernel(d_resid, mine, one, two, three, gains, hat, scale, out):
+    total = collected(mine, (one, two, three))
+    made = d_resid[...] + norm_back(total * gains[0:1], hat[...], scale[...])
+    out[...] = made.astype(BF)
+
+
+def tokens_back(d_resid, mine, others, gains, hat, scale):
+    return run(
+        tokens_kernel,
+        (1,),
+        [ROWS] * 5 + [whole((8, 2048)), ROWS, whole((64, 1))],
+        [(shape((64, 2048), BF), ROWS)],
+        [d_resid, mine, *others, gains, hat, scale],
+    )[0]
 
 
 def kv_kernel(
@@ -359,7 +478,7 @@
             (shape((512, 512), BF), pl.BlockSpec((256, 512), lambda h: (h, 0))),
         ],
         [rate, place, own, other, early, early_other, early, early_other, cosine, sine],
-        2 * 256 * 2048 * 1536,
+        limit=61,
     )
 
 
@@ -392,17 +511,28 @@
         ],
         [
             (shape((256, 512), BF), columns(256, 256)),
-            (shape((256, 1024), F32), columns(256, 512)),
+            (shape((256, 1024), F32), columns(256, 512), "hbm"),
             (shape((2, 256, 256), BF), pl.BlockSpec((1, 256, 256), lambda h: (h, 0, 0))),
             (shape((256, 1024), F32), columns(256, 512)),
         ],
         [rate, place, normed1, late, late, key, value, cosine, sine],
-        2 * 256 * 2048 * 1536,
-    )
+        limit=61,
+    )
+
+
+def cut_rows(full, parts):
+    parts[0][...] = full[:64]
+    for k in range(1, 4):
+        parts[k][...] = full[k * 64 : k * 64 + 64].astype(BF)
+
+
+def row_parts(cols, index):
+    spec = pl.BlockSpec((64, cols), index)
+    return [(shape((64, 2048), F32 if k == 0 else BF), spec) for k in range(4)]
 
 
 def retain_kernel(
-    rate, place, query, state, inner, gate, w_out, hat, scale, mixed, part, own, total
+    rate, place, query, state, inner, gate, w_out, hat, scale, mixed, mine, one, two, three, total
 ):
     h = pl.program_id(0)
     qdec, kdec = decays(rate[h], place[0])
@@ -421,9 +551,7 @@
 
     @pl.when(h == 1)
     def last():
-        full = total[...] + partial
-        part[...] = full.astype(BF)
-        own[...] = full[:64]
+        cut_rows(total[...] + partial, (mine, one, two, three))
 
 
 def retain(rate, place, query, state, inner, gate, late):
@@ -440,20 +568,29 @@
             columns(2048, 512, 2),
         ],
         [
-            (shape((256, 1024), F32), columns(256, 512)),
-            (shape((2, 256, 1), F32), pl.BlockSpec((1, 256, 1), lambda h: (h, 0, 0))),
+            (shape((256, 1024), F32), columns(256, 512), "hbm"),
+            (shape((2, 256, 1), F32), pl.BlockSpec((1, 256, 1), lambda h: (h, 0, 0)), "hbm"),
             (shape((256, 1024), BF), columns(256, 512)),
-            (shape((256, 2048), BF), whole((256, 2048))),
-            (shape((64, 2048), F32), whole((64, 2048))),
+            *row_parts(2048, lambda h: (0, 0)),
         ],
         [rate, place, query, state, inner, gate, late],
-        2 * 256 * 2048 * 1024,
         [pltpu.VMEM((256, 2048), F32)],
-    )
-
-
-def up_kernel(normed, w_up, d_hidden, hidden, d_up, part, own, total):
+        limit=61,
+    )
+
+
+def gathered(pieces, full):
+    @pl.when(pl.program_id(0) == 0)
+    def join():
+        for k, piece in enumerate(pieces):
+            full[k * 64 : k * 64 + 64, :] = piece[...]
+
+
+def up_kernel(
+    one, two, three, four, w_up, d_hidden, normed, hidden, d_up, mine, p1, p2, p3, total
+):
     j = pl.program_id(0)
+    gathered((one, two, three, four), normed)
     raw = nn(normed[...], w_up[...])
     root = 0.7978845608028654
     square = raw * raw
@@ -471,29 +608,29 @@
 
     @pl.when(j == 1)
     def last():
-        full = total[...] + partial
-        part[...] = full.astype(BF)
-        own[...] = full[:64]
-
-
-def up_back(normed2, late, d_hidden):
+        cut_rows(total[...] + partial, (mine, p1, p2, p3))
+
+
+def up_back(pieces, late, d_hidden):
     return run(
         up_kernel,
         (2,),
-        [whole((256, 2048)), columns(2048, 512, 4), columns(256, 512)],
-        [
+        [ROWS] * 4 + [columns(2048, 512, 4), columns(256, 512)],
+        [
+            (shape((256, 2048), BF), whole((256, 2048))),
             (shape((256, 1024), BF), columns(256, 512)),
             (shape((256, 1024), BF), columns(256, 512)),
-            (shape((256, 2048), BF), whole((256, 2048))),
-            (shape((64, 2048), F32), whole((64, 2048))),
-        ],
-        [normed2, late, d_hidden],
-        4 * 256 * 2048 * 1024,
+            *row_parts(2048, lambda h: (0, 0)),
+        ],
+        [*pieces, late, d_hidden],
         [pltpu.VMEM((256, 2048), F32)],
     )
 
 
-def mixed_kernel(rate, place, d_attn, w_out, gate, hat, scale, query, d_gate, d_ret, outgoing):
+def mixed_kernel(
+    rate, place, one, two, three, four, w_out, gate, hat, scale, query, d_attn, d_gate, d_ret, outgoing
+):
+    gathered((one, two, three, four), d_attn)
     qdec, kdec = decays(rate[pl.program_id(0)], place[0])
     d_mixed = nn(d_attn[...], w_out[...])
     wide, normed = gate[...], hat[...]
@@ -504,14 +641,14 @@
     outgoing[...] = tn((qdec * query[...].astype(F32)).astype(BF), made).astype(BF)
 
 
-def mixed_back(rate, place, d_attn, late, gate, hat, scale, query):
+def mixed_back(rate, place, pieces, late, gate, hat, scale, query):
     return run(
         mixed_kernel,
         (2,),
         [
             SCALARS,
             SCALARS,
-            whole((256, 2048)),
+            *[ROWS] * 4,
             columns(2048, 512, 2),
             columns(256, 512),
             columns(256, 512),
@@ -519,12 +656,13 @@
             columns(256, 256),
         ],
         [
+            (shape((256, 2048), BF), whole((256, 2048))),
             (shape((256, 1024), BF), columns(256, 512)),
             (shape((256, 1024), BF), columns(256, 512)),
             (shape((512, 512), BF), pl.BlockSpec((256, 512), lambda h: (h, 0))),
         ],
-        [rate, place, d_attn, late, gate, hat, scale, query],
-        2 * 256 * 2048 * 1024,
+        [rate, place, *pieces, late, gate, hat, scale, query],
+        limit=61,
     )
 
 
@@ -563,7 +701,6 @@
             (shape((256, 1024), F32), columns(256, 512)),
         ],
         [rate, place, d_ret, value, key, query, probs, state, cosine, sine],
-        2 * 256 * 256 * 2 * 2000,
     )
 
 
@@ -597,7 +734,7 @@
         ],
         [(shape((256, 1536), BF), whole((256, 1536)))],
         [rate, place, key_part, value_part, key, value, later, cosine, sine],
-        2 * 256 * 256 * 512 * 4,
+        limit=61,
     )[0]
 
 
@@ -617,19 +754,17 @@
         ],
         [(shape((256, 2048), F32), columns(256, 512))],
         [d_query, d_gate, late, late],
-        2 * 256 * 2048 * 1536,
-    )[0]
-
-
-def normed_back_kernel(place, first, d_both, w_own, w_other, hat, part, own, vectors):
+    )[0]
+
+
+def normed_back_kernel(place, first, d_both, w_own, w_other, hat, mine, one, two, three, vectors):
     left = nt(d_both[...], w_own[:, :1536])
     right = nt(d_both[...], w_other[:, :1536])
     low = place[1] == 0
     total = first[...] + jnp.concatenate(
         [jnp.where(low, left, right), jnp.where(low, right, left)], axis=1
     )
-    part[...] = total.astype(BF)
-    own[...] = total[:64]
+    cut_rows(total, (mine, one, two, three))
     vectors[0:1] = jnp.sum(total * hat[...], axis=0, keepdims=True)
     vectors[1:2] = jnp.sum(total, axis=0, keepdims=True)
 
@@ -648,63 +783,177 @@
             columns(256, 512),
         ],
         [
-            (shape((256, 2048), BF), columns(256, 512)),
-            (shape((64, 2048), F32), columns(64, 512)),
+            *row_parts(512, lambda i: (0, i)),
             (shape((2, 2048), F32), columns(2, 512)),
         ],
         [place, first, d_both, early, early_other, hat],
-        2 * 256 * 2048 * 1536,
-    )
-
-
-def triple_kernel(*refs):
-    w, out = pl.program_id(0), refs[-1]
-    for k in range(3):
-
-        @pl.when(w == k)
-        def one(k=k):
-            out[...] = tn(refs[2 * k][...], refs[2 * k + 1][...]).astype(BF)
-
-
-def grad_triple(*operands):
+    )
+
+
+def pair_kernel(left_one, right_one, left_two, right_two, out):
+    w = pl.program_id(0)
+
+    @pl.when(w == 0)
+    def first():
+        out[...] = tn(left_one[...], right_one[...]).astype(BF)
+
+    @pl.when(w == 1)
+    def second():
+        out[...] = tn(left_two[...], right_two[...]).astype(BF)
+
+
+def grad_pair(left_one, right_one, left_two, right_two):
     def left(w):
-        return pl.BlockSpec(
-            (256, 512), lambda v, i: (0, jnp.where(v == w, i, jnp.where(v > w, 3, 0)))
-        )
+        return pl.BlockSpec((256, 512), lambda v, i: (0, jnp.where(v == w, i, 3 * (1 - w))))
 
     right = pl.BlockSpec((256, 1024), lambda v, i: (0, 0))
     return run(
-        triple_kernel,
-        (3, 4),
-        [left(0), right, left(1), right, left(2), right],
-        [(shape((2048, 3072), BF), pl.BlockSpec((512, 1024), lambda v, i: (i, v)))],
-        list(operands),
-        2 * 256 * 2048 * 3072,
-    )[0]
+        pair_kernel,
+        (2, 4),
+        [left(0), right, left(1), right],
+        [(shape((2048, 2048), BF), pl.BlockSpec((512, 1024), lambda v, i: (i, v)))],
+        [left_one, right_one, left_two, right_two],
+        flops=4 * 256 * 2048 * 1024,
+        moved=16 * 2048 * 1024,
+    )[0]
+
+
+def down_kernel(out_grad, w_down, d_hidden):
+    d_hidden[...] = nn(out_grad[...], w_down[...])
+
+
+def down_back(out_grad, late):
+    return run(
+        down_kernel,
+        (2,),
+        [whole((256, 2048)), columns(2048, 512, 6)],
+        [(shape((256, 1024), F32), columns(256, 512))],
+        [out_grad, late],
+    )[0]
+
+
+def ffn_kernel(hidden, w_down, mine, one, two, three):
+    cut_rows(nt(hidden[...], w_down[...]), (mine, one, two, three))
+
+
+def ffn_parts(hidden, late):
+    return run(
+        ffn_kernel,
+        (4,),
+        [whole((256, 1024)), pl.BlockSpec((512, 1024), lambda i: (i, 3))],
+        row_parts(512, lambda i: (0, i)),
+        [hidden, late],
+    )
+
+
+def store_rows(ref, made, side, start):
+    i = pl.program_id(0)
+    for j in range(4):
+        to = jnp.where(side == 0, i * 256 + j * 64, j * 256 + i * 64)
+        ref[pl.ds(pl.multiple_of(to, 64), 64), start : start + made.shape[1]] = made[
+            j * 64 : j * 64 + 64
+        ]
 
 
 def split_kernel(place, left, *refs):
     rights, own, other = refs[:-2], refs[-2], refs[-1]
     for ref, side in ((own, place[1]), (other, 1 - place[1])):
-        at = pl.multiple_of(side * 256, 256)
-        rows = left[:, pl.ds(at, 256)]
+        rows = left[:, pl.ds(pl.multiple_of(side * 256, 256), 256)]
         start = 0
         for right in rights:
-            ref[:, start : start + right.shape[1]] = tn(rows, right[...]).astype(BF)
+            store_rows(ref, tn(rows, right[...]).astype(BF), side, start)
             start += right.shape[1]
 
 
 def grad_split(place, left, rights):
     cols = sum(r.shape[1] for r in rights)
-    half = (shape((1024, cols), BF), pl.BlockSpec((256, cols), lambda i: (i, 0)))
+    half = (shape((1024, cols), BF), whole((1024, cols)))
     return run(
         split_kernel,
         (4,),
         [SCALARS, columns(256, 512)] + [whole(r.shape) for r in rights],
         [half, half],
         [place, left, *rights],
-        2 * 256 * 2048 * cols,
-    )
+    )
+
+
+def vector_kernel(place, vectors, own, other):
+    for ref, side in ((own, place[1]), (other, 1 - place[1])):
+        rows = vectors[:, pl.ds(pl.multiple_of(side * 256, 256), 256)]
+        rows = jnp.concatenate([rows, jnp.zeros((120, 256), F32)], axis=0)
+        store_rows(ref, rows.T.astype(BF), side, 0)
+
+
+def vector_split(place, vectors):
+    half = (shape((1024, 128), BF), whole((1024, 128)))
+    return run(
+        vector_kernel,
+        (4,),
+        [SCALARS, columns(8, 512)],
+        [half, half],
+        [place, vectors],
+    )
+
+
+def join_kernel(one, two, out):
+    start = 0
+    for ref in (one, two):
+        total = ref[0].astype(F32)
+        for k in range(1, 4):
+            total = total + ref[k].astype(F32)
+        out[:, start : start + total.shape[1]] = total.astype(BF)
+        start += total.shape[1]
+
+
+def join_sums(one, two):
+    def block(values):
+        return pl.BlockSpec((4, 64, values.shape[2]), lambda i: (0, i, 0))
+
+    cols = one.shape[2] + two.shape[2]
+    return run(
+        join_kernel,
+        (4,),
+        [block(one), block(two)],
+        [(shape((256, cols), BF), pl.BlockSpec((64, cols), lambda i: (i, 0)))],
+        [one, two],
+    )[0]
+
+
+def last_kernel(parts, main, rest):
+    total = parts[0].astype(F32)
+    for k in range(1, 4):
+        total = total + parts[k].astype(F32)
+    cols = main.shape[1]
+    main[...] = total[:, :cols].astype(BF)
+    rest[...] = total[:, cols:]
+
+
+def last_sum(parts):
+    cols = parts.shape[2] - 128
+    return run(
+        last_kernel,
+        (1,),
+        [whole(parts.shape)],
+        [(shape((64, cols), BF), whole((64, cols))), (shape((64, 128), F32), whole((64, 128)))],
+        [parts],
+    )
+
+
+def flip_kernel(*refs):
+    total = refs[0][...]
+    for ref in refs[1:-1]:
+        total = total + ref[...]
+    refs[-1][...] = total.T[:8]
+
+
+def flip_sum(*values):
+    return run(
+        flip_kernel,
+        (1,),
+        [whole((64, 128))] * len(values),
+        [(shape((8, 64), F32), whole((8, 64)))],
+        list(values),
+    )[0]
 
 
 def widen_kernel(values, *outs):
@@ -721,7 +970,6 @@
         [whole(values.shape)],
         [(shape((64, n), F32), whole((64, n))) for n in widths],
         [values],
-        1,
     )
 
 
@@ -746,17 +994,16 @@
     z = zh * 2 + zl
     home = (zh == c).astype(jnp.int32).reshape(1)
     span = x * 8 + c * 4 + y
-    place = jnp.stack([z, c]).astype(jnp.int32)
-
-    first = pack_first(
-        w_key, w_value, jnp.stack([norm1_gain, norm1_bias, norm2_gain, norm2_bias])
-    )
-    first, w_gate = lax.optimization_barrier((first, w_gate))
-    first = swap_roles(first)
-    second = swap_roles(pack(w_gate, w_out.T, w_up, w_down.T, w_query))
+    place = jnp.stack([z, c, x, y]).astype(jnp.int32)
+
+    gains = jnp.stack([norm1_gain, norm1_bias, norm2_gain, norm2_bias])
+    shards = swap_roles(
+        pack(gains, w_key, w_value, w_gate, w_out.T, w_up, w_down.T, w_query)
+    )
+    first, second = shards[:, :1664], shards[:, 1664:]
     rate = swap_roles(decay_rate)
+    tokens, kept = lax.optimization_barrier((tokens, shards))
     tokens = swap_roles(tokens)
-    out_grad = swap_roles(out_grad)
 
     cols = first.shape[1]
     early = lax.all_to_all(
@@ -764,102 +1011,107 @@
     ).reshape(1024, cols)
     late = lax.all_gather(second, SPANS, axis=0, tiled=True)
 
-    tokens = lax.dynamic_slice_in_dim(jnp.concatenate([tokens, tokens]), z * 64, 256, 0)
-    out_grad = lax.dynamic_slice_in_dim(jnp.concatenate([out_grad, out_grad]), z * 64, 256, 0)
+    tokens = roll_rows(place, tokens)
     index = ((jnp.arange(256) + z * 64) % 256).astype(F32)
     half = DK // 2
     position = (span * 256).astype(F32) + index
     freq = 10000.0 ** (-jnp.arange(half).astype(F32) / half)
     angle = position[:, None] * freq[None, :]
     cosine, sine = jnp.cos(angle), jnp.sin(angle)
-    early, tokens, out_grad, cosine, sine, rate = lax.optimization_barrier(
-        (early, tokens, out_grad, cosine, sine, rate)
+    early, tokens, cosine, sine, rate = lax.optimization_barrier(
+        (early, tokens, cosine, sine, rate)
     )
 
     early_other = core_swap(early)
     normed1, own, other, hat1, scale1, gains = norm_first(place, tokens, early, early_other)
-    gain1, gain2, bias2 = gains[0], gains[2], gains[3]
     key, value, fresh = key_value(rate, place, own, other, early, early_other, cosine, sine)
+    out_grad, fresh = lax.optimization_barrier((out_grad, fresh))
+    out_grad = roll_rows(place, swap_roles(out_grad))
     scan_rate = jnp.where(x < 2, rate[0], rate[1]).reshape(1)
     carried = scan_spans(scan_rate, scan_parts(fresh), False)
-    late, carried = lax.optimization_barrier((late, carried))
+    late, carried, out_grad = lax.optimization_barrier((late, carried, out_grad))
     state = scan_back(carried)
     query, gate, probs, inner = query_gate(
         rate, place, normed1, late, key, value, cosine, sine
     )
-    hat, scale, mixed, part, mine = retain(rate, place, query, state, inner, gate, late)
-
-    full_down = late[:, 3072:4096]
-    d_hidden = nn(out_grad, full_down)
-    resid = tokens[:64].astype(F32) + z_reduce(part, mine)
-    hat2, scale2 = norm_parts(resid)
-    normed2 = z_gather((hat2 * gain2 + bias2).astype(BF))
-    hidden, d_up, part, mine = up_back(normed2, late, d_hidden)
-    d_normed2 = z_reduce(part, mine)
-
-    ffn = nt(hidden, full_down)
-    ffn = z_reduce(ffn.astype(BF), ffn[:64])
-    block_out = z_gather_home((resid + ffn).astype(BF), place, home, BF)
-
-    own_grad = out_grad[:64].astype(F32)
-    d_resid = own_grad + norm_back(d_normed2 * gain2, hat2, scale2)
-    grad_gain2 = jnp.sum(d_normed2 * hat2, axis=0)
-    grad_bias2 = jnp.sum(d_normed2, axis=0)
-    d_attn = z_gather(d_resid.astype(BF))
-
-    d_gate, d_ret, outgoing = mixed_back(rate, place, d_attn, late, gate, hat, scale, query)
-    carried = scan_spans(scan_rate, scan_parts(outgoing), True)
+    hat, scale, mixed, mine, *parts = retain(rate, place, query, state, inner, gate, late)
+    parts = z_collect(parts)
+    out_grad, mine = lax.optimization_barrier((out_grad, mine))
+    d_hidden = down_back(out_grad, late)
+    resid, hat2, scale2, normed2 = resid_norm(tokens[:64], mine, parts, gains)
+    normed2, hidden, d_up, mine, *parts = up_back(z_gather(normed2), late, d_hidden)
+    parts = z_collect(parts)
+    grad_wide = grad_pair(normed2, d_up, out_grad, hidden)
+    mine, grad_wide = lax.optimization_barrier((mine, grad_wide))
+    d_resid, d_attn, vectors2 = resid_back(out_grad[:64], mine, parts, gains, hat2, scale2)
     grad_wide = swap_roles(
-        lax.psum_scatter(
-            grad_triple(normed2, d_up, out_grad, hidden, d_attn, mixed),
-            SPANS,
-            scatter_dimension=0,
-            tiled=True,
-        )
-    )
-    later = scan_back(carried)
+        lax.psum_scatter(grad_wide, SPANS, scatter_dimension=0, tiled=True)
+    )
+    d_attn, d_gate, d_ret, outgoing = mixed_back(
+        rate, place, z_gather(d_attn), late, gate, hat, scale, query
+    )
+    parts = scan_parts(outgoing)
 
     d_query, key_part, value_part = query_back(
         rate, place, d_ret, value, key, query, probs, state, cosine, sine
     )
+    gate_halves = grad_split(place, normed1, [d_gate, d_query])
+    out_halves = grad_split(place, d_attn, [mixed])
+    parts, gate_halves, out_halves = lax.optimization_barrier(
+        (parts, gate_halves, out_halves)
+    )
+    later = scan_back(scan_spans(scan_rate, parts, True))
+    hidden, d_query, parts = lax.optimization_barrier((hidden, d_query, parts))
     d_first = normed_back_first(d_query, d_gate, late)
-    grad_gate = halves_sum(*grad_split(place, normed1, [d_gate, d_query]))
-    grad_gate, later = lax.optimization_barrier((grad_gate, later))
-    grad_gate = scatter_sum(grad_gate)
+    ffn, *ffn_others = ffn_parts(hidden, late)
+    early_part = add_halves(gate_halves, out_halves)
+    early_part, later, ffn, d_first = lax.optimization_barrier(
+        (early_part, later, ffn, d_first)
+    )
+    early_part = exchange(early_part, FIRST_WAY)
+
     d_both = key_value_back(
         rate, place, key_part, value_part, key, value, later, cosine, sine
     )
-    grad_both = halves_sum(*grad_split(place, normed1, [d_both]))
-    grad_both, grad_gate = lax.optimization_barrier((grad_both, grad_gate))
-    grad_both = scatter_sum(grad_both)
-
-    part, mine, vectors1 = normed_back(place, d_first, d_both, early, early_other, hat1)
-    d_normed1 = z_reduce(part, mine)
-    tokens_grad = d_resid + norm_back(d_normed1 * gain1, hat1[:64], scale1[:64])
-    tokens_grad = z_gather_home(tokens_grad.astype(BF), place, home, F32)
-
-    vectors = jnp.concatenate([vectors1, jnp.stack([grad_gain2, grad_bias2])])
-    vectors = vectors.reshape(4, 32, 64).transpose(1, 0, 2).reshape(1, 32, 256)
-    vectors = jnp.broadcast_to(vectors, (4, 32, 256)).reshape(128, 256)
-    vectors, grad_both = lax.optimization_barrier((vectors, grad_both))
-    vectors = lax.all_to_all(vectors, AXES, 0, 0, tiled=True)
-    vectors = jnp.sum(vectors, axis=0)
-
-    grad_key, grad_value = widen(swap_roles(grad_both), [512, 1024])
-    grad_gate, grad_query = widen(swap_roles(grad_gate), [1024, 512])
-    grad_up, grad_down, grad_out = widen(grad_wide, [1024, 1024, 1024])
+    late_halves = grad_split(place, normed1, [d_both])
+    d_both, late_halves = lax.optimization_barrier((d_both, late_halves))
+    mine, *parts, vectors = normed_back(place, d_first, d_both, early, early_other, hat1)
+    vectors = jnp.concatenate([vectors, vectors2, jnp.zeros((4, 2048), F32)])
+    parts = z_collect(parts)
+    late_part = add_halves(late_halves, vector_split(place, vectors))
+    late_part, early_part = lax.optimization_barrier((late_part, early_part))
+    late_part = exchange(late_part, FIRST_WAY)
+
+    tokens_grad = tokens_back(d_resid, mine, parts, gains, hat1[:64], scale1[:64])
+    block_out = block_rows(resid, ffn, z_collect(ffn_others))
+    tokens_grad, late_part, block_out = lax.optimization_barrier(
+        (tokens_grad, late_part, block_out)
+    )
+    tokens_grad = z_gather_home(tokens_grad, place, home, F32)
+    block_out = z_gather_home(block_out, place, home, BF)
+
+    total = exchange(
+        join_sums(early_part.reshape(4, 256, -1), late_part.reshape(4, 256, -1)), SECOND_WAY
+    )
+    total, vectors = last_sum(total.reshape(4, 64, -1))
+    total = swap_roles(total)
+    vectors = flip_sum(*[to_owner(vectors, a, b) for a in (0, 1) for b in (0, 1)])
+    grad_gate, grad_query, grad_out, grad_key, grad_value = widen(
+        total, [1024, 512, 1024, 512, 1024]
+    )
+    grad_up, grad_down = widen(grad_wide, [1024, 1024])
     return (
         block_out,
         tokens_grad,
-        vectors[:64],
-        vectors[64:128],
+        vectors[0],
+        vectors[1],
         grad_query,
         grad_key,
         grad_value,
         grad_gate,
         grad_out.T,
-        vectors[128:192],
-        vectors[192:],
+        vectors[2],
+        vectors[3],
         grad_up,
         grad_down.T,
     )

time: 478 us -> 431 us (0.902)
  Pallas kernels: 68 us -> 109 us
  other arithmetic: 30.5 us -> 2.69 us
  waiting for transfers between devices: 165 us -> 139 us
  blocking collectives: 14.4 us -> 0 us
  starting transfers between devices: 134 us -> 120 us
  matrix products: 6.9 us -> 0 us
    all_to_all x3, waiting for transfers between devices: 50.5 us -> 2.85 us  [exchange(): lax.all_to_all(values, CHIPS, 0, 0, axis_index_groups=groups, tiled=True)]
    pallas_call x24 -> x37, Pallas kernels: 68 us -> 109 us  [run(): pl.pallas_call(kernel, grid=grid, in_specs=ins, out_specs=[o[1] for o in...]
    all_to_all x1, waiting for transfers between devices: 1.16 us -> 20.1 us  [body(): lax.all_to_all(jnp.broadcast_to(first[None], (16, 64, cols)), ('x', 'y'),...]
    all_to_all x1 -> x0, blocking collectives: 14.4 us -> none  [scan_parts(): return lax.all_to_all(fresh.reshape(32, 16, DV), SPANS, 0, 0, tiled=True)]
    convert_element_type x5 -> x0, other arithmetic: 11.8 us -> none  [the longest x2 10.2 us: halves_sum(): total = (own.astype(F32) + core_swap(other).astype(F32)).astype(BF)]
    reduce_sum x7 -> x0, other arithmetic: 10.4 us -> none  [the longest x2 6.17 us: scatter_sum(): return jnp.sum(total.astype(F32), axis=0).astype(BF)]
    all_to_all x3, starting transfers between devices: 23 us -> 12.7 us  [exchange(): lax.all_to_all(values, CHIPS, 0, 0, axis_index_groups=groups, tiled=True)]
    ppermute x18, waiting for transfers between devices: 46.8 us -> 56.2 us  [z_shift(): return lax.ppermute(values, ('zl', 'zh'), pairs(('zl', 'zh'), move))]
  transfers between devices with their start and end apart: 46 -> 51, of which waited for: 27 -> 25; matrix products, arithmetic and copies ran while one was open for 8% -> 2% of each run, Pallas kernels for 10% -> 21%
where the time goes in v3:
time: 431 us; the launch traced here: 428 us
  waiting for transfers between devices  139 us (32%)
  starting transfers between devices  120 us (28%)
  Pallas kernels  109 us (25%)
  local copies, waits for them, and re-layouts  41.5 us (10%)
  between operations  16.2 us (4%)
    pallas_call x37, Pallas kernels, run(): pl.pallas_call(kernel, grid=grid, in_specs=ins, out_specs=[o[1] for o in...  109 us
    ppermute x18, waiting for transfers between devices, z_shift(): return lax.ppermute(values, ('zl', 'zh'), pairs(('zl', 'zh'), move))  56.2 us
    unnamed x128, local copies, waits for them, and re-layouts  34.5 us
    ppermute x6, starting transfers between devices, swap_roles(): lax.ppermute(values, ('c', 'zh'), pairs(('c', 'zh'), lambda p: {'c': p['z...  32.5 us
    ppermute x18, starting transfers between devices, z_shift(): return lax.ppermute(values, ('zl', 'zh'), pairs(('zl', 'zh'), move))  21.6 us
    all_to_all x1, waiting for transfers between devices, body(): lax.all_to_all(jnp.broadcast_to(first[None], (16, 64, cols)), ('x', 'y'),...  20.1 us
    ppermute x6, waiting for transfers between devices, swap_roles(): lax.ppermute(values, ('c', 'zh'), pairs(('c', 'zh'), lambda p: {'c': p['z...  19.6 us
    all_to_all x2, waiting for transfers between devices, scan_parts(): return lax.all_to_all(fresh.reshape(32, 16, DV), SPANS, 0, 0, tiled=True)  13.4 us
  transfers between devices with their start and end apart: 51, of which 25 were waited for; matrix products, arithmetic and copies ran while one was open for 2% of the time, Pallas kernels for 21%

profile of v3, /device:TPU:1, one launch (start us, length us, event | category | flops | bytes accessed | tf_op | source)
XLA Modules:
  0.0 428.4 jit_solution(18303875450155349794)
XLA Ops:
  10.7 6.9 %collective-permute-start = (bf16[64,6272]{1,0:T(8,128)(2,1)}, bf16[64,6272]{1,0:T(8,128)(2,1)S(1)}, u32[]{:S(2)}, u32[]{:S(2)}) collective-permute-start(bf16[64,6272]{1,0:T(8,128)(2,1)} %shard_map.237), channel_id=1, source_target_pairs={{0,0},{4,32},{32,4},{36,36},{1,1},{5,33},{33,5},{37,37},{2,2},{6,3... | collective-permute-start | bytes 2408456 | tf_op jit(solution)/shard_map/ppermute | solution.py:48
  17.6 10.0 %collective-permute-done = bf16[64,6272]{1,0:T(8,128)(2,1)S(1)} collective-permute-done((bf16[64,6272]{1,0:T(8,128)(2,1)}, bf16[64,6272]{1,0:T(8,128)(2,1)S(1)}, u32[]{:S(2)}, u32[]{:S(2)}) %collective-permute-start) | collective-permute-done | bytes 802848 | tf_op jit(solution)/shard_map/ppermute | solution.py:48
  30.7 6.9 %all-to-all-start = ((bf16[16,64,1664]{2,1,0:T(8,128)(2,1)}), bf16[16,64,1664]{2,1,0:T(8,128)(2,1)}, u32[]{:S(2)}, u32[]{:S(2)}) async-start(bf16[16,64,1664]{2,1,0:T(8,128)(2,1)} %broadcast_in_dim.4), calls=%async_computation | async-start | bytes 6815744 | tf_op jit(solution)/shard_map/all_to_all | solution.py:1009
  37.7 5.4 %collective-permute-start.1 = (bf16[256,2048]{1,0:T(8,128)(2,1)S(1)}, bf16[256,2048]{1,0:T(8,128)(2,1)S(1)}, u32[]{:S(2)}, u32[]{:S(2)}) collective-permute-start(bf16[256,2048]{1,0:T(8,128)(2,1)S(1)} %copy-done.62), channel_id=1, source_target_pairs={{0,0},{4,32},{32,4},{36,36},{1,1},{5,33},{33,5},{37,37},{2,2},{6,3... | collective-permute-start | bytes 3145736 | tf_op jit(solution)/shard_map/ppermute | solution.py:48
  46.4 9.6 %collective-permute-done.1.values = bf16[256,2048]{1,0:T(8,128)(2,1)S(1)} collective-permute-done((bf16[256,2048]{1,0:T(8,128)(2,1)S(1)}, bf16[256,2048]{1,0:T(8,128)(2,1)S(1)}, u32[]{:S(2)}, u32[]{:S(2)}) %collective-permute-start.1) | collective-permute-done | bytes 1048608 | tf_op jit(solution)/shard_map/ppermute | solution.py:48
  57.6 20.1 %all-to-all-done = bf16[16,64,1664]{2,1,0:T(8,128)(2,1)} async-done(((bf16[16,64,1664]{2,1,0:T(8,128)(2,1)}), bf16[16,64,1664]{2,1,0:T(8,128)(2,1)}, u32[]{:S(2)}, u32[]{:S(2)}) %all-to-all-start) | async-done | bytes 3407904 | tf_op jit(solution)/shard_map/all_to_all | solution.py:1009
  77.7 6.4 %collective-permute-done.3.gains_other.key_other.value_other.w_other = bf16[1024,1664]{1,0:T(8,128)(2,1)} collective-permute-done((bf16[1024,1664]{1,0:T(8,128)(2,1)}, bf16[1024,1664]{1,0:T(8,128)(2,1)}, u32[]{:S(2)}, u32[]{:S(2)}) %collective-permute-start.3) | collective-permute-done | bytes 3407904 | tf_op jit(solution)/shard_map/ppermute | solution.py:81
  88.5 5.6 %shard_map.240 = (bf16[256,512]{1,0:T(8,128)(2,1)}, bf16[256,1024]{1,0:T(8,128)(2,1)}, bf16[512,512]{1,0:T(8,128)(2,1)}) custom-call(f32[2]{0:T(128)} %copy-done.47, s32[4]{0:T(128)} %copy-done.43, bf16[256,1024]{1,0:T(8,128)(2,1)} %get-tuple-element.118.own, bf16[256,1024]{1,0:T(8,128)(2,1)} %get-tuple-element.119.other, ...), custom_call_target="tpu_custom_call" | custom-call | flops 1 | bytes 1 | tf_op jit(solution)/shard_map/pallas_call | solution.py:143
  99.3 6.4 %all-to-all-start.1 = ((bf16[32,16,512]{2,1,0:T(8,128)(2,1)}), bf16[32,16,512]{2,1,0:T(8,128)(2,1)S(1)}, u32[]{:S(2)}, u32[]{:S(2)}) async-start(bf16[32,16,512]{2,1,0:T(8,128)(2,1)} %bitcast.43), calls=%async_computation.1 | async-start | bytes 1048576 | tf_op jit(solution)/shard_map/all_to_all | solution.py:131
  107.6 13.4 %all-to-all-done.1.parts = bf16[32,16,512]{2,1,0:T(8,128)(2,1)S(1)} async-done(((bf16[32,16,512]{2,1,0:T(8,128)(2,1)}), bf16[32,16,512]{2,1,0:T(8,128)(2,1)S(1)}, u32[]{:S(2)}, u32[]{:S(2)}) %all-to-all-start.1) | async-done | bytes 524320 | tf_op jit(solution)/shard_map/all_to_all | solution.py:131
  122.6 12.8 %all-gather.2.cloned.1.call-done.w_query.w_gate.w_out.w_down.w_up = bf16[2048,4608]{1,0:T(8,128)(2,1)} async-done(((bf16[64,4608]{1,0:T(8,128)(2,1)}), bf16[2048,4608]{1,0:T(8,128)(2,1)}) %all-gather.2.cloned.1.call-update) | async-done | bytes 18874384 | tf_op jit(solution)/shard_map/all_gather | solution.py:1012
  140.8 6.4 %shard_map.243 = (bf16[256,512]{1,0:T(8,128)(2,1)}, f32[256,1024]{1,0:T(8,128)}, bf16[2,256,256]{2,1,0:T(8,128)(2,1)}, f32[256,1024]{1,0:T(8,128)}) custom-call(f32[2]{0:T(128)} %copy-done.47, s32[4]{0:T(128)} %copy-done.43, bf16[256,2048]{1,0:T(8,128)(2,1)} %get-tuple-element.126.normed.left, ...), custom_call_target="tpu_custom_call" | custom-call | flops 1 | bytes 1 | tf_op jit(solution)/shard_map/pallas_call | solution.py:143
  152.6 6.1 %shard_map.244 = (f32[256,1024]{1,0:T(8,128)}, f32[2,256,1]{2,1,0:T(8,128)}, bf16[256,1024]{1,0:T(8,128)(2,1)}, f32[64,2048]{1,0:T(8,128)}, bf16[64,2048]{1,0:T(...) custom-call(f32[2]{0:T(128)} %copy-done.47, s32[4]{0:T(128)} %copy-done.43, ...), custom_call_target="tpu_custom_call" | custom-call | flops 1 | bytes 1 | tf_op jit(solution)/shard_map/pallas_call | solution.py:143
  167.0 6.8 %collective-permute-done.7.three = bf16[64,2048]{1,0:T(8,128)(2,1)S(1)} collective-permute-done((bf16[64,2048]{1,0:T(8,128)(2,1)}, bf16[64,2048]{1,0:T(8,128)(2,1)S(1)}, u32[]{:S(2)}, u32[]{:S(2)}) %collective-permute-start.7) | collective-permute-done | bytes 262176 | tf_op jit(solution)/shard_map/ppermute | solution.py:58
  195.9 6.6 %shard_map.248 = bf16[2048,2048]{1,0:T(8,128)(2,1)} custom-call(bf16[256,2048]{1,0:T(8,128)(2,1)S(1)} %get-tuple-element.143.left_one, bf16[256,1024]{1,0:T(8,128)(2,1)S(1)} %get-tuple-element.144.right_one, bf16[256,2048]{1,0:T(8,128)(2,1)S(1)} %shard_map.242.out_grad.left_two, bf16[256,1024]{1,0:T(8,128)(2,1)S(1)} %get-tuple-element.172.right_two.hidden), custom_call_target="tpu_custom_call" | custom-call | flops 2147483648 | bytes 33554432 | tf_op jit(solution)/shard_map/pallas_call | solution.py:143
  213.0 6.6 %collective-permute-done.13.three = bf16[64,2048]{1,0:T(8,128)(2,1)S(1)} collective-permute-done((bf16[64,2048]{1,0:T(8,128)(2,1)S(1)}, bf16[64,2048]{1,0:T(8,128)(2,1)S(1)}, u32[]{:S(2)}, u32[]{:S(2)}) %collective-permute-start.13) | collective-permute-done | bytes 262176 | tf_op jit(solution)/shard_map/ppermute | solution.py:58
  223.9 11.2 %collective-permute-done.16.four = bf16[64,2048]{1,0:T(8,128)(2,1)S(1)} collective-permute-done((bf16[64,2048]{1,0:T(8,128)(2,1)S(1)}, bf16[64,2048]{1,0:T(8,128)(2,1)S(1)}, u32[]{:S(2)}, u32[]{:S(2)}) %collective-permute-start.16) | collective-permute-done | bytes 262176 | tf_op jit(solution)/shard_map/ppermute | solution.py:58
  236.3 6.4 %shard_map.250 = (bf16[256,2048]{1,0:T(8,128)(2,1)}, bf16[256,1024]{1,0:T(8,128)(2,1)}, bf16[256,1024]{1,0:T(8,128)(2,1)}, bf16[512,512]{1,0:T(8,128)(2,1)}) custom-call(f32[2]{0:T(128)} %copy-done.47, s32[4]{0:T(128)} %copy-done.43, bf16[64,2048]{1,0:T(8,128)(2,1)} %copy-done.41, bf16[64,2048]{1,0:T(8,128)(2,1)} %copy-done.61, bf16[64,2048]{1,0:T(8,128)(2,1)} %copy-done.60, ...), custom_call_target="tpu_custom_call" | custom-call | flops 1 | bytes 1 | tf_op jit(solution)/shard_map/pallas_call | solution.py:143
  242.7 6.1 %all-to-all-start.3 = ((bf16[32,16,512]{2,1,0:T(8,128)(2,1)}), bf16[32,16,512]{2,1,0:T(8,128)(2,1)}, u32[]{:S(2)}, u32[]{:S(2)}) async-start(bf16[32,16,512]{2,1,0:T(8,128)(2,1)} %bitcast.42), calls=%async_computation.3 | async-start | bytes 1048576 | tf_op jit(solution)/shard_map/all_to_all | solution.py:131
  269.9 7.4 %all-to-all-start.4 = ((bf16[32,16,512]{2,1,0:T(8,128)(2,1)}), bf16[32,16,512]{2,1,0:T(8,128)(2,1)S(1)}, u32[]{:S(2)}, u32[]{:S(2)}) async-start(bf16[32,16,512]{2,1,0:T(8,128)(2,1)} %shard_map.255), calls=%async_computation.4 | async-start | bytes 1048576 | tf_op jit(solution)/shard_map/all_to_all | solution.py:135
  290.7 6.4 %shard_map.254 = bf16[1024,2560]{1,0:T(8,128)(2,1)} custom-call(bf16[1024,1536]{1,0:T(8,128)(2,1)} %copy-done.12, bf16[1024,1536]{1,0:T(8,128)(2,1)} %collective-permute-done.17.refs_1_, bf16[1024,1024]{1,0:T(8,128)(2,1)S(1)} %copy-done.18, bf16[1024,1024]{1,0:T(8,128)(2,1)} %collective-permute-done.18.refs_3_), custom_call_target="tpu_custom_call" | custom-call | flops 1 | bytes 1 | tf_op jit(solution)/shard_map/pallas_call | solution.py:143
  315.4 5.5 %shard_map.260 = (f32[64,2048]{1,0:T(8,128)S(1)}, bf16[64,2048]{1,0:T(8,128)(2,1)S(1)}, bf16[64,2048]{1,0:T(8,128)(2,1)S(1)}, bf16[64,2048]{1,0:T(8,128)(2,1)S(1)}, f32[2,2048]{1,0:T(2,128)S(1)}) custom-call(s32[4]{0:T(128)S(1)} %copy-done.46, f32[256,2048]{1,0:T(8,128)S(1)} %copy-done.3, bf16[256,1536]{1,0:T(8,128)(2,1)S(1)} %copy-done.5, ...), custom_call_target="tpu_custom_call" | custom-call | flops 1 | bytes 1 | tf_op jit(solution)/shard_map/pallas_call | solution.py:143
  359.2 6.6 %collective-permute-done.21.three = bf16[64,2048]{1,0:T(8,128)(2,1)S(1)} collective-permute-done((bf16[64,2048]{1,0:T(8,128)(2,1)}, bf16[64,2048]{1,0:T(8,128)(2,1)S(1)}, u32[]{:S(2)}, u32[]{:S(2)}) %collective-permute-start.21) | collective-permute-done | bytes 262176 | tf_op jit(solution)/shard_map/ppermute | solution.py:58
  397.4 8.1 %collective-permute-start.39 = (bf16[64,4096]{1,0:T(8,128)(2,1)}, bf16[64,4096]{1,0:T(8,128)(2,1)S(1)}, u32[]{:S(2)}, u32[]{:S(2)}) collective-permute-start(bf16[64,4096]{1,0:T(8,128)(2,1)} %get-tuple-element.206), channel_id=1, source_target_pairs={{0,0},{4,32},{32,4},{36,36},{1,1},{5,33},{33,5},{37,37},{2,2},{6,3... | collective-permute-start | bytes 1572872 | tf_op jit(solution)/shard_map/ppermute | solution.py:48
  (262 shorter events, 218.6 us)
Async XLA Ops:
  7.2 128.2 %all-gather.2.cloned.1.call-start = ((), (), s32[]{:S(2)}) async-start(), calls=%async_computation.9 | async-start | bytes 19464192 | tf_op jit(solution)/shard_map/all_gather | solution.py:1012
  10.7 16.9 %collective-permute-start = (bf16[64,6272]{1,0:T(8,128)(2,1)}, bf16[64,6272]{1,0:T(8,128)(2,1)S(1)}, u32[]{:S(2)}, u32[]{:S(2)}) collective-permute-start(bf16[64,6272]{1,0:T(8,128)(2,1)} %shard_map.237), channel_id=1, source_target_pairs={{0,0},{4,32},{32,4},{36,36},{1,1},{5,33},{33,5},{37,37},{2,2},{6,3... | collective-permute-start | bytes 2408456 | tf_op jit(solution)/shard_map/ppermute | solution.py:48
  30.7 47.0 %all-to-all-start = ((bf16[16,64,1664]{2,1,0:T(8,128)(2,1)}), bf16[16,64,1664]{2,1,0:T(8,128)(2,1)}, u32[]{:S(2)}, u32[]{:S(2)}) async-start(bf16[16,64,1664]{2,1,0:T(8,128)(2,1)} %broadcast_in_dim.4), calls=%async_computation | async-start | bytes 6815744 | tf_op jit(solution)/shard_map/all_to_all | solution.py:1009
  37.7 18.3 %collective-permute-start.1 = (bf16[256,2048]{1,0:T(8,128)(2,1)S(1)}, bf16[256,2048]{1,0:T(8,128)(2,1)S(1)}, u32[]{:S(2)}, u32[]{:S(2)}) collective-permute-start(bf16[256,2048]{1,0:T(8,128)(2,1)S(1)} %copy-done.62), channel_id=1, source_target_pairs={{0,0},{4,32},{32,4},{36,36},{1,1},{5,33},{33,5},{37,37},{2,2},{6,3... | collective-permute-start | bytes 3145736 | tf_op jit(solution)/shard_map/ppermute | solution.py:48
  43.1 14.5 %collective-permute-start.2 = (f32[2]{0:T(128)S(1)}, f32[2]{0:T(128)S(1)}, u32[]{:S(2)}, u32[]{:S(2)}) collective-permute-start(f32[2]{0:T(128)S(1)} %copy-done.63), channel_id=1, source_target_pairs={{0,0},{4,32},{32,4},{36,36},{1,1},{5,33},{33,5},{37,37},{2,2},{6,3... | collective-permute-start | bytes 32 | tf_op jit(solution)/shard_map/ppermute | solution.py:48
  94.1 27.9 %collective-permute-start.4 = (bf16[256,2048]{1,0:T(8,128)(2,1)}, bf16[256,2048]{1,0:T(8,128)(2,1)S(1)}, u32[]{:S(2)}, u32[]{:S(2)}) collective-permute-start(bf16[256,2048]{1,0:T(8,128)(2,1)} %param.27), channel_id=1, source_target_pairs={{0,0},{4,32},{32,4},{36,36},{1,1},{5,33},{33,5},{37,37},{2,2},{6,3... | collective-permute-start | bytes 3145736 | tf_op jit(solution)/shard_map/ppermute | solution.py:48
  99.3 21.7 %all-to-all-start.1 = ((bf16[32,16,512]{2,1,0:T(8,128)(2,1)}), bf16[32,16,512]{2,1,0:T(8,128)(2,1)S(1)}, u32[]{:S(2)}, u32[]{:S(2)}) async-start(bf16[32,16,512]{2,1,0:T(8,128)(2,1)} %bitcast.43), calls=%async_computation.1 | async-start | bytes 1048576 | tf_op jit(solution)/shard_map/all_to_all | solution.py:131
  135.4 16.4 %all-to-all-start.2 = ((bf16[32,16,512]{2,1,0:T(8,128)(2,1)}), bf16[32,16,512]{2,1,0:T(8,128)(2,1)S(1)}, u32[]{:S(2)}, u32[]{:S(2)}) async-start(bf16[32,16,512]{2,1,0:T(8,128)(2,1)} %shard_map.241), calls=%async_computation.2 | async-start | bytes 1048576 | tf_op jit(solution)/shard_map/all_to_all | solution.py:135
  140.8 264.7 %reduce-scatter.2.cloned.1.call-start = ((), (), s32[]{:S(2)}) async-start(), calls=%async_computation.10 | async-start | bytes 8650752 | tf_op jit(solution)/shard_map/reduce_scatter | solution.py:1048
  242.7 24.8 %all-to-all-start.3 = ((bf16[32,16,512]{2,1,0:T(8,128)(2,1)}), bf16[32,16,512]{2,1,0:T(8,128)(2,1)}, u32[]{:S(2)}, u32[]{:S(2)}) async-start(bf16[32,16,512]{2,1,0:T(8,128)(2,1)} %bitcast.42), calls=%async_computation.3 | async-start | bytes 1048576 | tf_op jit(solution)/shard_map/all_to_all | solution.py:131
  267.5 23.2 %collective-permute-start.17 = (bf16[1024,1536]{1,0:T(8,128)(2,1)}, bf16[1024,1536]{1,0:T(8,128)(2,1)}, u32[]{:S(2)}, u32[]{:S(2)}) collective-permute-start(bf16[1024,1536]{1,0:T(8,128)(2,1)} %get-tuple-element.168), channel_id=1, source_target_pairs={{0,32},{32,0},{1,33},{33,1},{2,34},{34,2},{3,35},{35,3},{4,36},{36... | collective-permute-start | bytes 9437192 | tf_op jit(solution)/shard_map/ppermute | solution.py:81
  267.8 22.9 %collective-permute-start.18 = (bf16[1024,1024]{1,0:T(8,128)(2,1)}, bf16[1024,1024]{1,0:T(8,128)(2,1)}, u32[]{:S(2)}, u32[]{:S(2)}) collective-permute-start(bf16[1024,1024]{1,0:T(8,128)(2,1)} %copy-done.50), channel_id=1, source_target_pairs={{0,32},{32,0},{1,33},{33,1},{2,34},{34,2},{3,35},{35,3},{4,36},{36... | collective-permute-start | bytes 6291464 | tf_op jit(solution)/shard_map/ppermute | solution.py:81
  269.9 27.2 %all-to-all-start.4 = ((bf16[32,16,512]{2,1,0:T(8,128)(2,1)}), bf16[32,16,512]{2,1,0:T(8,128)(2,1)S(1)}, u32[]{:S(2)}, u32[]{:S(2)}) async-start(bf16[32,16,512]{2,1,0:T(8,128)(2,1)} %shard_map.255), calls=%async_computation.4 | async-start | bytes 1048576 | tf_op jit(solution)/shard_map/all_to_all | solution.py:135
  298.0 37.8 %all-to-all-start.5 = ((bf16[4,256,2560]{2,1,0:T(8,128)(2,1)}), bf16[4,256,2560]{2,1,0:T(8,128)(2,1)}, u32[]{:S(2)}, u32[]{:S(2)}) async-start(bf16[4,256,2560]{2,1,0:T(8,128)(2,1)} %bitcast.39), calls=%async_computation.5 | async-start | bytes 10485760 | tf_op jit(solution)/shard_map/all_to_all | solution.py:139
  312.4 14.3 %collective-permute-start.22 = (bf16[1024,1536]{1,0:T(8,128)(2,1)}, bf16[1024,1536]{1,0:T(8,128)(2,1)S(1)}, u32[]{:S(2)}, u32[]{:S(2)}) collective-permute-start(bf16[1024,1536]{1,0:T(8,128)(2,1)} %get-tuple-element.189), channel_id=1, source_target_pairs={{0,32},{32,0},{1,33},{33,1},{2,34},{34,2},{3,35},{35,3},{4,36},{36... | collective-permute-start | bytes 9437192 | tf_op jit(solution)/shard_map/ppermute | solution.py:81
  335.8 31.0 %all-to-all-start.6 = ((bf16[4,256,1664]{2,1,0:T(8,128)(2,1)}), bf16[4,256,1664]{2,1,0:T(8,128)(2,1)S(1)}, u32[]{:S(2)}, u32[]{:S(2)}) async-start(bf16[4,256,1664]{2,1,0:T(8,128)(2,1)} %bitcast.40), calls=%async_computation.6 | async-start | bytes 6815744 | tf_op jit(solution)/shard_map/all_to_all | solution.py:139
  343.2 16.0 %collective-permute-start.19 = (bf16[64,2048]{1,0:T(8,128)(2,1)}, bf16[64,2048]{1,0:T(8,128)(2,1)S(1)}, u32[]{:S(2)}, u32[]{:S(2)}) collective-permute-start(bf16[64,2048]{1,0:T(8,128)(2,1)} %copy-done.56), channel_id=1, source_target_pairs={{0,64},{4,68},{64,4},{68,0},{1,65},{5,69},{65,5},{69,1},{2,66},{6,... | collective-permute-start | bytes 786440 | tf_op jit(solution)/shard_map/ppermute | solution.py:58
  344.0 15.1 %collective-permute-start.20 = (bf16[64,2048]{1,0:T(8,128)(2,1)}, bf16[64,2048]{1,0:T(8,128)(2,1)S(1)}, u32[]{:S(2)}, u32[]{:S(2)}) collective-permute-start(bf16[64,2048]{1,0:T(8,128)(2,1)} %copy-done.55), channel_id=1, source_target_pairs={{0,68},{4,64},{64,0},{68,4},{1,69},{5,65},{65,1},{69,5},{2,70},{6,... | collective-permute-start | bytes 786440 | tf_op jit(solution)/shard_map/ppermute | solution.py:58
  347.9 17.8 %collective-permute-start.21 = (bf16[64,2048]{1,0:T(8,128)(2,1)}, bf16[64,2048]{1,0:T(8,128)(2,1)S(1)}, u32[]{:S(2)}, u32[]{:S(2)}) collective-permute-start(bf16[64,2048]{1,0:T(8,128)(2,1)} %copy-done.54), channel_id=1, source_target_pairs={{0,4},{4,0},{64,68},{68,64},{1,5},{5,1},{65,69},{69,65},{2,6},{6,2... | collective-permute-start | bytes 786440 | tf_op jit(solution)/shard_map/ppermute | solution.py:58
  371.8 24.4 %all-to-all-start.7 = ((bf16[4,64,4224]{2,1,0:T(8,128)(2,1)}), bf16[4,64,4224]{2,1,0:T(8,128)(2,1)S(1)}, u32[]{:S(2)}, u32[]{:S(2)}) async-start(bf16[4,64,4224]{2,1,0:T(8,128)(2,1)} %bitcast.36), calls=%async_computation.7 | async-start | bytes 4325376 | tf_op jit(solution)/shard_map/all_to_all | solution.py:139
  390.4 20.2 %collective-permute-start.34 = (bf16[256,2048]{1,0:T(8,128)(2,1)S(1)}, bf16[256,2048]{1,0:T(8,128)(2,1)}, u32[]{:S(2)}, u32[]{:S(2)}) collective-permute-start(bf16[256,2048]{1,0:T(8,128)(2,1)S(1)} %shard_map.267.mine), channel_id=1, source_target_pairs={{0,32},{36,4},{1,33},{37,5},{2,34},{38,6},{3,35},{39,7},{8,40},{44... | collective-permute-start | bytes 3145736 | tf_op jit(solution)/shard_map/ppermute | solution.py:77
  395.0 16.3 %collective-permute-start.30 = (bf16[256,2048]{1,0:T(8,128)(2,1)}, bf16[256,2048]{1,0:T(8,128)(2,1)}, u32[]{:S(2)}, u32[]{:S(2)}) collective-permute-start(bf16[256,2048]{1,0:T(8,128)(2,1)} %shard_map.265.mine), channel_id=1, source_target_pairs={{0,32},{36,4},{1,33},{37,5},{2,34},{38,6},{3,35},{39,7},{8,40},{44... | collective-permute-start | bytes 3145736 | tf_op jit(solution)/shard_map/ppermute | solution.py:77
  397.4 22.3 %collective-permute-start.39 = (bf16[64,4096]{1,0:T(8,128)(2,1)}, bf16[64,4096]{1,0:T(8,128)(2,1)S(1)}, u32[]{:S(2)}, u32[]{:S(2)}) collective-permute-start(bf16[64,4096]{1,0:T(8,128)(2,1)} %get-tuple-element.206), channel_id=1, source_target_pairs={{0,0},{4,32},{32,4},{36,36},{1,1},{5,33},{33,5},{37,37},{2,2},{6,3... | collective-permute-start | bytes 1572872 | tf_op jit(solution)/shard_map/ppermute | solution.py:48
  405.5 15.2 %collective-permute-start.40 = (bf16[64,2048]{1,0:T(8,128)(2,1)}, bf16[64,2048]{1,0:T(8,128)(2,1)S(1)}, u32[]{:S(2)}, u32[]{:S(2)}) collective-permute-start(bf16[64,2048]{1,0:T(8,128)(2,1)} %reduce-scatter.2.cloned.1.call-done), channel_id=1, source_target_pairs={{0,0},{4,32},{32,4},{36,36},{1,1},{5,33},{33,5},{37,37},{2,2},{6,3... | collective-permute-start | bytes 786440 | tf_op jit(solution)/shard_map/ppermute | solution.py:48
  (91 other events, 711.8 us)
Sparse Core Ops, SparseCore 0:
  28.7 106.6 all-gather.1
  203.5 92.9 reduce-scatter.1

commit v4 on v3

--- a/solution.py
+++ b/solution.py
@@ -89,17 +89,10 @@
     return [values, z_shift(values, 3), z_shift(values, 2), z_shift(values, 1)]
 
 
-def z_gather_home(values, place, home, dtype):
+def z_gather_home(values, place, home):
     near, far, across = z_shift_home(values, 3), z_shift_home(values, 1), z_shift_home(values, 2)
     full = in_place(place, values, near, across, far)
-    return chosen(home, full, core_from_home(full), dtype)
-
-
-def to_owner(values, flip_z, flip_core):
-    def move(place):
-        return {"zl": place["zl"] ^ flip_z, "zh": place["c"], "c": place["zh"] ^ flip_core}
-
-    return lax.ppermute(values, ("zl", "c", "zh"), pairs(("zl", "c", "zh"), move))
+    return chosen(home, full, core_from_home(full))
 
 
 def nn(left, right):
@@ -201,31 +194,33 @@
     return run(
         in_place_kernel,
         (1,),
-        [SCALARS] + [whole((64, 2048))] * 4,
-        [(shape((256, 2048), BF), whole((256, 2048)))],
+        [SCALARS] + [whole((64, 4096))] * 4,
+        [(shape((256, 4096), BF), whole((256, 4096)))],
         [place, *pieces],
     )[0]
 
 
-def chosen_kernel(home, mine, other, out):
-    @pl.when(home[0] == 1)
-    def here():
-        out[...] = mine[...].astype(out.dtype)
-
-    @pl.when(home[0] == 0)
-    def there():
-        out[...] = other[...].astype(out.dtype)
-
-
-def chosen(home, mine, other, dtype):
-    block = pl.BlockSpec((128, 2048), lambda i: (i, 0))
+def chosen_kernel(home, mine, other, block_out, tokens_grad):
+    for flag, ref in ((1, mine), (0, other)):
+
+        @pl.when(home[0] == flag)
+        def take(ref=ref):
+            block_out[...] = ref[:, :2048]
+            tokens_grad[...] = ref[:, 2048:].astype(F32)
+
+
+def chosen(home, mine, other):
+    def block(cols):
+        return pl.BlockSpec((64, cols), lambda i: (i, 0))
+
     return run(
         chosen_kernel,
-        (2,),
-        [SCALARS, block, block],
-        [(shape((256, 2048), dtype), block)],
+        (4,),
+        [SCALARS, block(4096), block(4096)],
+        [(shape((256, 2048), BF), block(2048)), (shape((256, 2048), F32), block(2048))],
         [home, mine, other],
-    )[0]
+        limit=61,
+    )
 
 
 def scan_kernel(reverse, rate, parts, out):
@@ -278,38 +273,23 @@
     )[0]
 
 
-def norm_kernel(place, tokens, gains_own, gains_other, normed, own, other, hat, scale, gains):
-    values = tokens[...].astype(F32)
-    made, spread = norm_parts(values)
+def norm_kernel(tokens, hat, scale):
+    made, spread = norm_parts(tokens[...].astype(F32))
+    hat[...] = made
     scale[...] = spread
-    hat[...] = made
-    mine = gains_own[...].astype(F32).T
-    yours = gains_other[...].astype(F32).T
-    for i in range(4):
-        for ref, rows, side in ((own, mine, place[1]), (other, yours, 1 - place[1])):
-            at = pl.multiple_of((2 * i + side) * 256, 256)
-            rows = rows[:8, i * 256 : i * 256 + 256]
-            gains[:, pl.ds(at, 256)] = rows
-            out = (hat[:, pl.ds(at, 256)] * rows[0:1] + rows[1:2]).astype(BF)
-            normed[:, pl.ds(at, 256)] = out
-            ref[:, i * 256 : i * 256 + 256] = out
-
-
-def norm_first(place, tokens, early, early_other):
-    gains = pl.BlockSpec((1024, 128), lambda h: (0, 12))
+
+
+def norm_tokens(tokens):
+    block = pl.BlockSpec((64, 2048), lambda i: (i, 0))
     return run(
         norm_kernel,
-        (1,),
-        [SCALARS, whole((256, 2048)), gains, gains],
-        [
-            (shape((256, 2048), BF), whole((256, 2048))),
-            (shape((256, 1024), BF), whole((256, 1024))),
-            (shape((256, 1024), BF), whole((256, 1024))),
-            (shape((256, 2048), F32), whole((256, 2048)), "hbm"),
-            (shape((256, 1), F32), whole((256, 1))),
-            (shape((8, 2048), F32), whole((8, 2048))),
-        ],
-        [place, tokens, early, early_other],
+        (4,),
+        [block],
+        [
+            (shape((256, 2048), F32), block, "hbm"),
+            (shape((256, 1), F32), pl.BlockSpec((64, 1), lambda i: (i, 0)), "hbm"),
+        ],
+        [tokens],
         limit=61,
     )
 
@@ -415,39 +395,57 @@
     )
 
 
-def out_kernel(resid, mine, one, two, three, out):
-    out[...] = (resid[...] + collected(mine, (one, two, three))).astype(BF)
-
-
-def block_rows(resid, mine, others):
-    return run(
-        out_kernel,
+def rows_kernel(resid, f0, f1, f2, f3, d_resid, d0, d1, d2, d3, gains, hat, scale, out):
+    out[:, :2048] = (resid[...] + collected(f0, (f1, f2, f3))).astype(BF)
+    total = collected(d0, (d1, d2, d3))
+    made = d_resid[...] + norm_back(total * gains[0:1], hat[...], scale[...])
+    out[:, 2048:] = made.astype(BF)
+
+
+def final_rows(resid, ffn, ffn_others, d_resid, mine, others, gains, hat, scale):
+    return run(
+        rows_kernel,
         (1,),
-        [ROWS] * 5,
-        [(shape((64, 2048), BF), ROWS)],
-        [resid, mine, *others],
+        [ROWS] * 10 + [whole((8, 2048)), ROWS, pl.BlockSpec((64, 1), lambda h: (0, 0))],
+        [(shape((64, 4096), BF), whole((64, 4096)))],
+        [resid, ffn, *ffn_others, d_resid, mine, *others, gains, hat, scale],
+        limit=61,
     )[0]
 
 
-def tokens_kernel(d_resid, mine, one, two, three, gains, hat, scale, out):
-    total = collected(mine, (one, two, three))
-    made = d_resid[...] + norm_back(total * gains[0:1], hat[...], scale[...])
-    out[...] = made.astype(BF)
-
-
-def tokens_back(d_resid, mine, others, gains, hat, scale):
-    return run(
-        tokens_kernel,
-        (1,),
-        [ROWS] * 5 + [whole((8, 2048)), ROWS, whole((64, 1))],
-        [(shape((64, 2048), BF), ROWS)],
-        [d_resid, mine, *others, gains, hat, scale],
-    )[0]
-
-
 def kv_kernel(
-    rate, place, own, other, key_own, key_other, value_own, value_other, cosine, sine, key, value, fresh
+    rate,
+    place,
+    hat,
+    gains_own,
+    gains_other,
+    key_own,
+    key_other,
+    value_own,
+    value_other,
+    cosine,
+    sine,
+    key,
+    value,
+    fresh,
+    normed,
+    gains,
+    own,
+    other,
 ):
+    @pl.when(pl.program_id(0) == 0)
+    def norm():
+        mine = gains_own[...].astype(F32).T
+        yours = gains_other[...].astype(F32).T
+        for i in range(4):
+            for ref, rows, side in ((own, mine, place[1]), (other, yours, 1 - place[1])):
+                at = pl.multiple_of((2 * i + side) * 256, 256)
+                rows = rows[:8, i * 256 : i * 256 + 256]
+                gains[:, pl.ds(at, 256)] = rows
+                out = (hat[:, pl.ds(at, 256)] * rows[0:1] + rows[1:2]).astype(BF)
+                normed[:, pl.ds(at, 256)] = out
+                ref[:, i * 256 : i * 256 + 256] = out
+
     qdec, kdec = decays(rate[pl.program_id(0)], place[0])
     raw = nn(own[...], key_own[...]) + nn(other[...], key_other[...])
     turn_into(key, raw, cosine[...], sine[...])
@@ -456,15 +454,17 @@
     fresh[...] = tn((kdec * key[...].astype(F32)).astype(BF), made).astype(BF)
 
 
-def key_value(rate, place, own, other, early, early_other, cosine, sine):
+def key_value(rate, place, hat, early, early_other, cosine, sine):
+    gains = pl.BlockSpec((1024, 128), lambda h: (0, 12))
     return run(
         kv_kernel,
         (2,),
         [
             SCALARS,
             SCALARS,
-            whole((256, 1024)),
-            whole((256, 1024)),
+            whole((256, 2048)),
+            gains,
+            gains,
             columns(1024, 256),
             columns(1024, 256),
             columns(1024, 512, 1),
@@ -476,8 +476,23 @@
             (shape((256, 512), BF), columns(256, 256)),
             (shape((256, 1024), BF), columns(256, 512)),
             (shape((512, 512), BF), pl.BlockSpec((256, 512), lambda h: (h, 0))),
-        ],
-        [rate, place, own, other, early, early_other, early, early_other, cosine, sine],
+            (shape((256, 2048), BF), whole((256, 2048))),
+            (shape((8, 2048), F32), whole((8, 2048))),
+        ],
+        [
+            rate,
+            place,
+            hat,
+            early,
+            early_other,
+            early,
+            early_other,
+            early,
+            early_other,
+            cosine,
+            sine,
+        ],
+        [pltpu.VMEM((256, 1024), BF), pltpu.VMEM((256, 1024), BF)],
         limit=61,
     )
 
@@ -502,7 +517,7 @@
             SCALARS,
             SCALARS,
             whole((256, 2048)),
-            columns(2048, 256, 16),
+            columns(2048, 256, 12),
             columns(2048, 512),
             columns(256, 256),
             columns(256, 512),
@@ -701,6 +716,7 @@
             (shape((256, 1024), F32), columns(256, 512)),
         ],
         [rate, place, d_ret, value, key, query, probs, state, cosine, sine],
+        limit=61,
     )
 
 
@@ -749,7 +765,7 @@
         [
             whole((256, 512)),
             whole((256, 1024)),
-            pl.BlockSpec((512, 512), lambda i: (i, 8)),
+            pl.BlockSpec((512, 512), lambda i: (i, 6)),
             pl.BlockSpec((512, 1024), lambda i: (i, 0)),
         ],
         [(shape((256, 2048), F32), columns(256, 512))],
@@ -818,31 +834,40 @@
     )[0]
 
 
-def down_kernel(out_grad, w_down, d_hidden):
-    d_hidden[...] = nn(out_grad[...], w_down[...])
-
-
-def down_back(out_grad, late):
+def down_kernel(place, out_grad, w_own, w_other, d_hidden):
+    total = jnp.zeros(d_hidden.shape, F32)
+    for w, side in ((w_own, place[1]), (w_other, 1 - place[1])):
+        for i in range(4):
+            at = pl.multiple_of((2 * i + side) * 256, 256)
+            total = total + nn(out_grad[:, pl.ds(at, 256)], w[i * 256 : i * 256 + 256, :])
+    d_hidden[...] = total
+
+
+def down_back(place, out_grad, w_own, w_other):
     return run(
         down_kernel,
         (2,),
-        [whole((256, 2048)), columns(2048, 512, 6)],
+        [SCALARS, whole((256, 2048)), columns(1024, 512), columns(1024, 512)],
         [(shape((256, 1024), F32), columns(256, 512))],
-        [out_grad, late],
+        [place, out_grad, w_own, w_other],
     )[0]
 
 
-def ffn_kernel(hidden, w_down, mine, one, two, three):
-    cut_rows(nt(hidden[...], w_down[...]), (mine, one, two, three))
-
-
-def ffn_parts(hidden, late):
+def ffn_kernel(place, hidden, w_own, w_other, mine, one, two, three):
+    left, right = nt(hidden[...], w_own[...]), nt(hidden[...], w_other[...])
+    low = place[1] == 0
+    total = jnp.concatenate([jnp.where(low, left, right), jnp.where(low, right, left)], axis=1)
+    cut_rows(total, (mine, one, two, three))
+
+
+def ffn_parts(place, hidden, w_own, w_other):
+    weights = pl.BlockSpec((256, 1024), lambda i: (i, 0))
     return run(
         ffn_kernel,
         (4,),
-        [whole((256, 1024)), pl.BlockSpec((512, 1024), lambda i: (i, 3))],
+        [SCALARS, whole((256, 1024)), weights, weights],
         row_parts(512, lambda i: (0, i)),
-        [hidden, late],
+        [place, hidden, w_own, w_other],
     )
 
 
@@ -874,24 +899,26 @@
         [SCALARS, columns(256, 512)] + [whole(r.shape) for r in rights],
         [half, half],
         [place, left, *rights],
-    )
-
-
-def vector_kernel(place, vectors, own, other):
-    for ref, side in ((own, place[1]), (other, 1 - place[1])):
-        rows = vectors[:, pl.ds(pl.multiple_of(side * 256, 256), 256)]
+        limit=61,
+    )
+
+
+def vector_kernel(place, one, two, three, four, own, other):
+    total = one[...] + two[...] + three[...] + four[...]
+    for ref, side in ((own, 0), (other, 1)):
+        rows = jnp.where(place[1] == side, total[:, :256], total[:, 256:])
         rows = jnp.concatenate([rows, jnp.zeros((120, 256), F32)], axis=0)
-        store_rows(ref, rows.T.astype(BF), side, 0)
-
-
-def vector_split(place, vectors):
+        store_rows(ref, rows.T.astype(BF), place[1] if side == 0 else 1 - place[1], 0)
+
+
+def vector_split(place, *vectors):
     half = (shape((1024, 128), BF), whole((1024, 128)))
     return run(
         vector_kernel,
         (4,),
-        [SCALARS, columns(8, 512)],
+        [SCALARS] + [columns(8, 512)] * 4,
         [half, half],
-        [place, vectors],
+        [place, *vectors],
     )
 
 
@@ -919,58 +946,39 @@
     )[0]
 
 
-def last_kernel(parts, main, rest):
+def last_kernel(parts, out):
     total = parts[0].astype(F32)
     for k in range(1, 4):
         total = total + parts[k].astype(F32)
-    cols = main.shape[1]
-    main[...] = total[:, :cols].astype(BF)
-    rest[...] = total[:, cols:]
+    out[...] = total.astype(BF)
 
 
 def last_sum(parts):
-    cols = parts.shape[2] - 128
+    dims = parts.shape[1:]
     return run(
         last_kernel,
         (1,),
         [whole(parts.shape)],
-        [(shape((64, cols), BF), whole((64, cols))), (shape((64, 128), F32), whole((64, 128)))],
+        [(shape(dims, BF), whole(dims))],
         [parts],
-    )
-
-
-def flip_kernel(*refs):
-    total = refs[0][...]
-    for ref in refs[1:-1]:
-        total = total + ref[...]
-    refs[-1][...] = total.T[:8]
-
-
-def flip_sum(*values):
-    return run(
-        flip_kernel,
-        (1,),
-        [whole((64, 128))] * len(values),
-        [(shape((8, 64), F32), whole((8, 64)))],
-        list(values),
     )[0]
 
 
 def widen_kernel(values, *outs):
     start = 0
     for out in outs:
-        out[...] = values[:, start : start + out.shape[1]].astype(F32)
-        start += out.shape[1]
-
-
-def widen(values, widths):
-    return run(
-        widen_kernel,
-        (1,),
-        [whole(values.shape)],
-        [(shape((64, n), F32), whole((64, n))) for n in widths],
-        [values],
-    )
+        if out.shape[0] == 64:
+            out[...] = values[:, start : start + out.shape[1]].astype(F32)
+            start += out.shape[1]
+        else:
+            out[...] = values[:, start : start + 128].astype(F32).T[:8]
+
+
+def widen(values, widths, vectors=False):
+    outs = [(shape((64, n), F32), whole((64, n))) for n in widths]
+    if vectors:
+        outs.append((shape((8, 64), F32), whole((8, 64))))
+    return run(widen_kernel, (1,), [whole(values.shape)], outs, [values])
 
 
 def body(
@@ -998,12 +1006,16 @@
 
     gains = jnp.stack([norm1_gain, norm1_bias, norm2_gain, norm2_bias])
     shards = swap_roles(
-        pack(gains, w_key, w_value, w_gate, w_out.T, w_up, w_down.T, w_query)
+        pack(gains, w_key, w_value, w_gate, w_out.T, w_up, w_query)
     )
     first, second = shards[:, :1664], shards[:, 1664:]
     rate = swap_roles(decay_rate)
     tokens, kept = lax.optimization_barrier((tokens, shards))
     tokens = swap_roles(tokens)
+    third, kept = lax.optimization_barrier((w_down.T, tokens))
+    third = jnp.broadcast_to(swap_roles(third)[None], (16, 64, 1024))
+    out_grad, kept = lax.optimization_barrier((out_grad, tokens))
+    out_grad = swap_roles(out_grad)
 
     cols = first.shape[1]
     early = lax.all_to_all(
@@ -1012,62 +1024,68 @@
     late = lax.all_gather(second, SPANS, axis=0, tiled=True)
 
     tokens = roll_rows(place, tokens)
+    hat1, scale1 = norm_tokens(tokens)
+    out_grad = roll_rows(place, out_grad)
     index = ((jnp.arange(256) + z * 64) % 256).astype(F32)
     half = DK // 2
     position = (span * 256).astype(F32) + index
     freq = 10000.0 ** (-jnp.arange(half).astype(F32) / half)
     angle = position[:, None] * freq[None, :]
     cosine, sine = jnp.cos(angle), jnp.sin(angle)
-    early, tokens, cosine, sine, rate = lax.optimization_barrier(
-        (early, tokens, cosine, sine, rate)
+    early, tokens, hat1, out_grad, third, cosine, sine, rate = lax.optimization_barrier(
+        (early, tokens, hat1, out_grad, third, cosine, sine, rate)
     )
 
     early_other = core_swap(early)
-    normed1, own, other, hat1, scale1, gains = norm_first(place, tokens, early, early_other)
-    key, value, fresh = key_value(rate, place, own, other, early, early_other, cosine, sine)
-    out_grad, fresh = lax.optimization_barrier((out_grad, fresh))
-    out_grad = roll_rows(place, swap_roles(out_grad))
+    key, value, fresh, normed1, gains = key_value(
+        rate, place, hat1, early, early_other, cosine, sine
+    )
     scan_rate = jnp.where(x < 2, rate[0], rate[1]).reshape(1)
     carried = scan_spans(scan_rate, scan_parts(fresh), False)
-    late, carried, out_grad = lax.optimization_barrier((late, carried, out_grad))
     state = scan_back(carried)
     query, gate, probs, inner = query_gate(
         rate, place, normed1, late, key, value, cosine, sine
     )
+    third, state, query = lax.optimization_barrier((third, state, query))
+    down = lax.all_to_all(third, ("x", "y"), 0, 0, tiled=True).reshape(1024, 1024)
     hat, scale, mixed, mine, *parts = retain(rate, place, query, state, inner, gate, late)
     parts = z_collect(parts)
-    out_grad, mine = lax.optimization_barrier((out_grad, mine))
-    d_hidden = down_back(out_grad, late)
     resid, hat2, scale2, normed2 = resid_norm(tokens[:64], mine, parts, gains)
+    down, kept = lax.optimization_barrier((down, normed2))
+    down_other = core_swap(down)
+    d_hidden = down_back(place, out_grad, down, down_other)
     normed2, hidden, d_up, mine, *parts = up_back(z_gather(normed2), late, d_hidden)
     parts = z_collect(parts)
     grad_wide = grad_pair(normed2, d_up, out_grad, hidden)
-    mine, grad_wide = lax.optimization_barrier((mine, grad_wide))
+    mine, parts, grad_wide = lax.optimization_barrier((mine, parts, grad_wide))
     d_resid, d_attn, vectors2 = resid_back(out_grad[:64], mine, parts, gains, hat2, scale2)
-    grad_wide = swap_roles(
-        lax.psum_scatter(grad_wide, SPANS, scatter_dimension=0, tiled=True)
-    )
+    grad_wide = lax.psum_scatter(grad_wide, SPANS, scatter_dimension=0, tiled=True)
+    hidden, d_attn = lax.optimization_barrier((hidden, d_attn))
+    ffn, *ffn_others = ffn_parts(place, hidden, down, down_other)
+    pieces = z_gather(d_attn)
+    pieces, ffn, ffn_others = lax.optimization_barrier((pieces, ffn, ffn_others))
     d_attn, d_gate, d_ret, outgoing = mixed_back(
-        rate, place, z_gather(d_attn), late, gate, hat, scale, query
-    )
+        rate, place, pieces, late, gate, hat, scale, query
+    )
+    ffn_others = z_collect(ffn_others)
     parts = scan_parts(outgoing)
 
     d_query, key_part, value_part = query_back(
         rate, place, d_ret, value, key, query, probs, state, cosine, sine
     )
+    out_halves = grad_split(place, d_attn, [mixed])
     gate_halves = grad_split(place, normed1, [d_gate, d_query])
-    out_halves = grad_split(place, d_attn, [mixed])
+    gate_halves, out_halves, ffn_others = lax.optimization_barrier(
+        (gate_halves, out_halves, ffn_others)
+    )
     parts, gate_halves, out_halves = lax.optimization_barrier(
         (parts, gate_halves, out_halves)
     )
     later = scan_back(scan_spans(scan_rate, parts, True))
-    hidden, d_query, parts = lax.optimization_barrier((hidden, d_query, parts))
+    early_part = add_halves(gate_halves, out_halves)
+    d_query, parts = lax.optimization_barrier((d_query, parts))
     d_first = normed_back_first(d_query, d_gate, late)
-    ffn, *ffn_others = ffn_parts(hidden, late)
-    early_part = add_halves(gate_halves, out_halves)
-    early_part, later, ffn, d_first = lax.optimization_barrier(
-        (early_part, later, ffn, d_first)
-    )
+    early_part, later, d_first = lax.optimization_barrier((early_part, later, d_first))
     early_part = exchange(early_part, FIRST_WAY)
 
     d_both = key_value_back(
@@ -1077,29 +1095,25 @@
     d_both, late_halves = lax.optimization_barrier((d_both, late_halves))
     mine, *parts, vectors = normed_back(place, d_first, d_both, early, early_other, hat1)
     vectors = jnp.concatenate([vectors, vectors2, jnp.zeros((4, 2048), F32)])
+    shifted = [z_shift(vectors, shift) for shift in (1, 3, 2)]
     parts = z_collect(parts)
-    late_part = add_halves(late_halves, vector_split(place, vectors))
+    late_part = add_halves(late_halves, vector_split(place, vectors, *shifted))
     late_part, early_part = lax.optimization_barrier((late_part, early_part))
     late_part = exchange(late_part, FIRST_WAY)
 
-    tokens_grad = tokens_back(d_resid, mine, parts, gains, hat1[:64], scale1[:64])
-    block_out = block_rows(resid, ffn, z_collect(ffn_others))
-    tokens_grad, late_part, block_out = lax.optimization_barrier(
-        (tokens_grad, late_part, block_out)
-    )
-    tokens_grad = z_gather_home(tokens_grad, place, home, F32)
-    block_out = z_gather_home(block_out, place, home, BF)
+    rows = final_rows(resid, ffn, ffn_others, d_resid, mine, parts, gains, hat1, scale1)
+    rows, late_part, grad_wide = lax.optimization_barrier((rows, late_part, grad_wide))
+    block_out, tokens_grad = z_gather_home(rows, place, home)
 
     total = exchange(
         join_sums(early_part.reshape(4, 256, -1), late_part.reshape(4, 256, -1)), SECOND_WAY
     )
-    total, vectors = last_sum(total.reshape(4, 64, -1))
-    total = swap_roles(total)
-    vectors = flip_sum(*[to_owner(vectors, a, b) for a in (0, 1) for b in (0, 1)])
-    grad_gate, grad_query, grad_out, grad_key, grad_value = widen(
-        total, [1024, 512, 1024, 512, 1024]
-    )
-    grad_up, grad_down = widen(grad_wide, [1024, 1024])
+    total = swap_roles(last_sum(total.reshape(4, 64, -1)))
+    total, block_out, tokens_grad = lax.optimization_barrier((total, block_out, tokens_grad))
+    grad_gate, grad_query, grad_out, grad_key, grad_value, vectors = widen(
+        total, [1024, 512, 1024, 512, 1024], True
+    )
+    grad_up, grad_down = widen(swap_roles(grad_wide), [1024, 1024])
     return (
         block_out,
         tokens_grad,

time: 431 us -> 417 us (0.968)
  waiting for transfers between devices: 139 us -> 118 us
  local copies, waits for them, and re-layouts: 41.5 us -> 29.7 us
  Pallas kernels: 109 us -> 120 us
  starting transfers between devices: 120 us -> 128 us
    all_to_all x1, waiting for transfers between devices: 20.1 us -> 0.93 us  [body(): lax.all_to_all(jnp.broadcast_to(first[None], (16, 64, cols)), ('x', 'y'),...]
    ppermute x18 -> x21, waiting for transfers between devices: 56.2 us -> 40.2 us  [z_shift(): return lax.ppermute(values, ('zl', 'zh'), pairs(('zl', 'zh'), move))]
    all_to_all x3, waiting for transfers between devices: 2.85 us -> 16.5 us  [exchange(): lax.all_to_all(values, CHIPS, 0, 0, axis_index_groups=groups, tiled=True)]
    unnamed x128 -> x102, local copies, waits for them, and re-layouts: 34.5 us -> 21.2 us
    pallas_call x37 -> x33, Pallas kernels: 109 us -> 120 us  [run(): pl.pallas_call(kernel, grid=grid, in_specs=ins, out_specs=[o[1] for o in...]
    ppermute x6 -> x7, waiting for transfers between devices: 19.6 us -> 29.4 us  [swap_roles(): lax.ppermute(values, ('c', 'zh'), pairs(('c', 'zh'), lambda p: {'c': p['z...]
    all_gather x1, waiting for transfers between devices: 12.8 us -> 3.74 us  [body(): late = lax.all_gather(second, SPANS, axis=0, tiled=True)]
    ppermute x18 -> x21, starting transfers between devices: 21.6 us -> 27.8 us  [z_shift(): return lax.ppermute(values, ('zl', 'zh'), pairs(('zl', 'zh'), move))]
  transfers between devices with their start and end apart: 51 -> 49, of which waited for: 25 -> 25; matrix products, arithmetic and copies ran while one was open for 2% -> 2% of each run, Pallas kernels for 21% -> 27%
where the time goes in v4:
time: 417 us; the launch traced here: 415 us
  starting transfers between devices  128 us (31%)
  Pallas kernels  120 us (29%)
  waiting for transfers between devices  118 us (28%)
  local copies, waits for them, and re-layouts  29.7 us (7%)
  between operations  16 us (4%)
    pallas_call x33, Pallas kernels, run(): pl.pallas_call(kernel, grid=grid, in_specs=ins, out_specs=[o[1] for o in...  120 us
    ppermute x21, waiting for transfers between devices, z_shift(): return lax.ppermute(values, ('zl', 'zh'), pairs(('zl', 'zh'), move))  40.2 us
    ppermute x7, starting transfers between devices, swap_roles(): lax.ppermute(values, ('c', 'zh'), pairs(('c', 'zh'), lambda p: {'c': p['z...  32.7 us
    ppermute x7, waiting for transfers between devices, swap_roles(): lax.ppermute(values, ('c', 'zh'), pairs(('c', 'zh'), lambda p: {'c': p['z...  29.4 us
    ppermute x21, starting transfers between devices, z_shift(): return lax.ppermute(values, ('zl', 'zh'), pairs(('zl', 'zh'), move))  27.8 us
    unnamed x102, local copies, waits for them, and re-layouts  21.2 us
    all_to_all x3, waiting for transfers between devices, exchange(): lax.all_to_all(values, CHIPS, 0, 0, axis_index_groups=groups, tiled=True)  16.5 us
    all_to_all x2, starting transfers between devices, scan_back(): return lax.all_to_all(carried, SPANS, 0, 0, tiled=True).reshape(2 * DK, DV)  13.6 us
  transfers between devices with their start and end apart: 49, of which 25 were waited for; matrix products, arithmetic and copies ran while one was open for 2% of the time, Pallas kernels for 27%

profile of v4, /device:TPU:1, one launch (start us, length us, event | category | flops | bytes accessed | tf_op | source)
XLA Modules:
  0.0 415.0 jit_solution(13095847878151042517)
XLA Ops:
  10.6 6.9 %collective-permute-start = (bf16[64,5248]{1,0:T(8,128)(2,1)}, bf16[64,5248]{1,0:T(8,128)(2,1)S(1)}, u32[]{:S(2)}, u32[]{:S(2)}) collective-permute-start(bf16[64,5248]{1,0:T(8,128)(2,1)} %shard_map.237), channel_id=1, source_target_pairs={{0,0},{4,32},{32,4},{36,36},{1,1},{5,33},{33,5},{37,37},{2,2},{6,3... | collective-permute-start | bytes 2015240 | tf_op jit(solution)/shard_map/ppermute | solution.py:48
  17.5 8.6 %collective-permute-done = bf16[64,5248]{1,0:T(8,128)(2,1)S(1)} collective-permute-done((bf16[64,5248]{1,0:T(8,128)(2,1)}, bf16[64,5248]{1,0:T(8,128)(2,1)S(1)}, u32[]{:S(2)}, u32[]{:S(2)}) %collective-permute-start) | collective-permute-done | bytes 671776 | tf_op jit(solution)/shard_map/ppermute | solution.py:48
  29.1 6.9 %all-to-all-start = ((bf16[16,64,1664]{2,1,0:T(8,128)(2,1)}), bf16[16,64,1664]{2,1,0:T(8,128)(2,1)}, u32[]{:S(2)}, u32[]{:S(2)}) async-start(bf16[16,64,1664]{2,1,0:T(8,128)(2,1)} %broadcast_in_dim.6), calls=%async_computation | async-start | bytes 6815744 | tf_op jit(solution)/shard_map/all_to_all | solution.py:1021
  41.5 12.9 %collective-permute-done.1.values = bf16[256,2048]{1,0:T(8,128)(2,1)S(1)} collective-permute-done((bf16[256,2048]{1,0:T(8,128)(2,1)S(1)}, bf16[256,2048]{1,0:T(8,128)(2,1)S(1)}, u32[]{:S(2)}, u32[]{:S(2)}) %collective-permute-start.1) | collective-permute-done | bytes 1048608 | tf_op jit(solution)/shard_map/ppermute | solution.py:48
  77.3 6.4 %collective-permute-done.5.gains_other.key_other.value_other.w_other = bf16[1024,1664]{1,0:T(8,128)(2,1)} collective-permute-done((bf16[1024,1664]{1,0:T(8,128)(2,1)}, bf16[1024,1664]{1,0:T(8,128)(2,1)}, u32[]{:S(2)}, u32[]{:S(2)}) %collective-permute-start.5) | collective-permute-done | bytes 3407904 | tf_op jit(solution)/shard_map/ppermute | solution.py:81
  83.7 6.9 %shard_map.241 = (bf16[256,512]{1,0:T(8,128)(2,1)}, bf16[256,1024]{1,0:T(8,128)(2,1)}, bf16[512,512]{1,0:T(8,128)(2,1)}, bf16[256,2048]{1,0:T(8,128)(2,1)}, f32[8,2048]{1,0:T(8,128)}) custom-call(f32[2]{0:T(128)} %copy-done.46, s32[4]{0:T(128)} %copy-done.26, f32[256,2048]{1,0:T(8,128)} %get-tuple-element.143.hat, ...), custom_call_target="tpu_custom_call" | custom-call | flops 1 | bytes 1 | tf_op jit(solution)/shard_map/pallas_call | solution.py:136
  90.6 7.4 %all-to-all-start.1 = ((bf16[32,16,512]{2,1,0:T(8,128)(2,1)}), bf16[32,16,512]{2,1,0:T(8,128)(2,1)S(1)}, u32[]{:S(2)}, u32[]{:S(2)}) async-start(bf16[32,16,512]{2,1,0:T(8,128)(2,1)} %bitcast.46), calls=%async_computation.1 | async-start | bytes 1048576 | tf_op jit(solution)/shard_map/all_to_all | solution.py:124
  100.6 12.7 %all-to-all-done.1.parts = bf16[32,16,512]{2,1,0:T(8,128)(2,1)S(1)} async-done(((bf16[32,16,512]{2,1,0:T(8,128)(2,1)}), bf16[32,16,512]{2,1,0:T(8,128)(2,1)S(1)}, u32[]{:S(2)}, u32[]{:S(2)}) %all-to-all-start.1) | async-done | bytes 524320 | tf_op jit(solution)/shard_map/all_to_all | solution.py:124
  114.2 5.9 %all-to-all-start.2 = ((bf16[32,16,512]{2,1,0:T(8,128)(2,1)}), bf16[32,16,512]{2,1,0:T(8,128)(2,1)S(1)}, u32[]{:S(2)}, u32[]{:S(2)}) async-start(bf16[32,16,512]{2,1,0:T(8,128)(2,1)} %shard_map.242), calls=%async_computation.2 | async-start | bytes 1048576 | tf_op jit(solution)/shard_map/all_to_all | solution.py:128
  123.8 6.4 %shard_map.243 = (bf16[256,512]{1,0:T(8,128)(2,1)}, f32[256,1024]{1,0:T(8,128)}, bf16[2,256,256]{2,1,0:T(8,128)(2,1)}, f32[256,1024]{1,0:T(8,128)}) custom-call(f32[2]{0:T(128)} %copy-done.46, s32[4]{0:T(128)} %copy-done.26, bf16[256,2048]{1,0:T(8,128)(2,1)} %get-tuple-element.148.normed.left, ...), custom_call_target="tpu_custom_call" | custom-call | flops 1 | bytes 1 | tf_op jit(solution)/shard_map/pallas_call | solution.py:136
  135.1 6.0 %shard_map.244 = (f32[256,1024]{1,0:T(8,128)}, f32[2,256,1]{2,1,0:T(8,128)}, bf16[256,1024]{1,0:T(8,128)(2,1)}, f32[64,2048]{1,0:T(8,128)}, bf16[64,2048]{1,0:T(...) custom-call(f32[2]{0:T(128)} %copy-done.46, s32[4]{0:T(128)} %copy-done.26, ...), custom_call_target="tpu_custom_call" | custom-call | flops 1 | bytes 1 | tf_op jit(solution)/shard_map/pallas_call | solution.py:136
  149.8 6.7 %collective-permute-done.8.three = bf16[64,2048]{1,0:T(8,128)(2,1)S(1)} collective-permute-done((bf16[64,2048]{1,0:T(8,128)(2,1)}, bf16[64,2048]{1,0:T(8,128)(2,1)S(1)}, u32[]{:S(2)}, u32[]{:S(2)}) %collective-permute-start.8) | collective-permute-done | bytes 262176 | tf_op jit(solution)/shard_map/ppermute | solution.py:58
  182.6 6.2 %shard_map.247 = (bf16[256,2048]{1,0:T(8,128)(2,1)S(1)}, bf16[256,1024]{1,0:T(8,128)(2,1)S(1)}, bf16[256,1024]{1,0:T(8,128)(2,1)S(1)}, f32[64,2048]{1,0:T(8,128)...) custom-call(bf16[64,2048]{1,0:T(8,128)(2,1)S(1)} %get-tuple-element.161.one, ...), custom_call_target="tpu_custom_call" | custom-call | flops 1 | bytes 1 | tf_op jit(solution)/shard_map/pallas_call | solution.py:136
  193.1 6.6 %shard_map.248 = bf16[2048,2048]{1,0:T(8,128)(2,1)} custom-call(bf16[256,2048]{1,0:T(8,128)(2,1)S(1)} %get-tuple-element.170.left_one, bf16[256,1024]{1,0:T(8,128)(2,1)S(1)} %get-tuple-element.171.right_one, bf16[256,2048]{1,0:T(8,128)(2,1)S(1)} %copy-done.2, bf16[256,1024]{1,0:T(8,128)(2,1)S(1)} %get-tuple-element.180.right_two.hidden), custom_call_target="tpu_custom_call" | custom-call | flops 2147483648 | bytes 33554432 | tf_op jit(solution)/shard_map/pallas_call | solution.py:136
  226.5 6.4 %shard_map.251 = (bf16[256,2048]{1,0:T(8,128)(2,1)}, bf16[256,1024]{1,0:T(8,128)(2,1)}, bf16[256,1024]{1,0:T(8,128)(2,1)}, bf16[512,512]{1,0:T(8,128)(2,1)}) custom-call(f32[2]{0:T(128)} %copy-done.46, s32[4]{0:T(128)} %copy-done.26, bf16[64,2048]{1,0:T(8,128)(2,1)} %copy-done.23, bf16[64,2048]{1,0:T(8,128)(2,1)} %copy-done.39, bf16[64,2048]{1,0:T(8,128)(2,1)} %copy-done.38, ...), custom_call_target="tpu_custom_call" | custom-call | flops 1 | bytes 1 | tf_op jit(solution)/shard_map/pallas_call | solution.py:136
  250.8 6.5 %shard_map.253 = (bf16[1024,1536]{1,0:T(8,128)(2,1)}, bf16[1024,1536]{1,0:T(8,128)(2,1)}) custom-call(s32[4]{0:T(128)} %copy-done.26, bf16[256,2048]{1,0:T(8,128)(2,1)} %get-tuple-element.148.normed.left, bf16[256,1024]{1,0:T(8,128)(2,1)} %get-tuple-element.196.refs_0_.d_gate, bf16[256,512]{1,0:T(8,128)(2,1)} %get-tuple-element.216.refs_1_.d_query), custom_call_target="tpu_custom_call" | custom-call | flops 1 | bytes 1 | tf_op jit(solution)/shard_map/pallas_call | solution.py:136
  259.2 7.7 %all-to-all-start.5 = ((bf16[32,16,512]{2,1,0:T(8,128)(2,1)}), bf16[32,16,512]{2,1,0:T(8,128)(2,1)}, u32[]{:S(2)}, u32[]{:S(2)}) async-start(bf16[32,16,512]{2,1,0:T(8,128)(2,1)} %shard_map.256), calls=%async_computation.5 | async-start | bytes 1048576 | tf_op jit(solution)/shard_map/all_to_all | solution.py:128
  272.0 6.4 %shard_map.255 = bf16[1024,2560]{1,0:T(8,128)(2,1)} custom-call(bf16[1024,1536]{1,0:T(8,128)(2,1)} %get-tuple-element.211.refs_0_, bf16[1024,1536]{1,0:T(8,128)(2,1)} %collective-permute-done.22.refs_1_, bf16[1024,1024]{1,0:T(8,128)(2,1)S(1)} %copy-done.10, bf16[1024,1024]{1,0:T(8,128)(2,1)} %collective-permute-done.23.refs_3_), custom_call_target="tpu_custom_call" | custom-call | flops 1 | bytes 1 | tf_op jit(solution)/shard_map/pallas_call | solution.py:136
  288.0 6.6 %shard_map.259 = (bf16[1024,1536]{1,0:T(8,128)(2,1)}, bf16[1024,1536]{1,0:T(8,128)(2,1)}) custom-call(s32[4]{0:T(128)} %copy-done.26, bf16[256,2048]{1,0:T(8,128)(2,1)} %get-tuple-element.148.normed.left, bf16[256,1536]{1,0:T(8,128)(2,1)} %shard_map.258.refs_0_.d_both), custom_call_target="tpu_custom_call" | custom-call | flops 1 | bytes 1 | tf_op jit(solution)/shard_map/pallas_call | solution.py:136
  334.1 6.0 %collective-permute-done.31.d3 = bf16[64,2048]{1,0:T(8,128)(2,1)S(1)} collective-permute-done((bf16[64,2048]{1,0:T(8,128)(2,1)S(1)}, bf16[64,2048]{1,0:T(8,128)(2,1)S(1)}, u32[]{:S(2)}, u32[]{:S(2)}) %collective-permute-start.31) | collective-permute-done | bytes 262176 | tf_op jit(solution)/shard_map/ppermute | solution.py:58
  350.0 7.4 %collective-permute-start.34 = (bf16[64,4096]{1,0:T(8,128)(2,1)}, bf16[64,4096]{1,0:T(8,128)(2,1)}, u32[]{:S(2)}, u32[]{:S(2)}) collective-permute-start(bf16[64,4096]{1,0:T(8,128)(2,1)} %shard_map.263.refs_0_), channel_id=1, source_target_pairs={{4,0},{32,36},{68,64},{96,100},{5,1},{33,37},{69,65},{97,101},{6,2... | collective-permute-start | bytes 1572872 | tf_op jit(solution)/shard_map/ppermute | solution.py:68
  373.0 11.6 %all-to-all-done.8.parts = bf16[4,64,4224]{2,1,0:T(8,128)(2,1)S(1)} async-done(((bf16[4,64,4224]{2,1,0:T(8,128)(2,1)}), bf16[4,64,4224]{2,1,0:T(8,128)(2,1)S(1)}, u32[]{:S(2)}, u32[]{:S(2)}) %all-to-all-start.8) | async-done | bytes 2162720 | tf_op jit(solution)/shard_map/all_to_all | solution.py:132
  384.9 6.7 %collective-permute-start.32 = (bf16[64,4224]{1,0:T(8,128)(2,1)S(1)}, bf16[64,4224]{1,0:T(8,128)(2,1)S(1)}, u32[]{:S(2)}, u32[]{:S(2)}) collective-permute-start(bf16[64,4224]{1,0:T(8,128)(2,1)S(1)} %shard_map.265), channel_id=1, source_target_pairs={{0,0},{4,32},{32,4},{36,36},{1,1},{5,33},{33,5},{37,37},{2,2},{6,3... | collective-permute-start | bytes 1622024 | tf_op jit(solution)/shard_map/ppermute | solution.py:48
  393.6 7.9 %collective-permute-done.37.values = bf16[64,2048]{1,0:T(8,128)(2,1)S(1)} collective-permute-done((bf16[64,2048]{1,0:T(8,128)(2,1)S(1)}, bf16[64,2048]{1,0:T(8,128)(2,1)S(1)}, u32[]{:S(2)}, u32[]{:S(2)}) %collective-permute-start.37) | collective-permute-done | bytes 262176 | tf_op jit(solution)/shard_map/ppermute | solution.py:48
  (227 shorter events, 219.5 us)
Async XLA Ops:
  7.2 116.7 %all-gather.2.cloned.1.call-start = ((), (), s32[]{:S(2)}) async-start(), calls=%async_computation.10 | async-start | bytes 15138816 | tf_op jit(solution)/shard_map/all_gather | solution.py:1024
  10.6 15.5 %collective-permute-start = (bf16[64,5248]{1,0:T(8,128)(2,1)}, bf16[64,5248]{1,0:T(8,128)(2,1)S(1)}, u32[]{:S(2)}, u32[]{:S(2)}) collective-permute-start(bf16[64,5248]{1,0:T(8,128)(2,1)} %shard_map.237), channel_id=1, source_target_pairs={{0,0},{4,32},{32,4},{36,36},{1,1},{5,33},{33,5},{37,37},{2,2},{6,3... | collective-permute-start | bytes 2015240 | tf_op jit(solution)/shard_map/ppermute | solution.py:48
  29.1 46.6 %all-to-all-start = ((bf16[16,64,1664]{2,1,0:T(8,128)(2,1)}), bf16[16,64,1664]{2,1,0:T(8,128)(2,1)}, u32[]{:S(2)}, u32[]{:S(2)}) async-start(bf16[16,64,1664]{2,1,0:T(8,128)(2,1)} %broadcast_in_dim.6), calls=%async_computation | async-start | bytes 6815744 | tf_op jit(solution)/shard_map/all_to_all | solution.py:1021
  36.0 18.3 %collective-permute-start.1 = (bf16[256,2048]{1,0:T(8,128)(2,1)S(1)}, bf16[256,2048]{1,0:T(8,128)(2,1)S(1)}, u32[]{:S(2)}, u32[]{:S(2)}) collective-permute-start(bf16[256,2048]{1,0:T(8,128)(2,1)S(1)} %copy-done.47), channel_id=1, source_target_pairs={{0,0},{4,32},{32,4},{36,36},{1,1},{5,33},{33,5},{37,37},{2,2},{6,3... | collective-permute-start | bytes 3145736 | tf_op jit(solution)/shard_map/ppermute | solution.py:48
  54.3 18.8 %collective-permute-start.2 = (bf16[256,2048]{1,0:T(8,128)(2,1)}, bf16[256,2048]{1,0:T(8,128)(2,1)S(1)}, u32[]{:S(2)}, u32[]{:S(2)}) collective-permute-start(bf16[256,2048]{1,0:T(8,128)(2,1)} %param.27), channel_id=1, source_target_pairs={{0,0},{4,32},{32,4},{36,36},{1,1},{5,33},{33,5},{37,37},{2,2},{6,3... | collective-permute-start | bytes 3145736 | tf_op jit(solution)/shard_map/ppermute | solution.py:48
  59.1 15.7 %collective-permute-start.4 = (f32[2]{0:T(128)S(1)}, f32[2]{0:T(128)S(1)}, u32[]{:S(2)}, u32[]{:S(2)}) collective-permute-start(f32[2]{0:T(128)S(1)} %copy-done.50), channel_id=1, source_target_pairs={{0,0},{4,32},{32,4},{36,36},{1,1},{5,33},{33,5},{37,37},{2,2},{6,3... | collective-permute-start | bytes 32 | tf_op jit(solution)/shard_map/ppermute | solution.py:48
  90.6 22.7 %all-to-all-start.1 = ((bf16[32,16,512]{2,1,0:T(8,128)(2,1)}), bf16[32,16,512]{2,1,0:T(8,128)(2,1)S(1)}, u32[]{:S(2)}, u32[]{:S(2)}) async-start(bf16[32,16,512]{2,1,0:T(8,128)(2,1)} %bitcast.46), calls=%async_computation.1 | async-start | bytes 1048576 | tf_op jit(solution)/shard_map/all_to_all | solution.py:124
  114.2 16.9 %all-to-all-start.2 = ((bf16[32,16,512]{2,1,0:T(8,128)(2,1)}), bf16[32,16,512]{2,1,0:T(8,128)(2,1)S(1)}, u32[]{:S(2)}, u32[]{:S(2)}) async-start(bf16[32,16,512]{2,1,0:T(8,128)(2,1)} %shard_map.242), calls=%async_computation.2 | async-start | bytes 1048576 | tf_op jit(solution)/shard_map/all_to_all | solution.py:128
  131.1 32.9 %all-to-all-start.3 = ((bf16[16,64,1024]{2,1,0:T(8,128)(2,1)}), bf16[16,64,1024]{2,1,0:T(8,128)(2,1)S(1)}, u32[]{:S(2)}, u32[]{:S(2)}) async-start(bf16[16,64,1024]{2,1,0:T(8,128)(2,1)} %broadcast_in_dim.7), calls=%async_computation.3 | async-start | bytes 4194304 | tf_op jit(solution)/shard_map/all_to_all | solution.py:1050
  135.1 214.2 %reduce-scatter.2.cloned.1.call-start = ((), (), s32[]{:S(2)}) async-start(), calls=%async_computation.11 | async-start | bytes 8650752 | tf_op jit(solution)/shard_map/reduce_scatter | solution.py:1062
  167.8 14.8 %collective-permute-start.10 = (bf16[64,2048]{1,0:T(8,128)(2,1)S(1)}, bf16[64,2048]{1,0:T(8,128)(2,1)S(1)}, u32[]{:S(2)}, u32[]{:S(2)}) collective-permute-start(bf16[64,2048]{1,0:T(8,128)(2,1)S(1)} %get-tuple-element.161.one), channel_id=1, source_target_pairs={{0,4},{4,0},{64,68},{68,64},{1,5},{5,1},{65,69},{69,65},{2,6},{6,2... | collective-permute-start | bytes 786440 | tf_op jit(solution)/shard_map/ppermute | solution.py:58
  232.9 24.5 %all-to-all-start.4 = ((bf16[32,16,512]{2,1,0:T(8,128)(2,1)}), bf16[32,16,512]{2,1,0:T(8,128)(2,1)S(1)}, u32[]{:S(2)}, u32[]{:S(2)}) async-start(bf16[32,16,512]{2,1,0:T(8,128)(2,1)} %bitcast.45), calls=%async_computation.4 | async-start | bytes 1048576 | tf_op jit(solution)/shard_map/all_to_all | solution.py:124
  238.0 19.2 %collective-permute-start.19 = (bf16[64,2048]{1,0:T(8,128)(2,1)S(1)}, bf16[64,2048]{1,0:T(8,128)(2,1)S(1)}, u32[]{:S(2)}, u32[]{:S(2)}) collective-permute-start(bf16[64,2048]{1,0:T(8,128)(2,1)S(1)} %copy-done.34), channel_id=1, source_target_pairs={{0,64},{4,68},{64,4},{68,0},{1,65},{5,69},{65,5},{69,1},{2,66},{6,... | collective-permute-start | bytes 786440 | tf_op jit(solution)/shard_map/ppermute | solution.py:58
  238.4 18.9 %collective-permute-start.20 = (bf16[64,2048]{1,0:T(8,128)(2,1)S(1)}, bf16[64,2048]{1,0:T(8,128)(2,1)S(1)}, u32[]{:S(2)}, u32[]{:S(2)}) collective-permute-start(bf16[64,2048]{1,0:T(8,128)(2,1)S(1)} %copy-done.32), channel_id=1, source_target_pairs={{0,68},{4,64},{64,0},{68,4},{1,69},{5,65},{65,1},{69,5},{2,70},{6,... | collective-permute-start | bytes 786440 | tf_op jit(solution)/shard_map/ppermute | solution.py:58
  240.8 16.5 %collective-permute-start.21 = (bf16[64,2048]{1,0:T(8,128)(2,1)S(1)}, bf16[64,2048]{1,0:T(8,128)(2,1)S(1)}, u32[]{:S(2)}, u32[]{:S(2)}) collective-permute-start(bf16[64,2048]{1,0:T(8,128)(2,1)S(1)} %copy-done.30), channel_id=1, source_target_pairs={{0,4},{4,0},{64,68},{68,64},{1,5},{5,1},{65,69},{69,65},{2,6},{6,2... | collective-permute-start | bytes 786440 | tf_op jit(solution)/shard_map/ppermute | solution.py:58
  259.2 20.5 %all-to-all-start.5 = ((bf16[32,16,512]{2,1,0:T(8,128)(2,1)}), bf16[32,16,512]{2,1,0:T(8,128)(2,1)}, u32[]{:S(2)}, u32[]{:S(2)}) async-start(bf16[32,16,512]{2,1,0:T(8,128)(2,1)} %shard_map.256), calls=%async_computation.5 | async-start | bytes 1048576 | tf_op jit(solution)/shard_map/all_to_all | solution.py:128
  279.7 42.1 %all-to-all-start.6 = ((bf16[4,256,2560]{2,1,0:T(8,128)(2,1)}), bf16[4,256,2560]{2,1,0:T(8,128)(2,1)}, u32[]{:S(2)}, u32[]{:S(2)}) async-start(bf16[4,256,2560]{2,1,0:T(8,128)(2,1)} %bitcast.41), calls=%async_computation.6 | async-start | bytes 10485760 | tf_op jit(solution)/shard_map/all_to_all | solution.py:132
  294.5 21.0 %collective-permute-start.24 = (bf16[1024,1536]{1,0:T(8,128)(2,1)}, bf16[1024,1536]{1,0:T(8,128)(2,1)S(1)}, u32[]{:S(2)}, u32[]{:S(2)}) collective-permute-start(bf16[1024,1536]{1,0:T(8,128)(2,1)} %get-tuple-element.221), channel_id=1, source_target_pairs={{0,32},{32,0},{1,33},{33,1},{2,34},{34,2},{3,35},{35,3},{4,36},{36... | collective-permute-start | bytes 9437192 | tf_op jit(solution)/shard_map/ppermute | solution.py:81
  321.8 27.4 %all-to-all-start.7 = ((bf16[4,256,1664]{2,1,0:T(8,128)(2,1)}), bf16[4,256,1664]{2,1,0:T(8,128)(2,1)}, u32[]{:S(2)}, u32[]{:S(2)}) async-start(bf16[4,256,1664]{2,1,0:T(8,128)(2,1)} %bitcast.42), calls=%async_computation.7 | async-start | bytes 6815744 | tf_op jit(solution)/shard_map/all_to_all | solution.py:132
  349.3 19.7 %collective-permute-start.35 = (bf16[64,4096]{1,0:T(8,128)(2,1)}, bf16[64,4096]{1,0:T(8,128)(2,1)S(1)}, u32[]{:S(2)}, u32[]{:S(2)}) collective-permute-start(bf16[64,4096]{1,0:T(8,128)(2,1)} %shard_map.263.refs_0_), channel_id=1, source_target_pairs={{0,64},{36,100},{68,0},{96,36},{1,65},{37,101},{69,1},{97,37},{2,6... | collective-permute-start | bytes 1572872 | tf_op jit(solution)/shard_map/ppermute | solution.py:68
  350.0 19.0 %collective-permute-start.34 = (bf16[64,4096]{1,0:T(8,128)(2,1)}, bf16[64,4096]{1,0:T(8,128)(2,1)}, u32[]{:S(2)}, u32[]{:S(2)}) collective-permute-start(bf16[64,4096]{1,0:T(8,128)(2,1)} %shard_map.263.refs_0_), channel_id=1, source_target_pairs={{4,0},{32,36},{68,64},{96,100},{5,1},{33,37},{69,65},{97,101},{6,2... | collective-permute-start | bytes 1572872 | tf_op jit(solution)/shard_map/ppermute | solution.py:68
  365.2 19.4 %all-to-all-start.8 = ((bf16[4,64,4224]{2,1,0:T(8,128)(2,1)}), bf16[4,64,4224]{2,1,0:T(8,128)(2,1)S(1)}, u32[]{:S(2)}, u32[]{:S(2)}) async-start(bf16[4,64,4224]{2,1,0:T(8,128)(2,1)} %bitcast.40), calls=%async_computation.9 | async-start | bytes 4325376 | tf_op jit(solution)/shard_map/all_to_all | solution.py:132
  371.8 30.5 %collective-permute-start.36 = (bf16[256,4096]{1,0:T(8,128)(2,1)}, bf16[256,4096]{1,0:T(8,128)(2,1)}, u32[]{:S(2)}, u32[]{:S(2)}) collective-permute-start(bf16[256,4096]{1,0:T(8,128)(2,1)} %shard_map.266.mine), channel_id=1, source_target_pairs={{0,32},{36,4},{1,33},{37,5},{2,34},{38,6},{3,35},{39,7},{8,40},{44... | collective-permute-start | bytes 6291464 | tf_op jit(solution)/shard_map/ppermute | solution.py:77
  384.9 21.7 %collective-permute-start.32 = (bf16[64,4224]{1,0:T(8,128)(2,1)S(1)}, bf16[64,4224]{1,0:T(8,128)(2,1)S(1)}, u32[]{:S(2)}, u32[]{:S(2)}) collective-permute-start(bf16[64,4224]{1,0:T(8,128)(2,1)S(1)} %shard_map.265), channel_id=1, source_target_pairs={{0,0},{4,32},{32,4},{36,36},{1,1},{5,33},{33,5},{37,37},{2,2},{6,3... | collective-permute-start | bytes 1622024 | tf_op jit(solution)/shard_map/ppermute | solution.py:48
  (76 other events, 629.3 us)
Sparse Core Ops, SparseCore 0:
  27.1 96.7 all-gather.1
  204.9 95.9 reduce-scatter.1

commit v5 on v4

--- a/solution.py
+++ b/solution.py
@@ -311,31 +311,6 @@
     )[0]
 
 
-def add_kernel(*refs):
-    out, start = refs[-1], 0
-    for own, other in zip(refs[:-1:2], refs[1:-1:2]):
-        cols = own.shape[1]
-        total = own[...].astype(F32) + other[...].astype(F32)
-        out[:, start : start + cols] = total.astype(BF)
-        start += cols
-
-
-def add_halves(*pairs_of):
-    operands = [a for own, other in pairs_of for a in (own, core_swap(other))]
-    cols = sum(own.shape[1] for own, other in pairs_of)
-
-    def block(n):
-        return pl.BlockSpec((256, n), lambda i: (i, 0))
-
-    return run(
-        add_kernel,
-        (4,),
-        [block(a.shape[1]) for a in operands],
-        [(shape((1024, cols), BF), block(cols))],
-        operands,
-    )[0]
-
-
 def collected(mine, others):
     total = mine[...]
     for other in others:
@@ -392,6 +367,7 @@
             (shape((2, 2048), F32), whole((2, 2048))),
         ],
         [out_grad, mine, *others, gains, hat, scale],
+        limit=61,
     )
 
 
@@ -880,27 +856,70 @@
         ]
 
 
-def split_kernel(place, left, *refs):
-    rights, own, other = refs[:-2], refs[-2], refs[-1]
-    for ref, side in ((own, place[1]), (other, 1 - place[1])):
-        rows = left[:, pl.ds(pl.multiple_of(side * 256, 256), 256)]
-        start = 0
-        for right in rights:
-            store_rows(ref, tn(rows, right[...]).astype(BF), side, start)
-            start += right.shape[1]
-
-
-def grad_split(place, left, rights):
+def row_offsets(side):
+    i = pl.program_id(0)
+    for j in range(4):
+        to = jnp.where(side == 0, i * 256 + j * 64, j * 256 + i * 64)
+        yield slice(j * 64, j * 64 + 64), pl.ds(pl.multiple_of(to, 64), 64)
+
+
+def other_kernel(place, left, *refs):
+    rights, other = refs[:-1], refs[-1]
+    side = 1 - place[1]
+    rows = left[:, pl.ds(pl.multiple_of(side * 256, 256), 256)]
+    start = 0
+    for right in rights:
+        store_rows(other, tn(rows, right[...]).astype(BF), side, start)
+        start += right.shape[1]
+
+
+def grad_other(place, left, rights):
     cols = sum(r.shape[1] for r in rights)
-    half = (shape((1024, cols), BF), whole((1024, cols)))
-    return run(
-        split_kernel,
+    return run(
+        other_kernel,
         (4,),
         [SCALARS, columns(256, 512)] + [whole(r.shape) for r in rights],
-        [half, half],
+        [(shape((1024, cols), BF), whole((1024, cols)))],
         [place, left, *rights],
         limit=61,
-    )
+    )[0]
+
+
+def own_kernel(sizes, place, *refs):
+    out, refs, start = refs[-1], list(refs[:-1]), 0
+    side = place[1]
+    for size in sizes:
+        left, rights, given = refs[0], refs[1 : 1 + size], refs[1 + size]
+        refs, local = refs[2 + size :], 0
+        rows = left[:, pl.ds(pl.multiple_of(side * 256, 256), 256)]
+        for right in rights:
+            made, cols = tn(rows, right[...]), right.shape[1]
+            for take, to in row_offsets(side):
+                total = made[take] + given[to, local : local + cols].astype(F32)
+                out[to, start : start + cols] = total.astype(BF)
+            start, local = start + cols, local + cols
+    if refs:
+        for take, to in row_offsets(side):
+            total = refs[0][to, :].astype(F32) + refs[1][to, :].astype(F32)
+            out[to, start:] = total.astype(BF)
+
+
+def grad_own(place, groups, more=()):
+    specs, operands, sizes, cols = [SCALARS], [place], [], sum(m.shape[1] for m in more[:1])
+    for left, rights, given in groups:
+        specs += [columns(256, 512)] + [whole(r.shape) for r in rights] + [whole(given.shape)]
+        operands += [left, *rights, given]
+        sizes.append(len(rights))
+        cols += given.shape[1]
+    specs += [whole(m.shape) for m in more]
+    return run(
+        functools.partial(own_kernel, tuple(sizes)),
+        (4,),
+        specs,
+        [(shape((1024, cols), BF), whole((1024, cols)), "hbm")],
+        operands + list(more),
+        limit=61,
+    )[0]
 
 
 def vector_kernel(place, one, two, three, four, own, other):
@@ -922,28 +941,47 @@
     )
 
 
-def join_kernel(one, two, out):
-    start = 0
-    for ref in (one, two):
-        total = ref[0].astype(F32)
-        for k in range(1, 4):
-            total = total + ref[k].astype(F32)
-        out[:, start : start + total.shape[1]] = total.astype(BF)
-        start += total.shape[1]
-
-
-def join_sums(one, two):
-    def block(values):
-        return pl.BlockSpec((4, 64, values.shape[2]), lambda i: (0, i, 0))
-
-    cols = one.shape[2] + two.shape[2]
-    return run(
-        join_kernel,
+def four_sum(ref):
+    total = ref[0].astype(F32)
+    for k in range(1, 4):
+        total = total + ref[k].astype(F32)
+    return total.astype(BF)
+
+
+def early_kernel(parts, out):
+    out[:, out.shape[1] - parts.shape[2] :] = four_sum(parts)
+
+
+def early_sum(parts, cols):
+    return run(
+        early_kernel,
         (4,),
-        [block(one), block(two)],
-        [(shape((256, cols), BF), pl.BlockSpec((64, cols), lambda i: (i, 0)))],
-        [one, two],
+        [pl.BlockSpec((4, 64, parts.shape[2]), lambda i: (0, i, 0))],
+        [(shape((256, cols), BF), pl.BlockSpec((64, cols), lambda i: (i, 0)), "hbm")],
+        [parts],
+        limit=61,
     )[0]
+
+
+def late_kernel(kept, parts, out):
+    out[...] = four_sum(parts)
+
+
+def late_sum(wide, parts):
+    cols = parts.shape[2]
+    return pl.pallas_call(
+        late_kernel,
+        grid=(4,),
+        in_specs=[
+            pl.BlockSpec(memory_space=pl.ANY),
+            pl.BlockSpec((4, 64, cols), lambda i: (0, i, 0)),
+        ],
+        out_specs=pl.BlockSpec((64, cols), lambda i: (i, 0)),
+        out_shape=pltpu.HBM(wide.shape, BF),
+        input_output_aliases={0: 0},
+        compiler_params=pltpu.CompilerParams(vmem_limit_bytes=48 * 1024 * 1024),
+        cost_estimate=pl.CostEstimate(flops=1, bytes_accessed=1, transcendentals=0),
+    )(wide, parts)
 
 
 def last_kernel(parts, out):
@@ -972,12 +1010,12 @@
             start += out.shape[1]
         else:
             out[...] = values[:, start : start + 128].astype(F32).T[:8]
-
-
-def widen(values, widths, vectors=False):
-    outs = [(shape((64, n), F32), whole((64, n))) for n in widths]
-    if vectors:
-        outs.append((shape((8, 64), F32), whole((8, 64))))
+            start += 128
+
+
+def widen(values, widths):
+    dims = [(64, n) if n else (8, 64) for n in widths]
+    outs = [(shape(d, F32), whole(d)) for d in dims]
     return run(widen_kernel, (1,), [whole(values.shape)], outs, [values])
 
 
@@ -1058,7 +1096,7 @@
     parts = z_collect(parts)
     grad_wide = grad_pair(normed2, d_up, out_grad, hidden)
     mine, parts, grad_wide = lax.optimization_barrier((mine, parts, grad_wide))
-    d_resid, d_attn, vectors2 = resid_back(out_grad[:64], mine, parts, gains, hat2, scale2)
+    d_resid, d_attn, vectors2 = resid_back(out_grad, mine, parts, gains, hat2, scale2)
     grad_wide = lax.psum_scatter(grad_wide, SPANS, scatter_dimension=0, tiled=True)
     hidden, d_attn = lax.optimization_barrier((hidden, d_attn))
     ffn, *ffn_others = ffn_parts(place, hidden, down, down_other)
@@ -1073,16 +1111,20 @@
     d_query, key_part, value_part = query_back(
         rate, place, d_ret, value, key, query, probs, state, cosine, sine
     )
-    out_halves = grad_split(place, d_attn, [mixed])
-    gate_halves = grad_split(place, normed1, [d_gate, d_query])
-    gate_halves, out_halves, ffn_others = lax.optimization_barrier(
-        (gate_halves, out_halves, ffn_others)
-    )
-    parts, gate_halves, out_halves = lax.optimization_barrier(
-        (parts, gate_halves, out_halves)
-    )
+    out_other = grad_other(place, d_attn, [mixed])
+    gate_other = grad_other(place, normed1, [d_gate, d_query])
+    gate_other, out_other, ffn_others = lax.optimization_barrier(
+        (gate_other, out_other, ffn_others)
+    )
+    parts, gate_other, out_other = lax.optimization_barrier((parts, gate_other, out_other))
     later = scan_back(scan_spans(scan_rate, parts, True))
-    early_part = add_halves(gate_halves, out_halves)
+    early_part = grad_own(
+        place,
+        [
+            (normed1, [d_gate, d_query], core_swap(gate_other)),
+            (d_attn, [mixed], core_swap(out_other)),
+        ],
+    )
     d_query, parts = lax.optimization_barrier((d_query, parts))
     d_first = normed_back_first(d_query, d_gate, late)
     early_part, later, d_first = lax.optimization_barrier((early_part, later, d_first))
@@ -1091,29 +1133,34 @@
     d_both = key_value_back(
         rate, place, key_part, value_part, key, value, later, cosine, sine
     )
-    late_halves = grad_split(place, normed1, [d_both])
-    d_both, late_halves = lax.optimization_barrier((d_both, late_halves))
+    late_other = grad_other(place, normed1, [d_both])
+    d_both, late_other = lax.optimization_barrier((d_both, late_other))
+    late_other = core_swap(late_other)
     mine, *parts, vectors = normed_back(place, d_first, d_both, early, early_other, hat1)
     vectors = jnp.concatenate([vectors, vectors2, jnp.zeros((4, 2048), F32)])
     shifted = [z_shift(vectors, shift) for shift in (1, 3, 2)]
     parts = z_collect(parts)
-    late_part = add_halves(late_halves, vector_split(place, vectors, *shifted))
+    vector_own, vector_other = vector_split(place, vectors, *shifted)
+    late_part = grad_own(
+        place, [(normed1, [d_both], late_other)], (vector_own, core_swap(vector_other))
+    )
     late_part, early_part = lax.optimization_barrier((late_part, early_part))
     late_part = exchange(late_part, FIRST_WAY)
 
+    joined = early_sum(early_part.reshape(4, 256, -1), 4224)
+    parts, grad_wide, joined = lax.optimization_barrier((parts, grad_wide, joined))
     rows = final_rows(resid, ffn, ffn_others, d_resid, mine, parts, gains, hat1, scale1)
-    rows, late_part, grad_wide = lax.optimization_barrier((rows, late_part, grad_wide))
+    kept, late_part = lax.optimization_barrier((rows, late_part))
     block_out, tokens_grad = z_gather_home(rows, place, home)
 
-    total = exchange(
-        join_sums(early_part.reshape(4, 256, -1), late_part.reshape(4, 256, -1)), SECOND_WAY
-    )
+    total = exchange(late_sum(joined, late_part.reshape(4, 256, -1)), SECOND_WAY)
+    total, grad_wide = lax.optimization_barrier((total, swap_roles(grad_wide)))
     total = swap_roles(last_sum(total.reshape(4, 64, -1)))
     total, block_out, tokens_grad = lax.optimization_barrier((total, block_out, tokens_grad))
-    grad_gate, grad_query, grad_out, grad_key, grad_value, vectors = widen(
-        total, [1024, 512, 1024, 512, 1024], True
-    )
-    grad_up, grad_down = widen(swap_roles(grad_wide), [1024, 1024])
+    grad_key, grad_value, vectors, grad_gate, grad_query, grad_out = widen(
+        total, [512, 1024, 0, 1024, 512, 1024]
+    )
+    grad_up, grad_down = widen(grad_wide, [1024, 1024])
     return (
         block_out,
         tokens_grad,

time: 417 us -> 401 us (0.962)
  waiting for transfers between devices: 118 us -> 95.7 us
  Pallas kernels: 120 us -> 127 us
  local copies, waits for them, and re-layouts: 29.7 us -> 23.4 us
  starting transfers between devices: 128 us -> 134 us
    all_to_all x3, waiting for transfers between devices: 16.5 us -> 0.01 us  [exchange(): lax.all_to_all(values, CHIPS, 0, 0, axis_index_groups=groups, tiled=True)]
    ppermute x7, starting transfers between devices: 32.7 us -> 39.2 us  [swap_roles(): lax.ppermute(values, ('c', 'zh'), pairs(('c', 'zh'), lambda p: {'c': p['z...]
    unnamed x102 -> x90, local copies, waits for them, and re-layouts: 21.2 us -> 16 us
    ppermute x21, waiting for transfers between devices: 40.2 us -> 36 us  [z_shift(): return lax.ppermute(values, ('zl', 'zh'), pairs(('zl', 'zh'), move))]
  transfers between devices with their start and end apart: 49 -> 49, of which waited for: 25 -> 25; matrix products, arithmetic and copies ran while one was open for 2% -> 2% of each run, Pallas kernels for 27% -> 30%
where the time goes in v5:
time: 401 us; the launch traced here: 399 us
  starting transfers between devices  134 us (33%)
  Pallas kernels  127 us (32%)
  waiting for transfers between devices  95.7 us (24%)
  local copies, waits for them, and re-layouts  23.4 us (6%)
  between operations  15.9 us (4%)
    pallas_call x33, Pallas kernels, run(): pl.pallas_call(kernel, grid=grid, in_specs=ins, out_specs=[o[1] for o in...  123 us
    ppermute x7, starting transfers between devices, swap_roles(): lax.ppermute(values, ('c', 'zh'), pairs(('c', 'zh'), lambda p: {'c': p['z...  39.2 us
    ppermute x21, waiting for transfers between devices, z_shift(): return lax.ppermute(values, ('zl', 'zh'), pairs(('zl', 'zh'), move))  36 us
    ppermute x7, waiting for transfers between devices, swap_roles(): lax.ppermute(values, ('c', 'zh'), pairs(('c', 'zh'), lambda p: {'c': p['z...  27.4 us
    ppermute x21, starting transfers between devices, z_shift(): return lax.ppermute(values, ('zl', 'zh'), pairs(('zl', 'zh'), move))  26.1 us
    unnamed x90, local copies, waits for them, and re-layouts  16 us
    all_to_all x3, starting transfers between devices, exchange(): lax.all_to_all(values, CHIPS, 0, 0, axis_index_groups=groups, tiled=True)  14.9 us
    all_to_all x2, starting transfers between devices, scan_back(): return lax.all_to_all(carried, SPANS, 0, 0, tiled=True).reshape(2 * DK, DV)  13.4 us
  transfers between devices with their start and end apart: 49, of which 25 were waited for; matrix products, arithmetic and copies ran while one was open for 2% of the time, Pallas kernels for 30%

profile of v5, /device:TPU:1, one launch (start us, length us, event | category | flops | bytes accessed | tf_op | source)
XLA Modules:
  0.0 398.6 jit_solution(2191295823616148977)
XLA Ops:
  10.6 6.9 %collective-permute-start = (bf16[64,5248]{1,0:T(8,128)(2,1)}, bf16[64,5248]{1,0:T(8,128)(2,1)S(1)}, u32[]{:S(2)}, u32[]{:S(2)}) collective-permute-start(bf16[64,5248]{1,0:T(8,128)(2,1)} %shard_map.237), channel_id=1, source_target_pairs={{0,0},{4,32},{32,4},{36,36},{1,1},{5,33},{33,5},{37,37},{2,2},{6,3... | collective-permute-start | bytes 2015240 | tf_op jit(solution)/shard_map/ppermute | solution.py:48
  17.5 8.6 %collective-permute-done = bf16[64,5248]{1,0:T(8,128)(2,1)S(1)} collective-permute-done((bf16[64,5248]{1,0:T(8,128)(2,1)}, bf16[64,5248]{1,0:T(8,128)(2,1)S(1)}, u32[]{:S(2)}, u32[]{:S(2)}) %collective-permute-start) | collective-permute-done | bytes 671776 | tf_op jit(solution)/shard_map/ppermute | solution.py:48
  29.1 6.9 %all-to-all-start = ((bf16[16,64,1664]{2,1,0:T(8,128)(2,1)}), bf16[16,64,1664]{2,1,0:T(8,128)(2,1)}, u32[]{:S(2)}, u32[]{:S(2)}) async-start(bf16[16,64,1664]{2,1,0:T(8,128)(2,1)} %broadcast_in_dim.6), calls=%async_computation | async-start | bytes 6815744 | tf_op jit(solution)/shard_map/all_to_all | solution.py:1059
  36.0 5.4 %collective-permute-start.1 = (bf16[256,2048]{1,0:T(8,128)(2,1)S(1)}, bf16[256,2048]{1,0:T(8,128)(2,1)S(1)}, u32[]{:S(2)}, u32[]{:S(2)}) collective-permute-start(bf16[256,2048]{1,0:T(8,128)(2,1)S(1)} %copy-done.41), channel_id=1, source_target_pairs={{0,0},{4,32},{32,4},{36,36},{1,1},{5,33},{33,5},{37,37},{2,2},{6,3... | collective-permute-start | bytes 3145736 | tf_op jit(solution)/shard_map/ppermute | solution.py:48
  41.5 12.9 %collective-permute-done.1.values = bf16[256,2048]{1,0:T(8,128)(2,1)S(1)} collective-permute-done((bf16[256,2048]{1,0:T(8,128)(2,1)S(1)}, bf16[256,2048]{1,0:T(8,128)(2,1)S(1)}, u32[]{:S(2)}, u32[]{:S(2)}) %collective-permute-start.1) | collective-permute-done | bytes 1048608 | tf_op jit(solution)/shard_map/ppermute | solution.py:48
  77.3 6.4 %collective-permute-done.5.gains_other.key_other.value_other.w_other = bf16[1024,1664]{1,0:T(8,128)(2,1)} collective-permute-done((bf16[1024,1664]{1,0:T(8,128)(2,1)}, bf16[1024,1664]{1,0:T(8,128)(2,1)}, u32[]{:S(2)}, u32[]{:S(2)}) %collective-permute-start.5) | collective-permute-done | bytes 3407904 | tf_op jit(solution)/shard_map/ppermute | solution.py:81
  83.7 6.9 %shard_map.241 = (bf16[256,512]{1,0:T(8,128)(2,1)}, bf16[256,1024]{1,0:T(8,128)(2,1)}, bf16[512,512]{1,0:T(8,128)(2,1)}, bf16[256,2048]{1,0:T(8,128)(2,1)}, f32[8,2048]{1,0:T(8,128)}) custom-call(f32[2]{0:T(128)} %copy-done.39, s32[4]{0:T(128)} %copy-done.18, f32[256,2048]{1,0:T(8,128)} %get-tuple-element.135.hat, ...), custom_call_target="tpu_custom_call" | custom-call | flops 1 | bytes 1 | tf_op jit(solution)/shard_map/pallas_call | solution.py:136
  90.6 7.4 %all-to-all-start.1 = ((bf16[32,16,512]{2,1,0:T(8,128)(2,1)}), bf16[32,16,512]{2,1,0:T(8,128)(2,1)S(1)}, u32[]{:S(2)}, u32[]{:S(2)}) async-start(bf16[32,16,512]{2,1,0:T(8,128)(2,1)} %bitcast.48), calls=%async_computation.1 | async-start | bytes 1048576 | tf_op jit(solution)/shard_map/all_to_all | solution.py:124
  100.6 12.7 %all-to-all-done.1.parts = bf16[32,16,512]{2,1,0:T(8,128)(2,1)S(1)} async-done(((bf16[32,16,512]{2,1,0:T(8,128)(2,1)}), bf16[32,16,512]{2,1,0:T(8,128)(2,1)S(1)}, u32[]{:S(2)}, u32[]{:S(2)}) %all-to-all-start.1) | async-done | bytes 524320 | tf_op jit(solution)/shard_map/all_to_all | solution.py:124
  114.2 5.9 %all-to-all-start.2 = ((bf16[32,16,512]{2,1,0:T(8,128)(2,1)}), bf16[32,16,512]{2,1,0:T(8,128)(2,1)S(1)}, u32[]{:S(2)}, u32[]{:S(2)}) async-start(bf16[32,16,512]{2,1,0:T(8,128)(2,1)} %shard_map.242), calls=%async_computation.2 | async-start | bytes 1048576 | tf_op jit(solution)/shard_map/all_to_all | solution.py:128
  123.8 6.4 %shard_map.243 = (bf16[256,512]{1,0:T(8,128)(2,1)}, f32[256,1024]{1,0:T(8,128)}, bf16[2,256,256]{2,1,0:T(8,128)(2,1)}, f32[256,1024]{1,0:T(8,128)}) custom-call(f32[2]{0:T(128)} %copy-done.39, s32[4]{0:T(128)} %copy-done.18, bf16[256,2048]{1,0:T(8,128)(2,1)} %get-tuple-element.139.normed.left.refs_0_, ...), custom_call_target="tpu_custom_call" | custom-call | flops 1 | bytes 1 | tf_op jit(solution)/shard_map/pallas_call | solution.py:136
  135.2 6.1 %shard_map.244 = (f32[256,1024]{1,0:T(8,128)}, f32[2,256,1]{2,1,0:T(8,128)}, bf16[256,1024]{1,0:T(8,128)(2,1)}, f32[64,2048]{1,0:T(8,128)}, bf16[64,2048]{1,0:T(...) custom-call(f32[2]{0:T(128)} %copy-done.39, s32[4]{0:T(128)} %copy-done.18, ...), custom_call_target="tpu_custom_call" | custom-call | flops 1 | bytes 1 | tf_op jit(solution)/shard_map/pallas_call | solution.py:136
  149.9 6.7 %collective-permute-done.8.three = bf16[64,2048]{1,0:T(8,128)(2,1)S(1)} collective-permute-done((bf16[64,2048]{1,0:T(8,128)(2,1)}, bf16[64,2048]{1,0:T(8,128)(2,1)S(1)}, u32[]{:S(2)}, u32[]{:S(2)}) %collective-permute-start.8) | collective-permute-done | bytes 262176 | tf_op jit(solution)/shard_map/ppermute | solution.py:58
  177.3 5.6 %collective-permute-done.10.three = bf16[64,2048]{1,0:T(8,128)(2,1)S(1)} collective-permute-done((bf16[64,2048]{1,0:T(8,128)(2,1)S(1)}, bf16[64,2048]{1,0:T(8,128)(2,1)S(1)}, u32[]{:S(2)}, u32[]{:S(2)}) %collective-permute-start.10) | collective-permute-done | bytes 262176 | tf_op jit(solution)/shard_map/ppermute | solution.py:58
  182.9 6.1 %shard_map.247 = (bf16[256,2048]{1,0:T(8,128)(2,1)S(1)}, bf16[256,1024]{1,0:T(8,128)(2,1)S(1)}, bf16[256,1024]{1,0:T(8,128)(2,1)S(1)}, f32[64,2048]{1,0:T(8,128)...) custom-call(bf16[64,2048]{1,0:T(8,128)(2,1)S(1)} %get-tuple-element.155.one, ...), custom_call_target="tpu_custom_call" | custom-call | flops 1 | bytes 1 | tf_op jit(solution)/shard_map/pallas_call | solution.py:136
  193.2 6.6 %shard_map.248 = bf16[2048,2048]{1,0:T(8,128)(2,1)} custom-call(bf16[256,2048]{1,0:T(8,128)(2,1)S(1)} %get-tuple-element.164.left_one, bf16[256,1024]{1,0:T(8,128)(2,1)S(1)} %get-tuple-element.165.right_one, bf16[256,2048]{1,0:T(8,128)(2,1)S(1)} %copy-done.2, bf16[256,1024]{1,0:T(8,128)(2,1)S(1)} %get-tuple-element.174.right_two.hidden), custom_call_target="tpu_custom_call" | custom-call | flops 2147483648 | bytes 33554432 | tf_op jit(solution)/shard_map/pallas_call | solution.py:136
  222.7 6.3 %shard_map.251 = (bf16[256,2048]{1,0:T(8,128)(2,1)}, bf16[256,1024]{1,0:T(8,128)(2,1)}, bf16[256,1024]{1,0:T(8,128)(2,1)}, bf16[512,512]{1,0:T(8,128)(2,1)}) custom-call(f32[2]{0:T(128)} %copy-done.39, s32[4]{0:T(128)} %copy-done.18, bf16[64,2048]{1,0:T(8,128)(2,1)} %get-tuple-element.179.one, bf16[64,2048]{1,0:T(8,128)(2,1)} %collective-permute-done.16.two, ...), custom_call_target="tpu_custom_call" | custom-call | flops 1 | bytes 1 | tf_op jit(solution)/shard_map/pallas_call | solution.py:136
  254.0 7.6 %all-to-all-start.5 = ((bf16[32,16,512]{2,1,0:T(8,128)(2,1)}), bf16[32,16,512]{2,1,0:T(8,128)(2,1)}, u32[]{:S(2)}, u32[]{:S(2)}) async-start(bf16[32,16,512]{2,1,0:T(8,128)(2,1)} %shard_map.256), calls=%async_computation.5 | async-start | bytes 1048576 | tf_op jit(solution)/shard_map/all_to_all | solution.py:128
  266.5 8.3 %shard_map.255 = bf16[1024,2560]{1,0:T(8,128)(2,1)} custom-call(s32[4]{0:T(128)} %copy-done.18, bf16[256,2048]{1,0:T(8,128)(2,1)} %get-tuple-element.139.normed.left.refs_0_, bf16[256,1024]{1,0:T(8,128)(2,1)} %get-tuple-element.185.refs_0_.refs_1_.d_gate, bf16[256,512]{1,0:T(8,128)(2,1)} %get-tuple-element.200.refs_1_.refs_2_.d_query, ...), custom_call_target="tpu_custom_call" | custom-call | flops 1 | bytes 1 | tf_op jit(solution)/shard_map/pallas_call | solution.py:136
  292.6 5.6 %shard_map.260 = (f32[64,2048]{1,0:T(8,128)S(1)}, bf16[64,2048]{1,0:T(8,128)(2,1)S(1)}, bf16[64,2048]{1,0:T(8,128)(2,1)S(1)}, bf16[64,2048]{1,0:T(8,128)(2,1)S(1)}, f32[2,2048]{1,0:T(2,128)S(1)}) custom-call(s32[4]{0:T(128)S(1)} %copy-done.20, f32[256,2048]{1,0:T(8,128)S(1)} %shard_map.257.first, bf16[256,1536]{1,0:T(8,128)(2,1)S(1)} %copy-done.3, ...), custom_call_target="tpu_custom_call" | custom-call | flops 1 | bytes 1 | tf_op jit(solution)/shard_map/pallas_call | solution.py:136
  313.7 6.4 %shard_map.262 = bf16[1024,1664]{1,0:T(8,128)(2,1)} custom-call(s32[4]{0:T(128)} %copy-done.18, bf16[256,2048]{1,0:T(8,128)(2,1)} %get-tuple-element.139.normed.left.refs_0_, bf16[256,1536]{1,0:T(8,128)(2,1)} %shard_map.258.refs_0_.d_both.refs_1_, bf16[1024,1536]{1,0:T(8,128)(2,1)} %collective-permute-done.27.refs_2_, bf16[1024,128]{1,0:T(8,128)(2,1)} %copy-done.17, ...), custom_call_target="tpu_custom_call" | custom-call | flops 1 | bytes 1 | tf_op jit(solution)/shard_map/pallas_call | solution.py:136
  342.7 6.0 %collective-permute-start.35 = (bf16[64,4096]{1,0:T(8,128)(2,1)}, bf16[64,4096]{1,0:T(8,128)(2,1)}, u32[]{:S(2)}, u32[]{:S(2)}) collective-permute-start(bf16[64,4096]{1,0:T(8,128)(2,1)} %shard_map.264.refs_0_), channel_id=1, source_target_pairs={{4,0},{32,36},{68,64},{96,100},{5,1},{33,37},{69,65},{97,101},{6,2... | collective-permute-start | bytes 1572872 | tf_op jit(solution)/shard_map/ppermute | solution.py:68
  363.9 8.1 %collective-permute-start.32 = (bf16[64,2048]{1,0:T(8,128)(2,1)S(1)}, bf16[64,2048]{1,0:T(8,128)(2,1)S(1)}, u32[]{:S(2)}, u32[]{:S(2)}) collective-permute-start(bf16[64,2048]{1,0:T(8,128)(2,1)S(1)} %copy-done.42), channel_id=1, source_target_pairs={{0,0},{4,32},{32,4},{36,36},{1,1},{5,33},{33,5},{37,37},{2,2},{6,3... | collective-permute-start | bytes 786440 | tf_op jit(solution)/shard_map/ppermute | solution.py:48
  376.3 7.0 %collective-permute-start.33 = (bf16[64,4224]{1,0:T(8,128)(2,1)S(1)}, bf16[64,4224]{1,0:T(8,128)(2,1)S(1)}, u32[]{:S(2)}, u32[]{:S(2)}) collective-permute-start(bf16[64,4224]{1,0:T(8,128)(2,1)S(1)} %shard_map.266), channel_id=1, source_target_pairs={{0,0},{4,32},{32,4},{36,36},{1,1},{5,33},{33,5},{37,37},{2,2},{6,3... | collective-permute-start | bytes 1622024 | tf_op jit(solution)/shard_map/ppermute | solution.py:48
  (215 shorter events, 210.0 us)
Async XLA Ops:
  7.2 116.7 %all-gather.2.cloned.1.call-start = ((), (), s32[]{:S(2)}) async-start(), calls=%async_computation.10 | async-start | bytes 15138816 | tf_op jit(solution)/shard_map/all_gather | solution.py:1062
  10.6 15.5 %collective-permute-start = (bf16[64,5248]{1,0:T(8,128)(2,1)}, bf16[64,5248]{1,0:T(8,128)(2,1)S(1)}, u32[]{:S(2)}, u32[]{:S(2)}) collective-permute-start(bf16[64,5248]{1,0:T(8,128)(2,1)} %shard_map.237), channel_id=1, source_target_pairs={{0,0},{4,32},{32,4},{36,36},{1,1},{5,33},{33,5},{37,37},{2,2},{6,3... | collective-permute-start | bytes 2015240 | tf_op jit(solution)/shard_map/ppermute | solution.py:48
  29.1 46.6 %all-to-all-start = ((bf16[16,64,1664]{2,1,0:T(8,128)(2,1)}), bf16[16,64,1664]{2,1,0:T(8,128)(2,1)}, u32[]{:S(2)}, u32[]{:S(2)}) async-start(bf16[16,64,1664]{2,1,0:T(8,128)(2,1)} %broadcast_in_dim.6), calls=%async_computation | async-start | bytes 6815744 | tf_op jit(solution)/shard_map/all_to_all | solution.py:1059
  36.0 18.3 %collective-permute-start.1 = (bf16[256,2048]{1,0:T(8,128)(2,1)S(1)}, bf16[256,2048]{1,0:T(8,128)(2,1)S(1)}, u32[]{:S(2)}, u32[]{:S(2)}) collective-permute-start(bf16[256,2048]{1,0:T(8,128)(2,1)S(1)} %copy-done.41), channel_id=1, source_target_pairs={{0,0},{4,32},{32,4},{36,36},{1,1},{5,33},{33,5},{37,37},{2,2},{6,3... | collective-permute-start | bytes 3145736 | tf_op jit(solution)/shard_map/ppermute | solution.py:48
  54.3 18.9 %collective-permute-start.2 = (bf16[256,2048]{1,0:T(8,128)(2,1)}, bf16[256,2048]{1,0:T(8,128)(2,1)S(1)}, u32[]{:S(2)}, u32[]{:S(2)}) collective-permute-start(bf16[256,2048]{1,0:T(8,128)(2,1)} %param.27), channel_id=1, source_target_pairs={{0,0},{4,32},{32,4},{36,36},{1,1},{5,33},{33,5},{37,37},{2,2},{6,3... | collective-permute-start | bytes 3145736 | tf_op jit(solution)/shard_map/ppermute | solution.py:48
  59.1 15.7 %collective-permute-start.4 = (f32[2]{0:T(128)S(1)}, f32[2]{0:T(128)S(1)}, u32[]{:S(2)}, u32[]{:S(2)}) collective-permute-start(f32[2]{0:T(128)S(1)} %copy-done.44), channel_id=1, source_target_pairs={{0,0},{4,32},{32,4},{36,36},{1,1},{5,33},{33,5},{37,37},{2,2},{6,3... | collective-permute-start | bytes 32 | tf_op jit(solution)/shard_map/ppermute | solution.py:48
  90.6 22.7 %all-to-all-start.1 = ((bf16[32,16,512]{2,1,0:T(8,128)(2,1)}), bf16[32,16,512]{2,1,0:T(8,128)(2,1)S(1)}, u32[]{:S(2)}, u32[]{:S(2)}) async-start(bf16[32,16,512]{2,1,0:T(8,128)(2,1)} %bitcast.48), calls=%async_computation.1 | async-start | bytes 1048576 | tf_op jit(solution)/shard_map/all_to_all | solution.py:124
  114.2 16.9 %all-to-all-start.2 = ((bf16[32,16,512]{2,1,0:T(8,128)(2,1)}), bf16[32,16,512]{2,1,0:T(8,128)(2,1)S(1)}, u32[]{:S(2)}, u32[]{:S(2)}) async-start(bf16[32,16,512]{2,1,0:T(8,128)(2,1)} %shard_map.242), calls=%async_computation.2 | async-start | bytes 1048576 | tf_op jit(solution)/shard_map/all_to_all | solution.py:128
  131.2 33.1 %all-to-all-start.3 = ((bf16[16,64,1024]{2,1,0:T(8,128)(2,1)}), bf16[16,64,1024]{2,1,0:T(8,128)(2,1)S(1)}, u32[]{:S(2)}, u32[]{:S(2)}) async-start(bf16[16,64,1024]{2,1,0:T(8,128)(2,1)} %broadcast_in_dim.7), calls=%async_computation.3 | async-start | bytes 4194304 | tf_op jit(solution)/shard_map/all_to_all | solution.py:1088
  135.1 202.5 %reduce-scatter.2.cloned.1.call-start = ((), (), s32[]{:S(2)}) async-start(), calls=%async_computation.11 | async-start | bytes 8650752 | tf_op jit(solution)/shard_map/reduce_scatter | solution.py:1100
  167.8 15.0 %collective-permute-start.10 = (bf16[64,2048]{1,0:T(8,128)(2,1)S(1)}, bf16[64,2048]{1,0:T(8,128)(2,1)S(1)}, u32[]{:S(2)}, u32[]{:S(2)}) collective-permute-start(bf16[64,2048]{1,0:T(8,128)(2,1)S(1)} %get-tuple-element.155.one), channel_id=1, source_target_pairs={{0,4},{4,0},{64,68},{68,64},{1,5},{5,1},{65,69},{69,65},{2,6},{6,2... | collective-permute-start | bytes 786440 | tf_op jit(solution)/shard_map/ppermute | solution.py:58
  229.0 22.3 %all-to-all-start.4 = ((bf16[32,16,512]{2,1,0:T(8,128)(2,1)}), bf16[32,16,512]{2,1,0:T(8,128)(2,1)S(1)}, u32[]{:S(2)}, u32[]{:S(2)}) async-start(bf16[32,16,512]{2,1,0:T(8,128)(2,1)} %bitcast.47), calls=%async_computation.4 | async-start | bytes 1048576 | tf_op jit(solution)/shard_map/all_to_all | solution.py:124
  234.2 17.0 %collective-permute-start.19 = (bf16[64,2048]{1,0:T(8,128)(2,1)}, bf16[64,2048]{1,0:T(8,128)(2,1)S(1)}, u32[]{:S(2)}, u32[]{:S(2)}) collective-permute-start(bf16[64,2048]{1,0:T(8,128)(2,1)} %get-tuple-element.192), channel_id=1, source_target_pairs={{0,64},{4,68},{64,4},{68,0},{1,65},{5,69},{65,5},{69,1},{2,66},{6,... | collective-permute-start | bytes 786440 | tf_op jit(solution)/shard_map/ppermute | solution.py:58
  234.5 16.8 %collective-permute-start.20 = (bf16[64,2048]{1,0:T(8,128)(2,1)}, bf16[64,2048]{1,0:T(8,128)(2,1)S(1)}, u32[]{:S(2)}, u32[]{:S(2)}) collective-permute-start(bf16[64,2048]{1,0:T(8,128)(2,1)} %get-tuple-element.193), channel_id=1, source_target_pairs={{0,68},{4,64},{64,0},{68,4},{1,69},{5,65},{65,1},{69,5},{2,70},{6,... | collective-permute-start | bytes 786440 | tf_op jit(solution)/shard_map/ppermute | solution.py:58
  237.0 14.3 %collective-permute-start.21 = (bf16[64,2048]{1,0:T(8,128)(2,1)}, bf16[64,2048]{1,0:T(8,128)(2,1)S(1)}, u32[]{:S(2)}, u32[]{:S(2)}) collective-permute-start(bf16[64,2048]{1,0:T(8,128)(2,1)} %get-tuple-element.194), channel_id=1, source_target_pairs={{0,4},{4,0},{64,68},{68,64},{1,5},{5,1},{65,69},{69,65},{2,6},{6,2... | collective-permute-start | bytes 786440 | tf_op jit(solution)/shard_map/ppermute | solution.py:58
  252.0 14.6 %collective-permute-start.22 = (bf16[1024,1536]{1,0:T(8,128)(2,1)}, bf16[1024,1536]{1,0:T(8,128)(2,1)}, u32[]{:S(2)}, u32[]{:S(2)}) collective-permute-start(bf16[1024,1536]{1,0:T(8,128)(2,1)} %shard_map.253), channel_id=1, source_target_pairs={{0,32},{32,0},{1,33},{33,1},{2,34},{34,2},{3,35},{35,3},{4,36},{36... | collective-permute-start | bytes 9437192 | tf_op jit(solution)/shard_map/ppermute | solution.py:81
  254.0 23.0 %all-to-all-start.5 = ((bf16[32,16,512]{2,1,0:T(8,128)(2,1)}), bf16[32,16,512]{2,1,0:T(8,128)(2,1)}, u32[]{:S(2)}, u32[]{:S(2)}) async-start(bf16[32,16,512]{2,1,0:T(8,128)(2,1)} %shard_map.256), calls=%async_computation.5 | async-start | bytes 1048576 | tf_op jit(solution)/shard_map/all_to_all | solution.py:128
  277.0 43.1 %all-to-all-start.6 = ((bf16[4,256,2560]{2,1,0:T(8,128)(2,1)}), bf16[4,256,2560]{2,1,0:T(8,128)(2,1)}, u32[]{:S(2)}, u32[]{:S(2)}) async-start(bf16[4,256,2560]{2,1,0:T(8,128)(2,1)} %bitcast.42), calls=%async_computation.7 | async-start | bytes 10485760 | tf_op jit(solution)/shard_map/all_to_all | solution.py:132
  290.7 22.3 %collective-permute-start.27 = (bf16[1024,1536]{1,0:T(8,128)(2,1)}, bf16[1024,1536]{1,0:T(8,128)(2,1)}, u32[]{:S(2)}, u32[]{:S(2)}) collective-permute-start(bf16[1024,1536]{1,0:T(8,128)(2,1)} %shard_map.259), channel_id=1, source_target_pairs={{0,32},{32,0},{1,33},{33,1},{2,34},{34,2},{3,35},{35,3},{4,36},{36... | collective-permute-start | bytes 9437192 | tf_op jit(solution)/shard_map/ppermute | solution.py:81
  320.1 30.7 %all-to-all-start.7 = ((bf16[4,256,1664]{2,1,0:T(8,128)(2,1)}), bf16[4,256,1664]{2,1,0:T(8,128)(2,1)}, u32[]{:S(2)}, u32[]{:S(2)}) async-start(bf16[4,256,1664]{2,1,0:T(8,128)(2,1)} %bitcast.44), calls=%async_computation.8 | async-start | bytes 6815744 | tf_op jit(solution)/shard_map/all_to_all | solution.py:132
  342.0 17.6 %collective-permute-start.36 = (bf16[64,4096]{1,0:T(8,128)(2,1)}, bf16[64,4096]{1,0:T(8,128)(2,1)S(1)}, u32[]{:S(2)}, u32[]{:S(2)}) collective-permute-start(bf16[64,4096]{1,0:T(8,128)(2,1)} %shard_map.264.refs_0_), channel_id=1, source_target_pairs={{0,64},{36,100},{68,0},{96,36},{1,65},{37,101},{69,1},{97,37},{2,6... | collective-permute-start | bytes 1572872 | tf_op jit(solution)/shard_map/ppermute | solution.py:68
  342.7 17.3 %collective-permute-start.35 = (bf16[64,4096]{1,0:T(8,128)(2,1)}, bf16[64,4096]{1,0:T(8,128)(2,1)}, u32[]{:S(2)}, u32[]{:S(2)}) collective-permute-start(bf16[64,4096]{1,0:T(8,128)(2,1)} %shard_map.264.refs_0_), channel_id=1, source_target_pairs={{4,0},{32,36},{68,64},{96,100},{5,1},{33,37},{69,65},{97,101},{6,2... | collective-permute-start | bytes 1572872 | tf_op jit(solution)/shard_map/ppermute | solution.py:68
  354.9 21.2 %all-to-all-start.8 = ((bf16[4,64,4224]{2,1,0:T(8,128)(2,1)}), bf16[4,64,4224]{2,1,0:T(8,128)(2,1)S(1)}, u32[]{:S(2)}, u32[]{:S(2)}) async-start(bf16[4,64,4224]{2,1,0:T(8,128)(2,1)} %bitcast.43), calls=%async_computation.9 | async-start | bytes 4325376 | tf_op jit(solution)/shard_map/all_to_all | solution.py:132
  362.6 21.5 %collective-permute-start.37 = (bf16[256,4096]{1,0:T(8,128)(2,1)}, bf16[256,4096]{1,0:T(8,128)(2,1)}, u32[]{:S(2)}, u32[]{:S(2)}) collective-permute-start(bf16[256,4096]{1,0:T(8,128)(2,1)} %shard_map.267.mine), channel_id=1, source_target_pairs={{0,32},{36,4},{1,33},{37,5},{2,34},{38,6},{3,35},{39,7},{8,40},{44... | collective-permute-start | bytes 6291464 | tf_op jit(solution)/shard_map/ppermute | solution.py:77
  (70 other events, 546.9 us)
Sparse Core Ops, SparseCore 0:
  27.1 96.6 all-gather.1
  205.0 96.2 reduce-scatter.1

commit v6 on v5

--- a/solution.py
+++ b/solution.py
@@ -775,7 +775,7 @@
             columns(256, 512),
         ],
         [
-            *row_parts(512, lambda i: (0, i)),
+            *[(*part, "hbm") for part in row_parts(512, lambda i: (0, i))],
             (shape((2, 2048), F32), columns(2, 512)),
         ],
         [place, first, d_both, early, early_other, hat],
@@ -898,47 +898,48 @@
                 total = made[take] + given[to, local : local + cols].astype(F32)
                 out[to, start : start + cols] = total.astype(BF)
             start, local = start + cols, local + cols
-    if refs:
-        for take, to in row_offsets(side):
-            total = refs[0][to, :].astype(F32) + refs[1][to, :].astype(F32)
-            out[to, start:] = total.astype(BF)
-
-
-def grad_own(place, groups, more=()):
-    specs, operands, sizes, cols = [SCALARS], [place], [], sum(m.shape[1] for m in more[:1])
+
+
+def grad_own(place, groups, more=0):
+    specs, operands, sizes, cols = [SCALARS], [place], [], more
     for left, rights, given in groups:
         specs += [columns(256, 512)] + [whole(r.shape) for r in rights] + [whole(given.shape)]
         operands += [left, *rights, given]
         sizes.append(len(rights))
         cols += given.shape[1]
-    specs += [whole(m.shape) for m in more]
     return run(
         functools.partial(own_kernel, tuple(sizes)),
         (4,),
         specs,
         [(shape((1024, cols), BF), whole((1024, cols)), "hbm")],
-        operands + list(more),
+        operands,
         limit=61,
     )[0]
 
 
-def vector_kernel(place, one, two, three, four, own, other):
-    total = one[...] + two[...] + three[...] + four[...]
-    for ref, side in ((own, 0), (other, 1)):
-        rows = jnp.where(place[1] == side, total[:, :256], total[:, 256:])
-        rows = jnp.concatenate([rows, jnp.zeros((120, 256), F32)], axis=0)
-        store_rows(ref, rows.T.astype(BF), place[1] if side == 0 else 1 - place[1], 0)
-
-
-def vector_split(place, *vectors):
-    half = (shape((1024, 128), BF), whole((1024, 128)))
-    return run(
+def vector_kernel(place, kept, one, two, three, four, out):
+    wide = jnp.zeros((120, 256), F32)
+    for i in range(4):
+        at = pl.ds(pl.multiple_of((2 * i + place[1]) * 256, 256), 256)
+        rows = one[:, at] + two[:, at] + three[:, at] + four[:, at]
+        made = jnp.concatenate([rows, wide], axis=0).T.astype(BF)
+        for j in range(4):
+            to = jnp.where(place[1] == 0, i * 256 + j * 64, j * 256 + i * 64)
+            out[pl.ds(pl.multiple_of(to, 64), 64), :] = made[j * 64 : j * 64 + 64]
+
+
+def with_vectors(place, wide, *vectors):
+    last = wide.shape[1] // 128 - 1
+    return pl.pallas_call(
         vector_kernel,
-        (4,),
-        [SCALARS] + [columns(8, 512)] * 4,
-        [half, half],
-        [place, *vectors],
-    )
+        grid=(1,),
+        in_specs=[SCALARS, pl.BlockSpec(memory_space=pl.ANY)] + [whole((8, 2048))] * 4,
+        out_specs=pl.BlockSpec((1024, 128), lambda i: (0, last)),
+        out_shape=pltpu.HBM(wide.shape, BF),
+        input_output_aliases={1: 0},
+        compiler_params=pltpu.CompilerParams(vmem_limit_bytes=48 * 1024 * 1024),
+        cost_estimate=pl.CostEstimate(flops=1, bytes_accessed=1, transcendentals=0),
+    )(place, wide, *vectors)
 
 
 def four_sum(ref):
@@ -1138,12 +1139,12 @@
     late_other = core_swap(late_other)
     mine, *parts, vectors = normed_back(place, d_first, d_both, early, early_other, hat1)
     vectors = jnp.concatenate([vectors, vectors2, jnp.zeros((4, 2048), F32)])
+    vectors = vectors + core_swap(vectors)
     shifted = [z_shift(vectors, shift) for shift in (1, 3, 2)]
     parts = z_collect(parts)
-    vector_own, vector_other = vector_split(place, vectors, *shifted)
-    late_part = grad_own(
-        place, [(normed1, [d_both], late_other)], (vector_own, core_swap(vector_other))
-    )
+    late_part = grad_own(place, [(normed1, [d_both], late_other)], 128)
+    late_part, shifted = lax.optimization_barrier((late_part, shifted))
+    late_part = with_vectors(place, late_part, vectors, *shifted)
     late_part, early_part = lax.optimization_barrier((late_part, early_part))
     late_part = exchange(late_part, FIRST_WAY)
 

time: 401 us -> 401 us (level)
    ppermute x21, waiting for transfers between devices: 36 us -> 30 us  [z_shift(): return lax.ppermute(values, ('zl', 'zh'), pairs(('zl', 'zh'), move))]
    all_to_all x3, waiting for transfers between devices: 0.01 us -> 5.91 us  [exchange(): lax.all_to_all(values, CHIPS, 0, 0, axis_index_groups=groups, tiled=True)]
    pallas_call x33 -> x32, Pallas kernels: 123 us -> 121 us  [run(): pl.pallas_call(kernel, grid=grid, in_specs=ins, out_specs=[o[1] for o in...]
    unnamed x90 -> x98, local copies, waits for them, and re-layouts: 16 us -> 17.6 us
  transfers between devices with their start and end apart: 49 -> 49, of which waited for: 25 -> 21; matrix products, arithmetic and copies ran while one was open for 2% -> 2% of each run, Pallas kernels for 30% -> 29%
where the time goes in v6:
time: 401 us; the launch traced here: 399 us
  starting transfers between devices  134 us (33%)
  Pallas kernels  126 us (31%)
  waiting for transfers between devices  95.3 us (24%)
  local copies, waits for them, and re-layouts  25.2 us (6%)
  between operations  16 us (4%)
    pallas_call x32, Pallas kernels, run(): pl.pallas_call(kernel, grid=grid, in_specs=ins, out_specs=[o[1] for o in...  121 us
    ppermute x7, starting transfers between devices, swap_roles(): lax.ppermute(values, ('c', 'zh'), pairs(('c', 'zh'), lambda p: {'c': p['z...  39.4 us
    ppermute x21, waiting for transfers between devices, z_shift(): return lax.ppermute(values, ('zl', 'zh'), pairs(('zl', 'zh'), move))  30 us
    ppermute x7, waiting for transfers between devices, swap_roles(): lax.ppermute(values, ('c', 'zh'), pairs(('c', 'zh'), lambda p: {'c': p['z...  27.4 us
    ppermute x21, starting transfers between devices, z_shift(): return lax.ppermute(values, ('zl', 'zh'), pairs(('zl', 'zh'), move))  27.4 us
    unnamed x98, local copies, waits for them, and re-layouts  17.6 us
    all_to_all x3, starting transfers between devices, exchange(): lax.all_to_all(values, CHIPS, 0, 0, axis_index_groups=groups, tiled=True)  13.7 us
    all_to_all x2, starting transfers between devices, scan_back(): return lax.all_to_all(carried, SPANS, 0, 0, tiled=True).reshape(2 * DK, DV)  13.5 us
  transfers between devices with their start and end apart: 49, of which 21 were waited for; matrix products, arithmetic and copies ran while one was open for 2% of the time, Pallas kernels for 29%

profile of v6, /device:TPU:1, one launch (start us, length us, event | category | flops | bytes accessed | tf_op | source)
XLA Modules:
  0.0 398.6 jit_solution(11580488632350030002)
XLA Ops:
  10.6 6.9 %collective-permute-start = (bf16[64,5248]{1,0:T(8,128)(2,1)}, bf16[64,5248]{1,0:T(8,128)(2,1)S(1)}, u32[]{:S(2)}, u32[]{:S(2)}) collective-permute-start(bf16[64,5248]{1,0:T(8,128)(2,1)} %shard_map.237), channel_id=1, source_target_pairs={{0,0},{4,32},{32,4},{36,36},{1,1},{5,33},{33,5},{37,37},{2,2},{6,3... | collective-permute-start | bytes 2015240 | tf_op jit(solution)/shard_map/ppermute | solution.py:48
  17.5 8.6 %collective-permute-done = bf16[64,5248]{1,0:T(8,128)(2,1)S(1)} collective-permute-done((bf16[64,5248]{1,0:T(8,128)(2,1)}, bf16[64,5248]{1,0:T(8,128)(2,1)S(1)}, u32[]{:S(2)}, u32[]{:S(2)}) %collective-permute-start) | collective-permute-done | bytes 671776 | tf_op jit(solution)/shard_map/ppermute | solution.py:48
  29.1 6.9 %all-to-all-start = ((bf16[16,64,1664]{2,1,0:T(8,128)(2,1)}), bf16[16,64,1664]{2,1,0:T(8,128)(2,1)}, u32[]{:S(2)}, u32[]{:S(2)}) async-start(bf16[16,64,1664]{2,1,0:T(8,128)(2,1)} %broadcast_in_dim.6), calls=%async_computation | async-start | bytes 6815744 | tf_op jit(solution)/shard_map/all_to_all | solution.py:1060
  41.5 12.9 %collective-permute-done.1.values = bf16[256,2048]{1,0:T(8,128)(2,1)S(1)} collective-permute-done((bf16[256,2048]{1,0:T(8,128)(2,1)S(1)}, bf16[256,2048]{1,0:T(8,128)(2,1)S(1)}, u32[]{:S(2)}, u32[]{:S(2)}) %collective-permute-start.1) | collective-permute-done | bytes 1048608 | tf_op jit(solution)/shard_map/ppermute | solution.py:48
  77.4 6.4 %collective-permute-done.5.gains_other.key_other.value_other.w_other = bf16[1024,1664]{1,0:T(8,128)(2,1)} collective-permute-done((bf16[1024,1664]{1,0:T(8,128)(2,1)}, bf16[1024,1664]{1,0:T(8,128)(2,1)}, u32[]{:S(2)}, u32[]{:S(2)}) %collective-permute-start.5) | collective-permute-done | bytes 3407904 | tf_op jit(solution)/shard_map/ppermute | solution.py:81
  83.8 6.9 %shard_map.241 = (bf16[256,512]{1,0:T(8,128)(2,1)}, bf16[256,1024]{1,0:T(8,128)(2,1)}, bf16[512,512]{1,0:T(8,128)(2,1)}, bf16[256,2048]{1,0:T(8,128)(2,1)}, f32[8,2048]{1,0:T(8,128)}) custom-call(f32[2]{0:T(128)} %copy-done.41, s32[4]{0:T(128)} %copy-done.19, f32[256,2048]{1,0:T(8,128)} %get-tuple-element.137.hat, ...), custom_call_target="tpu_custom_call" | custom-call | flops 1 | bytes 1 | tf_op jit(solution)/shard_map/pallas_call | solution.py:136
  90.7 7.3 %all-to-all-start.1 = ((bf16[32,16,512]{2,1,0:T(8,128)(2,1)}), bf16[32,16,512]{2,1,0:T(8,128)(2,1)S(1)}, u32[]{:S(2)}, u32[]{:S(2)}) async-start(bf16[32,16,512]{2,1,0:T(8,128)(2,1)} %bitcast.49), calls=%async_computation.1 | async-start | bytes 1048576 | tf_op jit(solution)/shard_map/all_to_all | solution.py:124
  100.6 12.7 %all-to-all-done.1.parts = bf16[32,16,512]{2,1,0:T(8,128)(2,1)S(1)} async-done(((bf16[32,16,512]{2,1,0:T(8,128)(2,1)}), bf16[32,16,512]{2,1,0:T(8,128)(2,1)S(1)}, u32[]{:S(2)}, u32[]{:S(2)}) %all-to-all-start.1) | async-done | bytes 524320 | tf_op jit(solution)/shard_map/all_to_all | solution.py:124
  114.2 5.9 %all-to-all-start.2 = ((bf16[32,16,512]{2,1,0:T(8,128)(2,1)}), bf16[32,16,512]{2,1,0:T(8,128)(2,1)S(1)}, u32[]{:S(2)}, u32[]{:S(2)}) async-start(bf16[32,16,512]{2,1,0:T(8,128)(2,1)} %shard_map.242), calls=%async_computation.2 | async-start | bytes 1048576 | tf_op jit(solution)/shard_map/all_to_all | solution.py:128
  123.9 6.4 %shard_map.243 = (bf16[256,512]{1,0:T(8,128)(2,1)}, f32[256,1024]{1,0:T(8,128)}, bf16[2,256,256]{2,1,0:T(8,128)(2,1)}, f32[256,1024]{1,0:T(8,128)}) custom-call(f32[2]{0:T(128)} %copy-done.41, s32[4]{0:T(128)} %copy-done.19, bf16[256,2048]{1,0:T(8,128)(2,1)} %get-tuple-element.141.normed.left.refs_0_, ...), custom_call_target="tpu_custom_call" | custom-call | flops 1 | bytes 1 | tf_op jit(solution)/shard_map/pallas_call | solution.py:136
  135.2 6.0 %shard_map.244 = (f32[256,1024]{1,0:T(8,128)}, f32[2,256,1]{2,1,0:T(8,128)}, bf16[256,1024]{1,0:T(8,128)(2,1)}, f32[64,2048]{1,0:T(8,128)}, bf16[64,2048]{1,0:T(...) custom-call(f32[2]{0:T(128)} %copy-done.41, s32[4]{0:T(128)} %copy-done.19, ...), custom_call_target="tpu_custom_call" | custom-call | flops 1 | bytes 1 | tf_op jit(solution)/shard_map/pallas_call | solution.py:136
  149.9 6.8 %collective-permute-done.8.three = bf16[64,2048]{1,0:T(8,128)(2,1)S(1)} collective-permute-done((bf16[64,2048]{1,0:T(8,128)(2,1)}, bf16[64,2048]{1,0:T(8,128)(2,1)S(1)}, u32[]{:S(2)}, u32[]{:S(2)}) %collective-permute-start.8) | collective-permute-done | bytes 262176 | tf_op jit(solution)/shard_map/ppermute | solution.py:58
  177.3 5.6 %collective-permute-done.10.three = bf16[64,2048]{1,0:T(8,128)(2,1)S(1)} collective-permute-done((bf16[64,2048]{1,0:T(8,128)(2,1)S(1)}, bf16[64,2048]{1,0:T(8,128)(2,1)S(1)}, u32[]{:S(2)}, u32[]{:S(2)}) %collective-permute-start.10) | collective-permute-done | bytes 262176 | tf_op jit(solution)/shard_map/ppermute | solution.py:58
  182.9 6.1 %shard_map.247 = (bf16[256,2048]{1,0:T(8,128)(2,1)S(1)}, bf16[256,1024]{1,0:T(8,128)(2,1)S(1)}, bf16[256,1024]{1,0:T(8,128)(2,1)S(1)}, f32[64,2048]{1,0:T(8,128)...) custom-call(bf16[64,2048]{1,0:T(8,128)(2,1)S(1)} %get-tuple-element.157.one, ...), custom_call_target="tpu_custom_call" | custom-call | flops 1 | bytes 1 | tf_op jit(solution)/shard_map/pallas_call | solution.py:136
  193.3 6.6 %shard_map.248 = bf16[2048,2048]{1,0:T(8,128)(2,1)} custom-call(bf16[256,2048]{1,0:T(8,128)(2,1)S(1)} %get-tuple-element.166.left_one, bf16[256,1024]{1,0:T(8,128)(2,1)S(1)} %get-tuple-element.167.right_one, bf16[256,2048]{1,0:T(8,128)(2,1)S(1)} %copy-done.3, bf16[256,1024]{1,0:T(8,128)(2,1)S(1)} %get-tuple-element.176.right_two.hidden), custom_call_target="tpu_custom_call" | custom-call | flops 2147483648 | bytes 33554432 | tf_op jit(solution)/shard_map/pallas_call | solution.py:136
  223.4 6.4 %shard_map.251 = (bf16[256,2048]{1,0:T(8,128)(2,1)}, bf16[256,1024]{1,0:T(8,128)(2,1)}, bf16[256,1024]{1,0:T(8,128)(2,1)}, bf16[512,512]{1,0:T(8,128)(2,1)}) custom-call(f32[2]{0:T(128)} %copy-done.41, s32[4]{0:T(128)} %copy-done.19, bf16[64,2048]{1,0:T(8,128)(2,1)} %get-tuple-element.181.one, bf16[64,2048]{1,0:T(8,128)(2,1)} %copy-done.32, ...), custom_call_target="tpu_custom_call" | custom-call | flops 1 | bytes 1 | tf_op jit(solution)/shard_map/pallas_call | solution.py:136
  254.0 7.6 %all-to-all-start.5 = ((bf16[32,16,512]{2,1,0:T(8,128)(2,1)}), bf16[32,16,512]{2,1,0:T(8,128)(2,1)S(1)}, u32[]{:S(2)}, u32[]{:S(2)}) async-start(bf16[32,16,512]{2,1,0:T(8,128)(2,1)} %shard_map.256), calls=%async_computation.5 | async-start | bytes 1048576 | tf_op jit(solution)/shard_map/all_to_all | solution.py:128
  267.9 8.2 %shard_map.255 = bf16[1024,2560]{1,0:T(8,128)(2,1)} custom-call(s32[4]{0:T(128)} %copy-done.19, bf16[256,2048]{1,0:T(8,128)(2,1)} %get-tuple-element.141.normed.left.refs_0_, bf16[256,1024]{1,0:T(8,128)(2,1)} %get-tuple-element.187.refs_0_.refs_1_.d_gate, bf16[256,512]{1,0:T(8,128)(2,1)} %get-tuple-element.202.refs_1_.refs_2_.d_query, ...), custom_call_target="tpu_custom_call" | custom-call | flops 1 | bytes 1 | tf_op jit(solution)/shard_map/pallas_call | solution.py:136
  294.8 5.8 %shard_map.260 = (f32[64,2048]{1,0:T(8,128)}, bf16[64,2048]{1,0:T(8,128)(2,1)}, bf16[64,2048]{1,0:T(8,128)(2,1)}, bf16[64,2048]{1,0:T(8,128)(2,1)}, f32[2,2048]{1,0:T(2,128)S(1)}) custom-call(s32[4]{0:T(128)S(1)} %copy-done.21, f32[256,2048]{1,0:T(8,128)S(1)} %copy-done.8, bf16[256,1536]{1,0:T(8,128)(2,1)S(1)} %copy-done.4, ...), custom_call_target="tpu_custom_call" | custom-call | flops 1 | bytes 1 | tf_op jit(solution)/shard_map/pallas_call | solution.py:136
  306.1 6.2 %shard_map.261.kept = bf16[1024,1664]{1,0:T(8,128)(2,1)} custom-call(s32[4]{0:T(128)} %copy-done.19, bf16[256,2048]{1,0:T(8,128)(2,1)} %get-tuple-element.141.normed.left.refs_0_, bf16[256,1536]{1,0:T(8,128)(2,1)} %shard_map.258.refs_0_.d_both.refs_1_, bf16[1024,1536]{1,0:T(8,128)(2,1)} %collective-permute-done.27.refs_2_), custom_call_target="tpu_custom_call" | custom-call | flops 1 | bytes 1 | tf_op jit(solution)/shard_map/pallas_call | solution.py:136
  313.8 5.9 %all-to-all-done.6 = bf16[4,256,2560]{2,1,0:T(8,128)(2,1)} async-done(((bf16[4,256,2560]{2,1,0:T(8,128)(2,1)}), bf16[4,256,2560]{2,1,0:T(8,128)(2,1)}, u32[]{:S(2)}, u32[]{:S(2)}) %all-to-all-start.6) | async-done | bytes 5242912 | tf_op jit(solution)/shard_map/all_to_all | solution.py:132
  342.1 6.5 %collective-permute-start.35 = (bf16[64,4096]{1,0:T(8,128)(2,1)}, bf16[64,4096]{1,0:T(8,128)(2,1)}, u32[]{:S(2)}, u32[]{:S(2)}) collective-permute-start(bf16[64,4096]{1,0:T(8,128)(2,1)} %shard_map.264.refs_0_), channel_id=1, source_target_pairs={{4,0},{32,36},{68,64},{96,100},{5,1},{33,37},{69,65},{97,101},{6,2... | collective-permute-start | bytes 1572872 | tf_op jit(solution)/shard_map/ppermute | solution.py:68
  363.7 8.3 %collective-permute-start.32 = (bf16[64,2048]{1,0:T(8,128)(2,1)S(1)}, bf16[64,2048]{1,0:T(8,128)(2,1)S(1)}, u32[]{:S(2)}, u32[]{:S(2)}) collective-permute-start(bf16[64,2048]{1,0:T(8,128)(2,1)S(1)} %copy-done.43), channel_id=1, source_target_pairs={{0,0},{4,32},{32,4},{36,36},{1,1},{5,33},{33,5},{37,37},{2,2},{6,3... | collective-permute-start | bytes 786440 | tf_op jit(solution)/shard_map/ppermute | solution.py:48
  376.3 6.9 %collective-permute-start.33 = (bf16[64,4224]{1,0:T(8,128)(2,1)S(1)}, bf16[64,4224]{1,0:T(8,128)(2,1)S(1)}, u32[]{:S(2)}, u32[]{:S(2)}) collective-permute-start(bf16[64,4224]{1,0:T(8,128)(2,1)S(1)} %shard_map.266), channel_id=1, source_target_pairs={{0,0},{4,32},{32,4},{36,36},{1,1},{5,33},{33,5},{37,37},{2,2},{6,3... | collective-permute-start | bytes 1622024 | tf_op jit(solution)/shard_map/ppermute | solution.py:48
  (224 shorter events, 208.9 us)
Async XLA Ops:
  7.2 116.7 %all-gather.2.cloned.1.call-start = ((), (), s32[]{:S(2)}) async-start(), calls=%async_computation.10 | async-start | bytes 15138816 | tf_op jit(solution)/shard_map/all_gather | solution.py:1063
  10.6 15.5 %collective-permute-start = (bf16[64,5248]{1,0:T(8,128)(2,1)}, bf16[64,5248]{1,0:T(8,128)(2,1)S(1)}, u32[]{:S(2)}, u32[]{:S(2)}) collective-permute-start(bf16[64,5248]{1,0:T(8,128)(2,1)} %shard_map.237), channel_id=1, source_target_pairs={{0,0},{4,32},{32,4},{36,36},{1,1},{5,33},{33,5},{37,37},{2,2},{6,3... | collective-permute-start | bytes 2015240 | tf_op jit(solution)/shard_map/ppermute | solution.py:48
  29.1 46.6 %all-to-all-start = ((bf16[16,64,1664]{2,1,0:T(8,128)(2,1)}), bf16[16,64,1664]{2,1,0:T(8,128)(2,1)}, u32[]{:S(2)}, u32[]{:S(2)}) async-start(bf16[16,64,1664]{2,1,0:T(8,128)(2,1)} %broadcast_in_dim.6), calls=%async_computation | async-start | bytes 6815744 | tf_op jit(solution)/shard_map/all_to_all | solution.py:1060
  36.1 18.3 %collective-permute-start.1 = (bf16[256,2048]{1,0:T(8,128)(2,1)S(1)}, bf16[256,2048]{1,0:T(8,128)(2,1)S(1)}, u32[]{:S(2)}, u32[]{:S(2)}) collective-permute-start(bf16[256,2048]{1,0:T(8,128)(2,1)S(1)} %copy-done.42), channel_id=1, source_target_pairs={{0,0},{4,32},{32,4},{36,36},{1,1},{5,33},{33,5},{37,37},{2,2},{6,3... | collective-permute-start | bytes 3145736 | tf_op jit(solution)/shard_map/ppermute | solution.py:48
  54.4 18.9 %collective-permute-start.2 = (bf16[256,2048]{1,0:T(8,128)(2,1)}, bf16[256,2048]{1,0:T(8,128)(2,1)S(1)}, u32[]{:S(2)}, u32[]{:S(2)}) collective-permute-start(bf16[256,2048]{1,0:T(8,128)(2,1)} %param.27), channel_id=1, source_target_pairs={{0,0},{4,32},{32,4},{36,36},{1,1},{5,33},{33,5},{37,37},{2,2},{6,3... | collective-permute-start | bytes 3145736 | tf_op jit(solution)/shard_map/ppermute | solution.py:48
  59.2 15.7 %collective-permute-start.4 = (f32[2]{0:T(128)S(1)}, f32[2]{0:T(128)S(1)}, u32[]{:S(2)}, u32[]{:S(2)}) collective-permute-start(f32[2]{0:T(128)S(1)} %copy-done.48), channel_id=1, source_target_pairs={{0,0},{4,32},{32,4},{36,36},{1,1},{5,33},{33,5},{37,37},{2,2},{6,3... | collective-permute-start | bytes 32 | tf_op jit(solution)/shard_map/ppermute | solution.py:48
  90.7 22.6 %all-to-all-start.1 = ((bf16[32,16,512]{2,1,0:T(8,128)(2,1)}), bf16[32,16,512]{2,1,0:T(8,128)(2,1)S(1)}, u32[]{:S(2)}, u32[]{:S(2)}) async-start(bf16[32,16,512]{2,1,0:T(8,128)(2,1)} %bitcast.49), calls=%async_computation.1 | async-start | bytes 1048576 | tf_op jit(solution)/shard_map/all_to_all | solution.py:124
  114.2 16.9 %all-to-all-start.2 = ((bf16[32,16,512]{2,1,0:T(8,128)(2,1)}), bf16[32,16,512]{2,1,0:T(8,128)(2,1)S(1)}, u32[]{:S(2)}, u32[]{:S(2)}) async-start(bf16[32,16,512]{2,1,0:T(8,128)(2,1)} %shard_map.242), calls=%async_computation.2 | async-start | bytes 1048576 | tf_op jit(solution)/shard_map/all_to_all | solution.py:128
  131.2 33.1 %all-to-all-start.3 = ((bf16[16,64,1024]{2,1,0:T(8,128)(2,1)}), bf16[16,64,1024]{2,1,0:T(8,128)(2,1)S(1)}, u32[]{:S(2)}, u32[]{:S(2)}) async-start(bf16[16,64,1024]{2,1,0:T(8,128)(2,1)} %broadcast_in_dim.7), calls=%async_computation.3 | async-start | bytes 4194304 | tf_op jit(solution)/shard_map/all_to_all | solution.py:1089
  135.2 201.9 %reduce-scatter.2.cloned.1.call-start = ((), (), s32[]{:S(2)}) async-start(), calls=%async_computation.11 | async-start | bytes 8650752 | tf_op jit(solution)/shard_map/reduce_scatter | solution.py:1101
  167.9 15.0 %collective-permute-start.10 = (bf16[64,2048]{1,0:T(8,128)(2,1)S(1)}, bf16[64,2048]{1,0:T(8,128)(2,1)S(1)}, u32[]{:S(2)}, u32[]{:S(2)}) collective-permute-start(bf16[64,2048]{1,0:T(8,128)(2,1)S(1)} %get-tuple-element.157.one), channel_id=1, source_target_pairs={{0,4},{4,0},{64,68},{68,64},{1,5},{5,1},{65,69},{69,65},{2,6},{6,2... | collective-permute-start | bytes 786440 | tf_op jit(solution)/shard_map/ppermute | solution.py:58
  229.8 22.1 %all-to-all-start.4 = ((bf16[32,16,512]{2,1,0:T(8,128)(2,1)}), bf16[32,16,512]{2,1,0:T(8,128)(2,1)S(1)}, u32[]{:S(2)}, u32[]{:S(2)}) async-start(bf16[32,16,512]{2,1,0:T(8,128)(2,1)} %bitcast.48), calls=%async_computation.4 | async-start | bytes 1048576 | tf_op jit(solution)/shard_map/all_to_all | solution.py:124
  234.9 17.0 %collective-permute-start.19 = (bf16[64,2048]{1,0:T(8,128)(2,1)S(1)}, bf16[64,2048]{1,0:T(8,128)(2,1)S(1)}, u32[]{:S(2)}, u32[]{:S(2)}) collective-permute-start(bf16[64,2048]{1,0:T(8,128)(2,1)S(1)} %copy-done.27), channel_id=1, source_target_pairs={{0,64},{4,68},{64,4},{68,0},{1,65},{5,69},{65,5},{69,1},{2,66},{6,... | collective-permute-start | bytes 786440 | tf_op jit(solution)/shard_map/ppermute | solution.py:58
  235.2 16.7 %collective-permute-start.20 = (bf16[64,2048]{1,0:T(8,128)(2,1)S(1)}, bf16[64,2048]{1,0:T(8,128)(2,1)S(1)}, u32[]{:S(2)}, u32[]{:S(2)}) collective-permute-start(bf16[64,2048]{1,0:T(8,128)(2,1)S(1)} %copy-done.25), channel_id=1, source_target_pairs={{0,68},{4,64},{64,0},{68,4},{1,69},{5,65},{65,1},{69,5},{2,70},{6,... | collective-permute-start | bytes 786440 | tf_op jit(solution)/shard_map/ppermute | solution.py:58
  251.9 15.9 %collective-permute-start.22 = (bf16[1024,1536]{1,0:T(8,128)(2,1)}, bf16[1024,1536]{1,0:T(8,128)(2,1)}, u32[]{:S(2)}, u32[]{:S(2)}) collective-permute-start(bf16[1024,1536]{1,0:T(8,128)(2,1)} %shard_map.253), channel_id=1, source_target_pairs={{0,32},{32,0},{1,33},{33,1},{2,34},{34,2},{3,35},{35,3},{4,36},{36... | collective-permute-start | bytes 9437192 | tf_op jit(solution)/shard_map/ppermute | solution.py:81
  253.0 14.9 %collective-permute-start.23 = (bf16[1024,1024]{1,0:T(8,128)(2,1)}, bf16[1024,1024]{1,0:T(8,128)(2,1)}, u32[]{:S(2)}, u32[]{:S(2)}) collective-permute-start(bf16[1024,1024]{1,0:T(8,128)(2,1)} %shard_map.254), channel_id=1, source_target_pairs={{0,32},{32,0},{1,33},{33,1},{2,34},{34,2},{3,35},{35,3},{4,36},{36... | collective-permute-start | bytes 6291464 | tf_op jit(solution)/shard_map/ppermute | solution.py:81
  254.0 23.0 %all-to-all-start.5 = ((bf16[32,16,512]{2,1,0:T(8,128)(2,1)}), bf16[32,16,512]{2,1,0:T(8,128)(2,1)S(1)}, u32[]{:S(2)}, u32[]{:S(2)}) async-start(bf16[32,16,512]{2,1,0:T(8,128)(2,1)} %shard_map.256), calls=%async_computation.5 | async-start | bytes 1048576 | tf_op jit(solution)/shard_map/all_to_all | solution.py:128
  277.8 41.9 %all-to-all-start.6 = ((bf16[4,256,2560]{2,1,0:T(8,128)(2,1)}), bf16[4,256,2560]{2,1,0:T(8,128)(2,1)}, u32[]{:S(2)}, u32[]{:S(2)}) async-start(bf16[4,256,2560]{2,1,0:T(8,128)(2,1)} %bitcast.43), calls=%async_computation.7 | async-start | bytes 10485760 | tf_op jit(solution)/shard_map/all_to_all | solution.py:132
  291.3 14.8 %collective-permute-start.27 = (bf16[1024,1536]{1,0:T(8,128)(2,1)}, bf16[1024,1536]{1,0:T(8,128)(2,1)}, u32[]{:S(2)}, u32[]{:S(2)}) collective-permute-start(bf16[1024,1536]{1,0:T(8,128)(2,1)} %shard_map.259), channel_id=1, source_target_pairs={{0,32},{32,0},{1,33},{33,1},{2,34},{34,2},{3,35},{35,3},{4,36},{36... | collective-permute-start | bytes 9437192 | tf_op jit(solution)/shard_map/ppermute | solution.py:81
  319.7 31.0 %all-to-all-start.7 = ((bf16[4,256,1664]{2,1,0:T(8,128)(2,1)}), bf16[4,256,1664]{2,1,0:T(8,128)(2,1)}, u32[]{:S(2)}, u32[]{:S(2)}) async-start(bf16[4,256,1664]{2,1,0:T(8,128)(2,1)} %bitcast.42), calls=%async_computation.8 | async-start | bytes 6815744 | tf_op jit(solution)/shard_map/all_to_all | solution.py:132
  341.4 17.1 %collective-permute-start.36 = (bf16[64,4096]{1,0:T(8,128)(2,1)}, bf16[64,4096]{1,0:T(8,128)(2,1)S(1)}, u32[]{:S(2)}, u32[]{:S(2)}) collective-permute-start(bf16[64,4096]{1,0:T(8,128)(2,1)} %shard_map.264.refs_0_), channel_id=1, source_target_pairs={{0,64},{36,100},{68,0},{96,36},{1,65},{37,101},{69,1},{97,37},{2,6... | collective-permute-start | bytes 1572872 | tf_op jit(solution)/shard_map/ppermute | solution.py:68
  342.1 17.6 %collective-permute-start.35 = (bf16[64,4096]{1,0:T(8,128)(2,1)}, bf16[64,4096]{1,0:T(8,128)(2,1)}, u32[]{:S(2)}, u32[]{:S(2)}) collective-permute-start(bf16[64,4096]{1,0:T(8,128)(2,1)} %shard_map.264.refs_0_), channel_id=1, source_target_pairs={{4,0},{32,36},{68,64},{96,100},{5,1},{33,37},{69,65},{97,101},{6,2... | collective-permute-start | bytes 1572872 | tf_op jit(solution)/shard_map/ppermute | solution.py:68
  354.7 21.3 %all-to-all-start.8 = ((bf16[4,64,4224]{2,1,0:T(8,128)(2,1)}), bf16[4,64,4224]{2,1,0:T(8,128)(2,1)S(1)}, u32[]{:S(2)}, u32[]{:S(2)}) async-start(bf16[4,64,4224]{2,1,0:T(8,128)(2,1)} %bitcast.44), calls=%async_computation.9 | async-start | bytes 4325376 | tf_op jit(solution)/shard_map/all_to_all | solution.py:132
  362.4 21.7 %collective-permute-start.37 = (bf16[256,4096]{1,0:T(8,128)(2,1)}, bf16[256,4096]{1,0:T(8,128)(2,1)}, u32[]{:S(2)}, u32[]{:S(2)}) collective-permute-start(bf16[256,4096]{1,0:T(8,128)(2,1)} %shard_map.267.mine), channel_id=1, source_target_pairs={{0,32},{36,4},{1,33},{37,5},{2,34},{38,6},{3,35},{39,7},{8,40},{44... | collective-permute-start | bytes 6291464 | tf_op jit(solution)/shard_map/ppermute | solution.py:77
  (74 other events, 624.1 us)
Sparse Core Ops, SparseCore 0:
  27.1 96.7 all-gather.1
  205.1 96.1 reduce-scatter.1
